TPU v7x, 256 devices: a whole 4x4x8 slice. The times are simulated.
256 devices in a mesh: gx: 16 (over z, core), gy: 8 (over x, y_lo), seq: 2 (over y_hi).
Axes of the slice: x: 4, y: 4 (y_hi: 2, y_lo: 2; y = y_hi * 2 + y_lo), z: 8, core: 2. Of those that a mesh axis runs over, the one named last changes fastest.
Arguments:
- queries: bfloat16 [32, 64, 16, 1024], P('gx', 'gy', 'seq'), may hold values from -6 to 6
- keys: bfloat16 [2048, 1024], P(('gx', 'gy', 'seq')), may hold values from -8 to 8
- values: bfloat16 [2048, 1024], P(('gx', 'gy', 'seq')), may hold values from -6 to 6
- w_out: bfloat16 [1024, 256], replicated, may hold values from -0.1875 to 0.1875
- conv_first: bfloat16 [3, 3, 3, 256, 128], replicated, may hold values from -0.078125 to 0.078125
- conv_second: bfloat16 [3, 3, 3, 128, 128], replicated, may hold values from -0.109375 to 0.109375
Outputs:
- decoded: bfloat16 [64, 128, 32, 128], P('gx', 'gy', 'seq')
All inputs are finite; a program needn't handle non-finite values.
Results may differ from a plain program's by a relative error of at most 0.02.
Values may be sent and summed in bfloat16 or wider, within the bound.
No kernel may reach another device: no remote copies, remote signals or barrier semaphores. Data moves between devices by JAX's collectives and lax.ppermute only.
A program may use at most 64 MiB of HBM per device.

v0:
```python
import jax
import jax.numpy as jnp
from jax import lax
from jax.sharding import PartitionSpec as P

H = 8


def with_halo(cells, sides, width):
    for axis, dim in sides:
        count = lax.axis_size(axis)
        ends = count - 1
        head = lax.slice_in_dim(cells, 0, width, axis=dim)
        tail = lax.slice_in_dim(cells, cells.shape[dim] - width, cells.shape[dim], axis=dim)
        cells = jnp.concatenate(
            [
                lax.ppermute(tail, axis, [(i, (i + 1) % count) for i in range(ends)]),
                cells,
                lax.ppermute(head, axis, [((i + 1) % count, i) for i in range(ends)]),
            ],
            axis=dim,
        )
    return cells


def conv_layer(padded, weight, size_x, size_y, size_z):
    cin = weight.shape[3]
    cout = weight.shape[4]
    total = jnp.zeros((size_x * size_y * size_z, cout), jnp.float32)
    for a in range(3):
        for b in range(3):
            stacked = jnp.concatenate(
                [padded[a : a + size_x, b : b + size_y, c : c + size_z] for c in range(3)], axis=-1
            )
            stacked = stacked.reshape(-1, 3 * cin)
            total = total + jnp.dot(
                stacked, weight[a, b].reshape(3 * cin, cout), preferred_element_type=jnp.float32
            )
    return total.reshape(size_x, size_y, size_z, cout)


def upsample(field):
    return jnp.repeat(jnp.repeat(jnp.repeat(field, 2, axis=0), 2, axis=1), 2, axis=2)


def head_scores(rows, key_rows, head, head_size):
    query_part = rows[:, head * head_size : (head + 1) * head_size]
    key_part = key_rows[:, head * head_size : (head + 1) * head_size]
    scores = lax.dot_general(
        query_part, key_part, (((1,), (1,)), ((), ())), preferred_element_type=jnp.float32
    )
    return scores * head_size ** (-0.5)


def full_attention(rows, key_rows, value_rows, heads, head_size):
    outputs = []
    for head in range(heads):
        scores = head_scores(rows, key_rows, head, head_size)
        top = jnp.max(scores, axis=1, keepdims=True)
        weights = jnp.exp(scores - top).astype(jnp.bfloat16)
        total = jnp.sum(weights.astype(jnp.float32), axis=1, keepdims=True)
        summed = jnp.dot(
            weights,
            value_rows[:, head * head_size : (head + 1) * head_size],
            preferred_element_type=jnp.float32,
        )
        outputs.append(summed / total)
    return jnp.concatenate(outputs, axis=1).astype(jnp.bfloat16)


def body(queries, keys, values, w_out, conv_first, conv_second):
    size_x, size_y, size_z, width = queries.shape
    heads = H
    head_size = width // heads
    rows = queries.reshape(-1, width)
    key_rows, value_rows = (
        lax.all_gather(keys, ("gx", "gy", "seq"), axis=0, tiled=True),
        lax.all_gather(values, ("gx", "gy", "seq"), axis=0, tiled=True),
    )
    attended = full_attention(rows, key_rows, value_rows, heads, head_size)
    projected = jnp.dot(attended, w_out, preferred_element_type=jnp.float32)
    normed = projected * lax.rsqrt(jnp.mean(projected * projected, axis=-1, keepdims=True) + 1e-06)
    normed = normed.astype(jnp.bfloat16).reshape(size_x, size_y, size_z, w_out.shape[1])
    padded = with_halo(normed, (("gx", 0), ("gy", 1), ("seq", 2)), 1)
    first = conv_layer(padded, conv_first, size_x, size_y, size_z)
    hidden = jax.nn.silu(first).astype(jnp.bfloat16)
    upsampled = upsample(hidden)
    padded_up = with_halo(upsampled, (("gx", 0), ("gy", 1), ("seq", 2)), 1)
    second = conv_layer(padded_up, conv_second, 2 * size_x, 2 * size_y, 2 * size_z)
    return second.astype(jnp.bfloat16)


def solution(mesh):
    in_specs = (
        P("gx", "gy", "seq", None),
        P(("gx", "gy", "seq"), None),
        P(("gx", "gy", "seq"), None),
        P(),
        P(),
        P(),
    )
    out_specs = P("gx", "gy", "seq", None)
    return jax.shard_map(body, mesh=mesh, in_specs=in_specs, out_specs=out_specs, check_vma=False)
```

profile of v0, /device:TPU:1, one launch (start us, length us, event | category | flops | bytes accessed | tf_op | source)
XLA Modules:
  0.0 1505.8 jit_solution(7745640340206660496)
XLA Ops:
  6.5 0.7 all-gather.3.cloned.1.call-update
  7.3 0.7 all-gather.5.cloned.1.call-update
  8.0 712.3 %all-gather.3.cloned.1.call-done = bf16[2048,1024]{1,0:T(8,128)(2,1)} async-done(((bf16[8,1024]{1,0:T(8,128)(2,1)}), bf16[2048,1024]{1,0:T(8,128)(2,1)}) %all-gather.3.cloned.1.call-update) | async-done | bytes 4194320 | tf_op jit(solution)/shard_map/all_gather | solution.py:77
  720.4 1.6 fusion.71
  721.9 0.3 convert_reduce_fusion.7
  722.3 1.4 fusion.72
  723.7 0.3 convert_reduce_fusion.6
  724.0 0.4 fusion.73
  724.4 0.3 convert_reduce_fusion.5
  724.8 0.4 fusion.74
  725.2 0.3 convert_reduce_fusion.4
  725.5 0.4 fusion.75
  725.9 0.3 convert_reduce_fusion.3
  726.2 0.4 fusion.76
  726.6 0.3 convert_reduce_fusion.2
  726.9 0.4 fusion.77
  727.3 0.3 convert_reduce_fusion.1
  727.6 0.4 fusion.78
  728.0 0.2 copy-done.12
  728.3 0.3 convert_reduce_fusion
  728.6 700.2 %all-gather.5.cloned.1.call-done = bf16[2048,1024]{1,0:T(8,128)(2,1)} async-done(((bf16[8,1024]{1,0:T(8,128)(2,1)}), bf16[2048,1024]{1,0:T(8,128)(2,1)}) %all-gather.5.cloned.1.call-update) | async-done | bytes 4194320 | tf_op jit(solution)/shard_map/all_gather | solution.py:78
  1428.8 1.5 fusion.2
  1430.3 1.5 fusion.4
  1431.9 1.5 fusion.6
  1433.4 1.5 fusion.8
  1434.9 1.5 fusion.10
  1436.5 1.4 fusion.12
  1437.9 1.4 fusion.14
  1439.3 1.6 fusion.16
  1440.9 0.3 multiply_reduce_fusion
  1441.3 5.2 collective-permute-start
  1446.5 1.9 collective-permute-start.1
  1448.5 3.3 collective-permute-done.1
  1451.8 1.3 collective-permute-start.2
  1453.1 1.3 collective-permute-start.3
  1454.6 3.0 collective-permute-done.3
  1457.6 1.3 collective-permute-start.4
  1458.9 1.3 collective-permute-start.5
  1460.3 4.9 collective-permute-done.5
  1465.8 0.2 convolution_add_fusion.15
  1466.2 0.2 convolution_add_fusion.13
  1467.3 0.2 convolution_add_fusion.8
  1467.6 4.2 collective-permute-start.6
  1471.9 1.9 collective-permute-start.7
  1473.8 3.6 collective-permute-done.7
  1477.7 1.4 collective-permute-start.8
  1479.1 1.3 collective-permute-start.9
  1480.4 3.2 collective-permute-done.9
  1483.9 1.9 collective-permute-start.10
  1485.9 1.5 collective-permute-start.11
  1487.5 5.2 collective-permute-done.11
  1492.7 0.5 maximum_maximum_fusion
  1493.2 0.4 fusion.63
  1493.5 0.4 fusion.64
  1494.1 0.4 fusion.80
  1495.0 0.2 fusion.18
  1495.2 0.4 convolution_add_fusion.7
  1495.6 0.4 convolution_add_fusion.6
  1496.0 0.4 convolution_add_fusion.5
  1496.3 0.4 convolution_add_fusion.4
  1496.7 0.4 convolution_add_fusion.3
  1497.1 0.4 convolution_add_fusion.2
  1497.5 0.4 convolution_add_fusion.1
  1497.8 1.1 fusion
  (85 shorter events, 3.6 us)
Async XLA Ops:
  6.5 1434.4 %copy-start = (bf16[1024,256]{1,0:T(8,128)(2,1)S(1)}, bf16[1024,256]{1,0:T(8,128)(2,1)}, u32[]{:S(2)}) copy-start(bf16[1024,256]{1,0:T(8,128)(2,1)} %param.9) | copy-start | bytes 1572868
  6.5 715.7 %copy-start.16 = (bf16[2,8,8,1024]{3,2,1,0:T(8,128)(2,1)S(1)}, bf16[2,8,8,1024]{3,2,1,0:T(8,128)(2,1)}, u32[]{:S(2)}) copy-start(bf16[2,8,8,1024]{3,2,1,0:T(8,128)(2,1)} %param.6) | copy-start | bytes 786436
  6.5 713.8 %all-gather.3.cloned.1.call-start = ((), (), s32[]{:S(2)}) async-start(), calls=%async_computation | async-start | bytes 4210688 | tf_op jit(solution)/shard_map/all_gather | solution.py:77
  7.3 1421.5 %all-gather.5.cloned.1.call-start = ((), (), s32[]{:S(2)}) async-start(), calls=%async_computation.1 | async-start | bytes 4210688 | tf_op jit(solution)/shard_map/all_gather | solution.py:78
  720.4 3.6 copy-start.1
  723.7 1.1 copy-start.2
  724.4 1.1 copy-start.4
  725.2 1.0 copy-start.6
  725.9 1.0 copy-start.8
  726.6 1.0 copy-start.10
  727.3 1.0 copy-start.12
  1428.8 1.6 copy-start.3
  1428.8 3.1 copy-start.5
  1430.3 3.1 copy-start.7
  1431.9 3.1 copy-start.9
  1433.4 3.1 copy-start.11
  1434.9 3.0 copy-start.13
  1439.3 15.0 copy-start.14
  1441.3 7.1 collective-permute-start
  1446.5 5.2 collective-permute-start.1
  1451.8 2.8 collective-permute-start.2
  1453.1 4.5 collective-permute-start.3
  1457.6 2.7 collective-permute-start.4
  1458.9 6.3 collective-permute-start.5
  1466.9 13.5 copy-start.15
  1467.6 6.2 collective-permute-start.6
  1471.9 5.6 collective-permute-start.7
  1477.7 2.7 collective-permute-start.8
  1479.1 4.6 collective-permute-start.9
  1483.9 3.6 collective-permute-start.10
  1485.9 6.8 collective-permute-start.11
Sparse Core Ops, SparseCore 0:
  9.2 711.0 all-gather.2
  722.2 706.4 all-gather.4
where the time goes:
time: 1510 us
  waiting for transfers between devices  1440 us (95%)
  starting transfers between devices  24.5 us (2%)
  matrix products  23.6 us (2%)
    all_gather x1, waiting for transfers between devices, body(): lax.all_gather(keys, ('gx', 'gy', 'seq'), axis=0, tiled=True)  712 us
    all_gather x1, waiting for transfers between devices, body(): lax.all_gather(values, ('gx', 'gy', 'seq'), axis=0, tiled=True)  700 us
  transfers between devices with their start and end apart: 14, of which 8 were waited for; matrix products, arithmetic and copies ran while one was open for 1% of the time, Pallas kernels for 0%

commit v1 on v0

v1 whole, which is shorter than its diff:
```python
import jax
import jax.numpy as jnp
import numpy as np
from jax import lax
from jax.experimental import pallas as pl
from jax.experimental.pallas import tpu as pltpu
from jax.sharding import Mesh, PartitionSpec as P

H = 8
HD = 128
BF = jnp.bfloat16
F32 = jnp.float32
VM = pl.BlockSpec(memory_space=pltpu.VMEM)
LOG2E = 1.4426950408889634


def call(kernel, shape, dtype, count, flops, scratch=()):
    return pl.pallas_call(
        kernel,
        out_shape=jax.ShapeDtypeStruct(shape, dtype),
        in_specs=[VM] * count,
        out_specs=VM,
        scratch_shapes=list(scratch),
        compiler_params=pltpu.CompilerParams(vmem_limit_bytes=48 * 1024 * 1024),
        cost_estimate=pl.CostEstimate(flops=flops, bytes_accessed=1000000, transcendentals=0),
    )


def pack_kernel(q_ref, k_ref, v_ref, out_ref):
    for h in range(H):
        cols = slice(h * HD, (h + 1) * HD)
        pair = jnp.concatenate([k_ref[:, cols].astype(F32), v_ref[:, cols].astype(F32)], axis=0).astype(BF)
        for s in range(2):
            out_ref[2 * h + s, 0:64] = q_ref[s, :, cols]
            out_ref[2 * h + s, 64:80] = pair


def attention_kernel(q_ref, own_ref, other_ref, out_ref):
    keys = jnp.concatenate([own_ref[:, 0:128].reshape(1024, HD), other_ref[:, 0:128].reshape(1024, HD)], axis=0)
    vals = jnp.concatenate([own_ref[:, 128:256].reshape(1024, HD), other_ref[:, 128:256].reshape(1024, HD)], axis=0)
    vals = jnp.concatenate([vals, jnp.ones((2048, HD), BF)], axis=1)
    edge = jnp.zeros((32, HD), BF)
    for s in range(2):
        out_ref[s, 0:32] = edge
        out_ref[14 + s, 160:192] = edge
    for g in range(8):
        q = jnp.concatenate([q_ref[2 * g, 0:64], q_ref[2 * g + 1, 0:64]], axis=0)
        scores = lax.dot_general(q, keys, (((1,), (1,)), ((), ())), preferred_element_type=F32)
        top = jnp.max(scores, axis=1, keepdims=True)
        weights = jnp.exp2((scores - top) * (HD**-0.5 * LOG2E)).astype(BF)
        both = jnp.dot(weights, vals, preferred_element_type=F32)
        done = (both[:, 0:HD] / both[:, HD : 2 * HD]).reshape(2, 8, 8, HD)
        done = jnp.concatenate([done[0], done[1]], axis=1).reshape(128, HD).astype(BF)
        for s in range(2):
            out_ref[2 * g + s, 32:160] = done
            if g < 7:
                out_ref[2 * g + 2 + s, 0:32] = done[96:128]
            if g > 0:
                out_ref[2 * g - 2 + s, 160:192] = done[0:32]


def project_kernel(a_ref, w_ref, out_ref):
    for s in range(2):
        rows = jnp.concatenate([a_ref[2 * h + s] for h in range(H)], axis=1)
        projected = jnp.dot(rows, w_ref[...], preferred_element_type=F32)
        scale = lax.rsqrt(jnp.mean(projected * projected, axis=1, keepdims=True) + 1e-06)
        out_ref[s] = (projected * scale).astype(BF)


def merge_kernel(w_ref, out_ref):
    def both(parts):
        return ((parts[0], parts[1] + parts[2]), (parts[0] + parts[1], parts[2]))

    taps = [[[w_ref[9 * a + 3 * b + c].astype(F32) for c in range(3)] for b in range(3)] for a in range(3)]
    on_z = [[[m for p in both(taps[a][b]) for m in p] for b in range(3)] for a in range(3)]
    for n in range(4):
        on_y = [both([on_z[a][b][n] for b in range(3)]) for a in range(3)]
        for py in range(2):
            for b in range(2):
                on_x = both([on_y[a][py][b] for a in range(3)])
                for px in range(2):
                    for a in range(2):
                        rows = (2 * a + b) * 128
                        out_ref[2 * px + py, rows : rows + 128, n * 128 : (n + 1) * 128] = on_x[px][a].astype(BF)


def shifted(x, by):
    return pltpu.roll(x, by % x.shape[0], 0)


def conv_kernel(where_ref, own_ref, left_ref, right_ref, w1_ref, w2_ref, out_ref, field):
    gx, gy, seq = where_ref[0], where_ref[1], where_ref[2]
    slabs = [left_ref[0], left_ref[1], own_ref[0], own_ref[1], right_ref[0], right_ref[1]]
    row = lax.broadcasted_iota(jnp.int32, (160, 128), 0)
    at_z = row % 16
    at_y = gy * 8 - 1 + row // 16
    inside = (at_y >= 0) & (at_y < 64)
    hidden = []
    for x in range(4):
        total = jnp.zeros((160, 384), F32)
        for a in range(3):
            for b in range(3):
                t = 9 * a + 3 * b
                weight = jnp.concatenate([w1_ref[t], w1_ref[t + 1], w1_ref[t + 2]], axis=1)
                total = total + jnp.dot(slabs[x + a][16 * b : 16 * b + 160], weight, preferred_element_type=F32)
        first = (
            jnp.where(at_z > 0, shifted(total[:, 0:128], 1), 0.0)
            + total[:, 128:256]
            + jnp.where(at_z < 15, shifted(total[:, 256:384], -1), 0.0)
        )
        value = first / (1.0 + jnp.exp(-first))
        at_x = gx * 2 - 1 + x
        value = jnp.where(inside & (at_x >= 0) & (at_x < 32), value, 0.0)
        low = jnp.where(at_z > 0, shifted(value, 1), 0.0)
        high = jnp.where(at_z < 9, shifted(value, -7), 0.0)
        hidden.append(jnp.where(seq == 0, low, high).astype(BF))
    for px in range(2):
        for py in range(2):
            rows = jnp.concatenate(
                [
                    jnp.concatenate(
                        [
                            hidden[i + px + a][16 * (py + b) : 16 * (py + b) + 128]
                            for a in range(2)
                            for b in range(2)
                        ],
                        axis=1,
                    )
                    for i in range(2)
                ],
                axis=0,
            )
            parts = jnp.dot(rows, w2_ref[2 * px + py], preferred_element_type=F32)
            even = parts[:, 0:128] + shifted(parts[:, 128:256], -1)
            odd = shifted(parts[:, 256:384], -1) + shifted(parts[:, 384:512], -2)
            for pz, part in ((0, even), (1, odd)):
                part = part.reshape(2, 8, 16, 128)
                for i in range(2):
                    for j in range(8):
                        field[2 * i + px, 2 * j + py, pl.ds(pz, 8, stride=2), :] = part[i, j, 0:8]
    out_ref[...] = field[...].astype(BF)


def body(queries, keys, values, w_out, conv_first, conv_second):
    plane = ("gy", "seq")
    sent = call(pack_kernel, (16, 80, HD), BF, 3, 1000000)(queries.reshape(2, 64, H * HD), keys, values)
    got = lax.all_to_all(sent, plane, 0, 0, tiled=True)
    pair = got[:, 64:80].reshape(16, 2, 8, HD).transpose(1, 0, 2, 3).reshape(1, 256, HD)
    own = lax.all_to_all(jnp.broadcast_to(pair, (8, 256, HD)), "z", 0, 0, tiled=True)
    other = lax.ppermute(own, "core", [(0, 1), (1, 0)])
    attended = call(attention_kernel, (16, 192, HD), BF, 3, 2 * 10**9)(got, own, other)
    back = lax.all_to_all(attended, plane, 0, 0, tiled=True)
    normed = call(project_kernel, (2, 192, 256), BF, 2, 2 * 10**8)(back, w_out)
    left = lax.ppermute(normed, ("z", "core"), [(i, i + 1) for i in range(15)])
    right = lax.ppermute(normed, ("z", "core"), [(i + 1, i) for i in range(15)])
    merged = call(merge_kernel, (4, 512, 512), BF, 1, 10**9)(conv_second.reshape(27, 128, 128))
    place = jnp.stack([lax.axis_index(("z", "core")), lax.axis_index("gy"), lax.axis_index("seq")]).astype(jnp.int32)
    return pl.pallas_call(
        conv_kernel,
        out_shape=jax.ShapeDtypeStruct((4, 16, 16, 128), BF),
        in_specs=[pl.BlockSpec(memory_space=pltpu.SMEM)] + [VM] * 5,
        out_specs=VM,
        scratch_shapes=[pltpu.VMEM((4, 16, 16, 128), F32)],
        compiler_params=pltpu.CompilerParams(vmem_limit_bytes=48 * 1024 * 1024),
        cost_estimate=pl.CostEstimate(flops=2 * 10**9, bytes_accessed=3000000, transcendentals=0),
    )(place, normed, left, right, conv_first.reshape(27, 256, 128), merged)


def solution(mesh):
    cut = Mesh(mesh.devices.reshape(8, 2, 8, 2), ("z", "core", "gy", "seq"))
    tokens = P(("z", "core", "gy", "seq"), None)
    voxels = P(("z", "core"), "gy", "seq", None)
    return jax.shard_map(
        body, mesh=cut, in_specs=(voxels, tokens, tokens, P(), P(), P()), out_specs=voxels, check_vma=False
    )
```

time: 1510 us -> 81.2 us (0.05)
  waiting for transfers between devices: 1440 us -> 18.1 us
  blocking collectives: 0 us -> 38.1 us
  matrix products: 23.6 us -> 0 us
    all_gather x2 -> x0, waiting for transfers between devices: 1410 us -> none  [the longest x1 712 us: body(): lax.all_gather(keys, ('gx', 'gy', 'seq'), axis=0, tiled=True)]
    all_to_all x0 -> x2, blocking collectives: none -> 38.1 us  [the longest x1 22.4 us: body(): lax.all_to_all(jnp.broadcast_to(pair, (8, 256, HD)), 'z', 0, 0, tiled=True)]
    dot_general x35 -> x0, matrix products: 23.6 us -> none  [the longest x8 12 us: full_attention(): jnp.dot(weights, value_rows[:, head * head_size:(head + 1) * head_size],...]
    ppermute x12 -> x3, waiting for transfers between devices: 23.1 us -> 3.51 us  [the longest x1 1.54 us: body(): other = lax.ppermute(own, 'core', [(0, 1), (1, 0)])]
  transfers between devices with their start and end apart: 14 -> 4, of which waited for: 8 -> 4; matrix products, arithmetic and copies ran while one was open for 1% -> 0% of each run, Pallas kernels for 0% -> 1%
where the time goes in v1:
time: 81.2 us; the launch traced here: 80.8 us
  blocking collectives  38.1 us (47%)
  waiting for transfers between devices  18.1 us (22%)
  starting transfers between devices  13.4 us (17%)
  Pallas kernels  8.45 us (10%)
  local copies, waits for them, and re-layouts  2.48 us (3%)
    all_to_all x1, blocking collectives, body(): lax.all_to_all(jnp.broadcast_to(pair, (8, 256, HD)), 'z', 0, 0, tiled=True)  22.4 us
    all_to_all x1, blocking collectives, body(): got = lax.all_to_all(sent, plane, 0, 0, tiled=True)  15.7 us
    all_to_all x1, waiting for transfers between devices, body(): back = lax.all_to_all(attended, plane, 0, 0, tiled=True)  14.6 us
    ppermute x1, starting transfers between devices, body(): other = lax.ppermute(own, 'core', [(0, 1), (1, 0)])  4 us
    pallas_call x1, Pallas kernels, body(): call(attention_kernel, (16, 192, HD), BF, 3, 2 * 10 ** 9)(got, own, other)  3.78 us
    all_to_all x1, starting transfers between devices, body(): back = lax.all_to_all(attended, plane, 0, 0, tiled=True)  3.74 us
    pallas_call x1, Pallas kernels, body(): pl.pallas_call(conv_kernel, out_shape=jax.ShapeDtypeStruct((4, 16, 16, 12...  3.62 us
    ppermute x1, starting transfers between devices, body(): right = lax.ppermute(normed, ('z', 'core'), [(i + 1, i) for i in range(15)])  3.32 us
  transfers between devices with their start and end apart: 4, of which 4 were waited for; matrix products, arithmetic and copies ran while one was open for 0% of the time, Pallas kernels for 1%

profile of v1, /device:TPU:1, one launch (start us, length us, event | category | flops | bytes accessed | tf_op | source)
XLA Modules:
  0.0 80.8 jit_solution(11501878185499612737)
XLA Ops:
  0.0 0.0 copy-start.1
  0.0 0.9 %copy-done.1 = bf16[2,8,8,1024]{3,2,1,0:T(8,128)(2,1)S(1)} copy-done((bf16[2,8,8,1024]{3,2,1,0:T(8,128)(2,1)S(1)}, bf16[2,8,8,1024]{3,2,1,0:T(8,128)(2,1)}, u32[]{:S(2)}) %copy-start.1) | copy-done | bytes 262168
  1.0 0.0 copy-start.2
  1.0 0.7 copy-done.2
  1.7 0.0 copy-start.3
  1.7 0.7 copy-done.3
  2.4 0.1 shard_map.64
  2.4 15.7 %all_to_all.15.q_ref = bf16[16,80,128]{2,1,0:T(8,128)(2,1)S(1)} all-to-all(bf16[16,80,128]{2,1,0:T(8,128)(2,1)S(1)} %shard_map.64), channel_id=1, replica_groups=mesh['z'=8,'core'=2,'gy'=8,'seq'=2] {'gy','seq'}, dimensions={0} | all-to-all | bytes 655360 | tf_op jit(solution)/shard_map/all_to_all | solution.py:147
  18.2 0.1 broadcast_in_dim.8
  18.3 22.4 %all_to_all.16.own_ref = bf16[8,256,128]{2,1,0:T(8,128)(2,1)S(1)} all-to-all(bf16[8,256,128]{2,1,0:T(8,128)(2,1)S(1)} %broadcast_in_dim.8), channel_id=1, replica_groups=mesh['z'=8,'core'=2,'gy'=8,'seq'=2] {'z'}, dimensions={0} | all-to-all | bytes 1048576 | tf_op jit(solution)/shard_map/all_to_all | solution.py:149
  40.7 0.0 copy-start
  40.7 4.0 %collective-permute-start = (bf16[8,256,128]{2,1,0:T(8,128)(2,1)S(1)}, bf16[8,256,128]{2,1,0:T(8,128)(2,1)S(1)}, u32[]{:S(2)}, u32[]{:S(2)}) collective-permute-start(bf16[8,256,128]{2,1,0:T(8,128)(2,1)S(1)} %all_to_all.16.own_ref), channel_id=1, source_target_pairs={{0,16},{16,0},{1,17},{17,1},{2,18},{18,2},{3,19},{19,3},{4,20},{20... | collective-permute-start | bytes 1572872 | tf_op jit(solution)/shard_map/ppermute | solution.py:150
  44.7 1.5 %collective-permute-done.other_ref = bf16[8,256,128]{2,1,0:T(8,128)(2,1)S(1)} collective-permute-done((bf16[8,256,128]{2,1,0:T(8,128)(2,1)S(1)}, bf16[8,256,128]{2,1,0:T(8,128)(2,1)S(1)}, u32[]{:S(2)}, u32[]{:S(2)}) %collective-permute-start) | collective-permute-done | bytes 524320 | tf_op jit(solution)/shard_map/ppermute | solution.py:150
  46.2 3.8 %shard_map.65 = bf16[16,192,128]{2,1,0:T(8,128)(2,1)} custom-call(bf16[16,80,128]{2,1,0:T(8,128)(2,1)S(1)} %all_to_all.15.q_ref, bf16[8,256,128]{2,1,0:T(8,128)(2,1)S(1)} %all_to_all.16.own_ref, bf16[8,256,128]{2,1,0:T(8,128)(2,1)S(1)} %collective-permute-done.other_ref), custom_call_target="tpu_custom_call" | custom-call | flops 2000000000 | bytes 1000000 | tf_op jit(solution)/shard_map/pallas_call | solution.py:151
  50.0 0.0 copy-start.5
  50.0 3.7 %all-to-all-start.2 = ((bf16[16,192,128]{2,1,0:T(8,128)(2,1)}), bf16[16,192,128]{2,1,0:T(8,128)(2,1)S(1)}, u32[]{:S(2)}, u32[]{:S(2)}) async-start(bf16[16,192,128]{2,1,0:T(8,128)(2,1)} %shard_map.65), calls=%async_computation.2 | async-start | bytes 1572864 | tf_op jit(solution)/shard_map/all_to_all | solution.py:152
  53.8 14.6 %all-to-all-done.2.a_ref = bf16[16,192,128]{2,1,0:T(8,128)(2,1)S(1)} async-done(((bf16[16,192,128]{2,1,0:T(8,128)(2,1)}), bf16[16,192,128]{2,1,0:T(8,128)(2,1)S(1)}, u32[]{:S(2)}, u32[]{:S(2)}) %all-to-all-start.2) | async-done | bytes 786464 | tf_op jit(solution)/shard_map/all_to_all | solution.py:152
  68.3 0.0 copy-done
  68.3 0.5 shard_map.66.own_ref
  68.8 0.0 copy-start.4
  68.8 3.3 %collective-permute-start.2 = (bf16[2,192,256]{2,1,0:T(8,128)(2,1)S(1)}, bf16[2,192,256]{2,1,0:T(8,128)(2,1)S(1)}, u32[]{:S(2)}, u32[]{:S(2)}) collective-permute-start(bf16[2,192,256]{2,1,0:T(8,128)(2,1)S(1)} %shard_map.66.own_ref), channel_id=1, source_target_pairs={{16,0},{32,16},{48,32},{64,48},{80,64},{96,80},{112,96},{128,112},... | collective-permute-start | bytes 589832 | tf_op jit(solution)/shard_map/ppermute | solution.py:155
  72.2 2.4 %collective-permute-start.1 = (bf16[2,192,256]{2,1,0:T(8,128)(2,1)S(1)}, bf16[2,192,256]{2,1,0:T(8,128)(2,1)S(1)}, u32[]{:S(2)}, u32[]{:S(2)}) collective-permute-start(bf16[2,192,256]{2,1,0:T(8,128)(2,1)S(1)} %shard_map.66.own_ref), channel_id=1, source_target_pairs={{0,16},{16,32},{32,48},{48,64},{64,80},{80,96},{96,112},{112,128},... | collective-permute-start | bytes 589832 | tf_op jit(solution)/shard_map/ppermute | solution.py:154
  74.5 0.0 copy-done.5
  74.6 0.5 shard_map.67.w2_ref
  75.1 0.1 pad_add_fusion.where_ref
  75.2 0.8 collective-permute-done.2.right_ref
  76.0 1.2 %collective-permute-done.1.left_ref = bf16[2,192,256]{2,1,0:T(8,128)(2,1)S(1)} collective-permute-done((bf16[2,192,256]{2,1,0:T(8,128)(2,1)S(1)}, bf16[2,192,256]{2,1,0:T(8,128)(2,1)S(1)}, u32[]{:S(2)}, u32[]{:S(2)}) %collective-permute-start.1) | collective-permute-done | bytes 196640 | tf_op jit(solution)/shard_map/ppermute | solution.py:154
  77.1 0.0 copy-done.4
  77.1 3.6 %shard_map.68 = bf16[4,16,16,128]{3,2,1,0:T(8,128)(2,1)} custom-call(s32[3]{0:T(128)S(1)} %pad_add_fusion.where_ref, bf16[2,192,256]{2,1,0:T(8,128)(2,1)S(1)} %shard_map.66.own_ref, bf16[2,192,256]{2,1,0:T(8,128)(2,1)S(1)} %collective-permute-done.1.left_ref, bf16[2,192,256]{2,1,0:T(8,128)(2,1)S(1)} %collective-permute-done.2.right_ref, ...), custom_call_target="tpu_custom_call" | custom-call | flops 2000000000 | bytes 3000000 | tf_op jit(solution)/shard_map/pallas_call | solution.py:158
  (2 shorter events, 0.0 us)
Async XLA Ops:
  0.0 0.9 %copy-start.1 = (bf16[2,8,8,1024]{3,2,1,0:T(8,128)(2,1)S(1)}, bf16[2,8,8,1024]{3,2,1,0:T(8,128)(2,1)}, u32[]{:S(2)}) copy-start(bf16[2,8,8,1024]{3,2,1,0:T(8,128)(2,1)} %param.6) | copy-start | bytes 786436
  1.0 0.7 copy-start.2
  1.7 0.7 copy-start.3
  40.7 27.7 %copy-start = (bf16[1024,256]{1,0:T(8,128)(2,1)S(1)}, bf16[1024,256]{1,0:T(8,128)(2,1)}, u32[]{:S(2)}) copy-start(bf16[1024,256]{1,0:T(8,128)(2,1)} %w_ref.1) | copy-start | bytes 1572868
  40.7 5.5 %collective-permute-start = (bf16[8,256,128]{2,1,0:T(8,128)(2,1)S(1)}, bf16[8,256,128]{2,1,0:T(8,128)(2,1)S(1)}, u32[]{:S(2)}, u32[]{:S(2)}) collective-permute-start(bf16[8,256,128]{2,1,0:T(8,128)(2,1)S(1)} %all_to_all.16.own_ref), channel_id=1, source_target_pairs={{0,16},{16,0},{1,17},{17,1},{2,18},{18,2},{3,19},{19,3},{4,20},{20... | collective-permute-start | bytes 1572872 | tf_op jit(solution)/shard_map/ppermute | solution.py:150
  50.0 24.5 %copy-start.5 = (bf16[3,3,3,128,128]{4,3,2,1,0:T(8,128)(2,1)S(1)}, bf16[3,3,3,128,128]{4,3,2,1,0:T(8,128)(2,1)}, u32[]{:S(2)}) copy-start(bf16[3,3,3,128,128]{4,3,2,1,0:T(8,128)(2,1)} %param.11) | copy-start | bytes 2654212
  50.0 18.3 %all-to-all-start.2 = ((bf16[16,192,128]{2,1,0:T(8,128)(2,1)}), bf16[16,192,128]{2,1,0:T(8,128)(2,1)S(1)}, u32[]{:S(2)}, u32[]{:S(2)}) async-start(bf16[16,192,128]{2,1,0:T(8,128)(2,1)} %shard_map.65), calls=%async_computation.2 | async-start | bytes 1572864 | tf_op jit(solution)/shard_map/all_to_all | solution.py:152
  68.8 8.3 %copy-start.4 = (bf16[3,3,3,256,128]{4,3,2,1,0:T(8,128)(2,1)S(1)}, bf16[3,3,3,256,128]{4,3,2,1,0:T(8,128)(2,1)}, u32[]{:S(2)}) copy-start(bf16[3,3,3,256,128]{4,3,2,1,0:T(8,128)(2,1)} %param.10) | copy-start | bytes 5308420
  68.8 7.1 %collective-permute-start.2 = (bf16[2,192,256]{2,1,0:T(8,128)(2,1)S(1)}, bf16[2,192,256]{2,1,0:T(8,128)(2,1)S(1)}, u32[]{:S(2)}, u32[]{:S(2)}) collective-permute-start(bf16[2,192,256]{2,1,0:T(8,128)(2,1)S(1)} %shard_map.66.own_ref), channel_id=1, source_target_pairs={{16,0},{32,16},{48,32},{64,48},{80,64},{96,80},{112,96},{128,112},... | collective-permute-start | bytes 589832 | tf_op jit(solution)/shard_map/ppermute | solution.py:155
  72.2 5.0 %collective-permute-start.1 = (bf16[2,192,256]{2,1,0:T(8,128)(2,1)S(1)}, bf16[2,192,256]{2,1,0:T(8,128)(2,1)S(1)}, u32[]{:S(2)}, u32[]{:S(2)}) collective-permute-start(bf16[2,192,256]{2,1,0:T(8,128)(2,1)S(1)} %shard_map.66.own_ref), channel_id=1, source_target_pairs={{0,16},{16,32},{32,48},{48,64},{64,80},{80,96},{96,112},{112,128},... | collective-permute-start | bytes 589832 | tf_op jit(solution)/shard_map/ppermute | solution.py:154

commit v2 on v1

v2 whole, which is shorter than its diff:
```python
import jax
import jax.numpy as jnp
from jax import lax
from jax.experimental import pallas as pl
from jax.experimental.pallas import tpu as pltpu
from jax.sharding import Mesh, PartitionSpec as P

H = 8
HD = 128
BF = jnp.bfloat16
F32 = jnp.float32
VM = pl.BlockSpec(memory_space=pltpu.VMEM)
SM = pl.BlockSpec(memory_space=pltpu.SMEM)
HB = pl.BlockSpec(memory_space=pltpu.HBM)
LOG2E = 1.4426950408889634


def call(kernel, shape, dtype, in_specs, scratch=()):
    return pl.pallas_call(
        kernel,
        out_shape=jax.ShapeDtypeStruct(shape, dtype),
        in_specs=in_specs,
        out_specs=VM,
        scratch_shapes=list(scratch),
        compiler_params=pltpu.CompilerParams(vmem_limit_bytes=48 * 1024 * 1024),
        cost_estimate=pl.CostEstimate(flops=10**9, bytes_accessed=1000000, transcendentals=0),
    )


def pack_kernel(q_hbm, k_hbm, v_hbm, out_ref, q_ref, k_ref, v_ref, sems):
    copies = [
        pltpu.make_async_copy(src, dst, sems.at[i])
        for i, (src, dst) in enumerate(((q_hbm, q_ref), (k_hbm, k_ref), (v_hbm, v_ref)))
    ]
    for copy in copies:
        copy.start()
    for copy in copies:
        copy.wait()
    for h in range(H):
        cols = slice(h * HD, (h + 1) * HD)
        pair = jnp.concatenate([k_ref[:, cols].astype(F32), v_ref[:, cols].astype(F32)], axis=0).astype(BF)
        rows = [q_ref[x, :, cols].astype(F32).reshape(8, 8, HD) for x in range(2)]
        rows = jnp.concatenate(rows, axis=1).reshape(128, HD).astype(BF)
        for s in range(2):
            out_ref[2 * h + s, 0:128] = rows
            out_ref[2 * h + s, 128:144] = pair


def attention_kernel(where_ref, q_ref, own_ref, other_ref, out_ref):
    seq = where_ref[2]
    keys = jnp.concatenate([own_ref[:, 0:128].reshape(1024, HD), other_ref[:, 0:128].reshape(1024, HD)], axis=0)
    vals = jnp.concatenate([own_ref[:, 128:256].reshape(1024, HD), other_ref[:, 128:256].reshape(1024, HD)], axis=0)
    vals = jnp.concatenate([vals, jnp.ones((2048, HD), BF)], axis=1)

    def attend(q):
        scores = lax.dot_general(q, keys, (((1,), (1,)), ((), ())), preferred_element_type=F32)
        top = jnp.max(scores, axis=1, keepdims=True)
        weights = jnp.exp2((scores - top) * (HD**-0.5 * LOG2E)).astype(BF)
        both = jnp.dot(weights, vals, preferred_element_type=F32)
        return both[:, 0:HD] / both[:, HD : 2 * HD]

    edge = jnp.zeros((32, HD), BF)
    out_ref[0, 0:32] = edge
    out_ref[7, 160:192] = edge
    for g in range(0, 8, 2):
        pair = attend(jnp.concatenate([q_ref[2 * g + seq, 0:128], q_ref[2 * g + 2 + seq, 0:128]], axis=0)).astype(BF)
        for n, done in ((g, pair[0:128]), (g + 1, pair[128:256])):
            out_ref[n, 32:160] = done
            if n < 7:
                out_ref[n + 1, 0:32] = done[96:128]
            if n > 0:
                out_ref[n - 1, 160:192] = done[0:32]
    row = lax.broadcasted_iota(jnp.int32, (32, 128), 0)
    col = lax.broadcasted_iota(jnp.int32, (32, 128), 1)
    pick = (col == (row // 2) * 8 + row % 2 + 6 * seq).astype(F32).astype(BF)
    near = [jnp.dot(pick, q_ref[2 * g + 1 - seq, 0:128], preferred_element_type=F32).astype(BF) for g in range(8)]
    done = attend(jnp.concatenate(near, axis=0))
    none = jnp.zeros((8, HD), F32)
    done = jnp.concatenate([none, done, none], axis=0)
    for g in range(8):
        out_ref[g, 192:240] = done[32 * g : 32 * g + 48].astype(BF)


def project_kernel(where_ref, a_ref, w_ref, out_ref):
    seq = where_ref[2]
    rows = jnp.concatenate([a_ref[h] for h in range(H)], axis=1)
    projected = jnp.dot(rows, w_ref[...], preferred_element_type=F32)
    scale = lax.rsqrt(jnp.mean(projected * projected, axis=1, keepdims=True) + 1e-06)
    normed = (projected * scale).astype(BF)
    row = lax.broadcasted_iota(jnp.int32, (384, 1), 0)
    x = (row >= 192).astype(jnp.int32)
    y = (row - 192 * x) // 16
    z = row % 16
    near = z - jnp.where(seq == 0, 10, 0)
    source = jnp.where((near >= 0) & (near < 2), 192 + y * 4 + x * 2 + near, -1)
    source = jnp.where((z >= 2) & (z < 10), y * 16 + x * 8 + z - 2, source)
    place = (lax.broadcasted_iota(jnp.int32, (384, 240), 1) == source).astype(F32).astype(BF)
    out_ref[...] = jnp.dot(place, normed, preferred_element_type=F32).astype(BF).reshape(2, 192, 256)


def merge_kernel(w_ref, out_ref):
    def both(parts):
        return ((parts[0], parts[1] + parts[2]), (parts[0] + parts[1], parts[2]))

    taps = [[[w_ref[9 * a + 3 * b + c].astype(F32) for c in range(3)] for b in range(3)] for a in range(3)]
    on_z = [[[m for p in both(taps[a][b]) for m in p] for b in range(3)] for a in range(3)]
    for n in range(4):
        on_y = [both([on_z[a][b][n] for b in range(3)]) for a in range(3)]
        for py in range(2):
            for b in range(2):
                on_x = both([on_y[a][py][b] for a in range(3)])
                for px in range(2):
                    for a in range(2):
                        rows = (2 * a + b) * 128
                        out_ref[2 * px + py, rows : rows + 128, n * 128 : (n + 1) * 128] = on_x[px][a].astype(BF)


def shifted(x, by):
    return pltpu.roll(x, by % x.shape[0], 0)


def conv_kernel(where_ref, own_ref, near_ref, far_ref, w1_ref, w2_ref, out_ref, field):
    gx, gy, seq = where_ref[0], where_ref[1], where_ref[2]
    first_core = gx % 2 == 0
    none = jnp.zeros((192, 256), BF)
    slabs = [own_ref[0], own_ref[1]]
    left = [jnp.where(gx == 0, none, jnp.where(first_core, far_ref[x], near_ref[x])) for x in range(2)]
    right = [jnp.where(gx == 15, none, jnp.where(first_core, near_ref[x], far_ref[x])) for x in range(2)]
    slabs = left + slabs + right
    row = lax.broadcasted_iota(jnp.int32, (160, 128), 0)
    at_z = seq * 8 - 1 + row % 16
    at_y = gy * 8 - 1 + row // 16
    inside = (at_y >= 0) & (at_y < 64) & (at_z >= 0) & (at_z < 16)
    hidden = []
    for x in range(4):
        total = jnp.zeros((160, 384), F32)
        for a in range(3):
            for b in range(3):
                t = 9 * a + 3 * b
                weight = jnp.concatenate([w1_ref[t], w1_ref[t + 1], w1_ref[t + 2]], axis=1)
                total = total + jnp.dot(slabs[x + a][16 * b : 16 * b + 160], weight, preferred_element_type=F32)
        first = total[:, 0:128] + shifted(total[:, 128:256], -1) + shifted(total[:, 256:384], -2)
        value = first / (1.0 + jnp.exp(-first))
        at_x = gx * 2 - 1 + x
        hidden.append(jnp.where(inside & (at_x >= 0) & (at_x < 32), value, 0.0).astype(BF))
    for px in range(2):
        for py in range(2):
            rows = jnp.concatenate(
                [
                    jnp.concatenate(
                        [
                            hidden[i + px + a][16 * (py + b) : 16 * (py + b) + 128]
                            for a in range(2)
                            for b in range(2)
                        ],
                        axis=1,
                    )
                    for i in range(2)
                ],
                axis=0,
            )
            parts = jnp.dot(rows, w2_ref[2 * px + py], preferred_element_type=F32)
            even = parts[:, 0:128] + shifted(parts[:, 128:256], -1)
            odd = shifted(parts[:, 256:384], -1) + shifted(parts[:, 384:512], -2)
            for pz, part in ((0, even), (1, odd)):
                part = part.reshape(2, 8, 16, 128)
                for i in range(2):
                    for j in range(8):
                        field[2 * i + px, 2 * j + py, pl.ds(pz, 8, stride=2), :] = part[i, j, 0:8]
    out_ref[...] = field[...].astype(BF)


def body(queries, keys, values, w_out, conv_first, conv_second):
    z, core, gy, seq = (lax.axis_index(name) for name in ("z", "core", "gy", "seq"))
    place = jnp.stack([2 * z + core, gy, seq]).astype(jnp.int32)
    sent = call(
        pack_kernel,
        (16, 144, HD),
        BF,
        [HB] * 3,
        [
            pltpu.VMEM((2, 64, H * HD), BF),
            pltpu.VMEM((8, H * HD), BF),
            pltpu.VMEM((8, H * HD), BF),
            pltpu.SemaphoreType.DMA((3,)),
        ],
    )(queries.reshape(2, 64, H * HD), keys, values)
    got = lax.all_to_all(sent, ("gy", "seq"), 0, 0, tiled=True)
    pair = got[:, 128:144].reshape(16, 2, 8, HD).transpose(1, 0, 2, 3).reshape(1, 256, HD)
    own = lax.all_to_all(jnp.broadcast_to(pair, (8, 256, HD)), "z", 0, 0, tiled=True)
    other = lax.ppermute(own, "core", [(0, 1), (1, 0)])
    attended = call(attention_kernel, (8, 240, HD), BF, [SM] + [VM] * 3)(place, got, own, other)
    back = lax.all_to_all(attended, "gy", 0, 0, tiled=True)
    normed = call(project_kernel, (2, 192, 256), BF, [SM] + [VM] * 2)(place, back, w_out)
    far = lax.ppermute(normed, ("z", "core"), [(i, (i - 1 + 2 * (i % 2)) % 16) for i in range(16)])
    near = lax.ppermute(normed, "core", [(0, 1), (1, 0)])
    merged = call(merge_kernel, (4, 512, 512), BF, [VM])(conv_second.reshape(27, 128, 128))
    return call(conv_kernel, (4, 16, 16, 128), BF, [SM] + [VM] * 5, [pltpu.VMEM((4, 16, 16, 128), F32)])(
        place, normed, near, far, conv_first.reshape(27, 256, 128), merged
    )


def solution(mesh):
    cut = Mesh(mesh.devices.reshape(8, 2, 8, 2), ("z", "core", "gy", "seq"))
    tokens = P(("z", "core", "gy", "seq"), None)
    voxels = P(("z", "core"), "gy", "seq", None)
    return jax.shard_map(
        body, mesh=cut, in_specs=(voxels, tokens, tokens, P(), P(), P()), out_specs=voxels, check_vma=False
    )
```

time: 81.2 us -> 76.4 us (0.941)
  blocking collectives: 38.1 us -> 52.2 us
  waiting for transfers between devices: 18.1 us -> 4.57 us
  starting transfers between devices: 13.4 us -> 6.24 us
  Pallas kernels: 8.45 us -> 9.8 us
    all_to_all x1 -> x0, waiting for transfers between devices: 14.6 us -> none  [body(): back = lax.all_to_all(attended, plane, 0, 0, tiled=True)]
    all_to_all x1 -> x2, blocking collectives: 15.7 us -> 29.8 us  [the longest x1 18.8 us: body(): got = lax.all_to_all(sent, ('gy', 'seq'), 0, 0, tiled=True)]
    all_to_all x1 -> x0, starting transfers between devices: 3.74 us -> none  [body(): back = lax.all_to_all(attended, plane, 0, 0, tiled=True)]
    ppermute x2, starting transfers between devices: 5.69 us -> 2.23 us  [the longest x1 2.23 us: body(): lax.ppermute(normed, ('z', 'core'), [(i, (i - 1 + 2 * (i % 2)) % 16) for...]
    pallas_call x5, Pallas kernels: 8.45 us -> 9.8 us  [the longest x1 4.32 us: body(): call(attention_kernel, (8, 240, HD), BF, [SM] + [VM] * 3)]
    ppermute x2, waiting for transfers between devices: 1.97 us -> 3.11 us  [the longest x1 3.11 us: body(): lax.ppermute(normed, ('z', 'core'), [(i, (i - 1 + 2 * (i % 2)) % 16) for...]
  transfers between devices with their start and end apart: 4 -> 3, of which waited for: 4 -> 2; matrix products, arithmetic and copies ran while one was open for 0% -> 0% of each run, Pallas kernels for 1% -> 1%
where the time goes in v2:
time: 76.4 us; the launch traced here: 75.5 us
  blocking collectives  52.2 us (68%)
  Pallas kernels  9.8 us (13%)
  starting transfers between devices  6.24 us (8%)
  waiting for transfers between devices  4.57 us (6%)
  local copies, waits for them, and re-layouts  2.48 us (3%)
    all_to_all x1, blocking collectives, body(): lax.all_to_all(jnp.broadcast_to(pair, (8, 256, HD)), 'z', 0, 0, tiled=True)  22.4 us
    all_to_all x1, blocking collectives, body(): got = lax.all_to_all(sent, ('gy', 'seq'), 0, 0, tiled=True)  18.8 us
    all_to_all x1, blocking collectives, body(): back = lax.all_to_all(attended, 'gy', 0, 0, tiled=True)  10.9 us
    pallas_call x1, Pallas kernels, body(): call(attention_kernel, (8, 240, HD), BF, [SM] + [VM] * 3)  4.32 us
    ppermute x1, starting transfers between devices, body(): other = lax.ppermute(own, 'core', [(0, 1), (1, 0)])  4 us
    pallas_call x1, Pallas kernels, body(): call(conv_kernel, (4, 16, 16, 128), BF, [SM] + [VM] * 5, [pltpu.VMEM((4,...  3.61 us
    ppermute x1, waiting for transfers between devices, body(): lax.ppermute(normed, ('z', 'core'), [(i, (i - 1 + 2 * (i % 2)) % 16) for...  3.11 us
    unnamed x12, local copies, waits for them, and re-layouts  2.4 us
  transfers between devices with their start and end apart: 3, of which 2 were waited for; matrix products, arithmetic and copies ran while one was open for 0% of the time, Pallas kernels for 1%

profile of v2, /device:TPU:1, one launch (start us, length us, event | category | flops | bytes accessed | tf_op | source)
XLA Modules:
  0.0 75.5 jit_solution(16118293624258627079)
XLA Ops:
  0.0 0.0 copy-start.3
  0.0 0.9 %copy-done.3 = bf16[2,8,8,1024]{3,2,1,0:T(8,128)(2,1)S(1)} copy-done((bf16[2,8,8,1024]{3,2,1,0:T(8,128)(2,1)S(1)}, bf16[2,8,8,1024]{3,2,1,0:T(8,128)(2,1)}, u32[]{:S(2)}) %copy-start.3) | copy-done | bytes 262168
  1.0 0.0 copy-start.4
  1.0 0.7 copy-done.4
  1.7 0.0 copy-start.5
  1.7 0.7 copy-done.5
  2.4 0.2 shard_map.64
  2.6 18.8 %all_to_all.15.q_ref = bf16[16,144,128]{2,1,0:T(8,128)(2,1)S(1)} all-to-all(bf16[16,144,128]{2,1,0:T(8,128)(2,1)S(1)} %shard_map.64), channel_id=1, replica_groups=mesh['z'=8,'core'=2,'gy'=8,'seq'=2] {'gy','seq'}, dimensions={0} | all-to-all | bytes 1179648 | tf_op jit(solution)/shard_map/all_to_all | solution.py:188
  21.4 0.1 broadcast_in_dim.8
  21.5 22.4 %all_to_all.16.own_ref = bf16[8,256,128]{2,1,0:T(8,128)(2,1)S(1)} all-to-all(bf16[8,256,128]{2,1,0:T(8,128)(2,1)S(1)} %broadcast_in_dim.8), channel_id=1, replica_groups=mesh['z'=8,'core'=2,'gy'=8,'seq'=2] {'z'}, dimensions={0} | all-to-all | bytes 1048576 | tf_op jit(solution)/shard_map/all_to_all | solution.py:190
  43.9 4.0 %collective-permute-start = (bf16[8,256,128]{2,1,0:T(8,128)(2,1)S(1)}, bf16[8,256,128]{2,1,0:T(8,128)(2,1)S(1)}, u32[]{:S(2)}, u32[]{:S(2)}) collective-permute-start(bf16[8,256,128]{2,1,0:T(8,128)(2,1)S(1)} %all_to_all.16.own_ref), channel_id=1, source_target_pairs={{0,16},{16,0},{1,17},{17,1},{2,18},{18,2},{3,19},{19,3},{4,20},{20... | collective-permute-start | bytes 1572872 | tf_op jit(solution)/shard_map/ppermute | solution.py:191
  47.9 0.1 pad_add_fusion.where_ref
  48.0 0.0 copy-start.2
  48.0 1.5 %collective-permute-done.other_ref = bf16[8,256,128]{2,1,0:T(8,128)(2,1)S(1)} collective-permute-done((bf16[8,256,128]{2,1,0:T(8,128)(2,1)S(1)}, bf16[8,256,128]{2,1,0:T(8,128)(2,1)S(1)}, u32[]{:S(2)}, u32[]{:S(2)}) %collective-permute-start) | collective-permute-done | bytes 524320 | tf_op jit(solution)/shard_map/ppermute | solution.py:191
  49.5 4.3 %shard_map.65 = bf16[8,240,128]{2,1,0:T(8,128)(2,1)S(1)} custom-call(s32[3]{0:T(128)S(1)} %pad_add_fusion.where_ref, bf16[16,144,128]{2,1,0:T(8,128)(2,1)S(1)} %all_to_all.15.q_ref, bf16[8,256,128]{2,1,0:T(8,128)(2,1)S(1)} %all_to_all.16.own_ref, bf16[8,256,128]{2,1,0:T(8,128)(2,1)S(1)} %collective-permute-done.other_ref), custom_call_target="tpu_custom_call" | custom-call | flops 1000000000 | bytes 1000000 | tf_op jit(solution)/shard_map/pallas_call | solution.py:192
  53.8 0.0 copy-start.1
  53.8 10.9 %all_to_all.17.a_ref = bf16[8,240,128]{2,1,0:T(8,128)(2,1)S(1)} all-to-all(bf16[8,240,128]{2,1,0:T(8,128)(2,1)S(1)} %shard_map.65), channel_id=1, replica_groups=mesh['z'=8,'core'=2,'gy'=8,'seq'=2] {'gy'}, dimensions={0} | all-to-all | bytes 983040 | tf_op jit(solution)/shard_map/all_to_all | solution.py:193
  64.8 0.0 copy-done.2
  64.8 1.2 %shard_map.66.own_ref = bf16[2,192,256]{2,1,0:T(8,128)(2,1)S(1)} custom-call(s32[3]{0:T(128)S(1)} %pad_add_fusion.where_ref, bf16[8,240,128]{2,1,0:T(8,128)(2,1)S(1)} %all_to_all.17.a_ref, bf16[1024,256]{1,0:T(8,128)(2,1)S(1)} %copy-done.2), custom_call_target="tpu_custom_call" | custom-call | flops 1000000000 | bytes 1000000 | tf_op jit(solution)/shard_map/pallas_call | solution.py:194
  66.0 0.0 copy-start
  66.0 2.2 %collective-permute-start.2 = (bf16[2,192,256]{2,1,0:T(8,128)(2,1)S(1)}, bf16[2,192,256]{2,1,0:T(8,128)(2,1)S(1)}, u32[]{:S(2)}, u32[]{:S(2)}) collective-permute-start(bf16[2,192,256]{2,1,0:T(8,128)(2,1)S(1)} %shard_map.66.own_ref), channel_id=1, source_target_pairs={{0,240},{16,32},{32,16},{48,64},{64,48},{80,96},{96,80},{112,128},... | collective-permute-start | bytes 589832 | tf_op jit(solution)/shard_map/ppermute | solution.py:195
  68.2 0.0 collective-permute-start.1
  68.2 0.0 copy-done.1
  68.2 0.5 shard_map.67.w2_ref
  68.7 3.1 %collective-permute-done.2.far_ref = bf16[2,192,256]{2,1,0:T(8,128)(2,1)S(1)} collective-permute-done((bf16[2,192,256]{2,1,0:T(8,128)(2,1)S(1)}, bf16[2,192,256]{2,1,0:T(8,128)(2,1)S(1)}, u32[]{:S(2)}, u32[]{:S(2)}) %collective-permute-start.2) | collective-permute-done | bytes 196640 | tf_op jit(solution)/shard_map/ppermute | solution.py:195
  71.8 0.0 collective-permute-done.1.near_ref
  71.8 0.0 copy-done
  71.9 3.6 %shard_map.68 = bf16[4,16,16,128]{3,2,1,0:T(8,128)(2,1)} custom-call(s32[3]{0:T(128)S(1)} %pad_add_fusion.where_ref, bf16[2,192,256]{2,1,0:T(8,128)(2,1)S(1)} %shard_map.66.own_ref, bf16[2,192,256]{2,1,0:T(8,128)(2,1)S(1)} %collective-permute-done.1.near_ref, bf16[2,192,256]{2,1,0:T(8,128)(2,1)S(1)} %collective-permute-done.2.far_ref, ...), custom_call_target="tpu_custom_call" | custom-call | flops 1000000000 | bytes 1000000 | tf_op jit(solution)/shard_map/pallas_call | solution.py:198
  (2 shorter events, 0.0 us)
Async XLA Ops:
  0.0 0.9 %copy-start.3 = (bf16[2,8,8,1024]{3,2,1,0:T(8,128)(2,1)S(1)}, bf16[2,8,8,1024]{3,2,1,0:T(8,128)(2,1)}, u32[]{:S(2)}) copy-start(bf16[2,8,8,1024]{3,2,1,0:T(8,128)(2,1)} %param.6) | copy-start | bytes 786436
  1.0 0.7 copy-start.4
  1.7 0.7 copy-start.5
  43.9 5.5 %collective-permute-start = (bf16[8,256,128]{2,1,0:T(8,128)(2,1)S(1)}, bf16[8,256,128]{2,1,0:T(8,128)(2,1)S(1)}, u32[]{:S(2)}, u32[]{:S(2)}) collective-permute-start(bf16[8,256,128]{2,1,0:T(8,128)(2,1)S(1)} %all_to_all.16.own_ref), channel_id=1, source_target_pairs={{0,16},{16,0},{1,17},{17,1},{2,18},{18,2},{3,19},{19,3},{4,20},{20... | collective-permute-start | bytes 1572872 | tf_op jit(solution)/shard_map/ppermute | solution.py:191
  48.0 16.8 %copy-start.2 = (bf16[1024,256]{1,0:T(8,128)(2,1)S(1)}, bf16[1024,256]{1,0:T(8,128)(2,1)}, u32[]{:S(2)}) copy-start(bf16[1024,256]{1,0:T(8,128)(2,1)} %w_ref.1) | copy-start | bytes 1572868
  53.8 14.4 %copy-start.1 = (bf16[3,3,3,128,128]{4,3,2,1,0:T(8,128)(2,1)S(1)}, bf16[3,3,3,128,128]{4,3,2,1,0:T(8,128)(2,1)}, u32[]{:S(2)}) copy-start(bf16[3,3,3,128,128]{4,3,2,1,0:T(8,128)(2,1)} %param.11) | copy-start | bytes 2654212
  66.0 5.9 %copy-start = (bf16[3,3,3,256,128]{4,3,2,1,0:T(8,128)(2,1)S(1)}, bf16[3,3,3,256,128]{4,3,2,1,0:T(8,128)(2,1)}, u32[]{:S(2)}) copy-start(bf16[3,3,3,256,128]{4,3,2,1,0:T(8,128)(2,1)} %param.10) | copy-start | bytes 5308420
  66.0 5.9 %collective-permute-start.2 = (bf16[2,192,256]{2,1,0:T(8,128)(2,1)S(1)}, bf16[2,192,256]{2,1,0:T(8,128)(2,1)S(1)}, u32[]{:S(2)}, u32[]{:S(2)}) collective-permute-start(bf16[2,192,256]{2,1,0:T(8,128)(2,1)S(1)} %shard_map.66.own_ref), channel_id=1, source_target_pairs={{0,240},{16,32},{32,16},{48,64},{64,48},{80,96},{96,80},{112,128},... | collective-permute-start | bytes 589832 | tf_op jit(solution)/shard_map/ppermute | solution.py:195
  68.2 3.7 %collective-permute-start.1 = (bf16[2,192,256]{2,1,0:T(8,128)(2,1)S(1)}, bf16[2,192,256]{2,1,0:T(8,128)(2,1)S(1)}, u32[]{:S(2)}, u32[]{:S(2)}) collective-permute-start(bf16[2,192,256]{2,1,0:T(8,128)(2,1)S(1)} %shard_map.66.own_ref), channel_id=1, source_target_pairs={{0,16},{16,0},{1,17},{17,1},{2,18},{18,2},{3,19},{19,3},{4,20},{20... | collective-permute-start | bytes 589832 | tf_op jit(solution)/shard_map/ppermute | solution.py:196

commit v3 on v2

v3 whole, which is shorter than its diff:
```python
import jax
import jax.numpy as jnp
from jax import lax
from jax.experimental import pallas as pl
from jax.experimental.pallas import tpu as pltpu
from jax.sharding import Mesh, PartitionSpec as P

H = 8
HD = 128
BF = jnp.bfloat16
F32 = jnp.float32
VM = pl.BlockSpec(memory_space=pltpu.VMEM)
SM = pl.BlockSpec(memory_space=pltpu.SMEM)
HB = pl.BlockSpec(memory_space=pltpu.HBM)
SCALE = HD**-0.5 * 1.4426950408889634


def call(kernel, shapes, dtypes, in_specs, scratch=(), room=48):
    outs = [jax.ShapeDtypeStruct(shape, dtype) for shape, dtype in zip(shapes, dtypes)]
    one = len(outs) == 1
    return pl.pallas_call(
        kernel,
        out_shape=outs[0] if one else outs,
        in_specs=in_specs,
        out_specs=VM if one else [VM] * len(outs),
        scratch_shapes=list(scratch),
        compiler_params=pltpu.CompilerParams(vmem_limit_bytes=room * 1024 * 1024),
        cost_estimate=pl.CostEstimate(flops=10**9, bytes_accessed=1000000, transcendentals=0),
    )


def pack_kernel(q_hbm, k_hbm, v_hbm, out_ref, q_ref, k_ref, v_ref, sems):
    copies = [
        pltpu.make_async_copy(src, dst, sems.at[i])
        for i, (src, dst) in enumerate(((q_hbm, q_ref), (k_hbm, k_ref), (v_hbm, v_ref)))
    ]
    for copy in copies:
        copy.start()
    for copy in copies:
        copy.wait()
    for h in range(H):
        cols = slice(h * HD, (h + 1) * HD)
        pair = jnp.concatenate([k_ref[:, cols].astype(F32), v_ref[:, cols].astype(F32)], axis=0).astype(BF)
        rows = [q_ref[x, :, cols].astype(F32).reshape(8, 8, HD) for x in range(2)]
        rows = jnp.concatenate(rows, axis=1).reshape(128, HD).astype(BF)
        for s in range(2):
            out_ref[2 * h + s, 0:128] = rows
            out_ref[2 * h + s, 128:144] = pair


def halves(ref):
    keys = ref[:, 0:128].reshape(1024, HD)
    return keys, jnp.concatenate([ref[:, 128:256].reshape(1024, HD), jnp.ones((1024, HD), BF)], axis=1)


def scores_of(q, keys):
    scores = lax.dot_general(q, keys, (((1,), (1,)), ((), ())), preferred_element_type=F32)
    return scores, jnp.max(scores, axis=1, keepdims=True)


def first_half_kernel(where_ref, q_ref, kv_ref, q_out, sum_out, top_out):
    seq = where_ref[2]
    keys, vals = halves(kv_ref)
    row = lax.broadcasted_iota(jnp.int32, (32, 128), 0)
    col = lax.broadcasted_iota(jnp.int32, (32, 128), 1)
    pick = (col == (row // 2) * 8 + row % 2 + 6 * seq).astype(F32).astype(BF)
    near = [jnp.dot(pick, q_ref[2 * g + 1 - seq, 0:128], preferred_element_type=F32).astype(BF) for g in range(8)]
    for n in range(10):
        rows = slice(128 * n, 128 * n + 128)
        q = q_ref[2 * n + seq, 0:128] if n < 8 else jnp.concatenate(near[4 * n - 32 : 4 * n - 28], axis=0)
        scores, top = scores_of(q, keys)
        weights = jnp.exp2((scores - top) * SCALE).astype(BF)
        q_out[rows] = q
        sum_out[rows] = jnp.dot(weights, vals, preferred_element_type=F32)
        top_out[rows] = jnp.broadcast_to(top, (128, HD))


def second_half_kernel(q_ref, kv_ref, sum_ref, top_ref, out_ref):
    keys, vals = halves(kv_ref)
    edge = jnp.zeros((32, HD), BF)
    out_ref[0, 0:32] = edge
    out_ref[7, 160:192] = edge
    near = []
    for n in range(10):
        rows = slice(128 * n, 128 * n + 128)
        scores, top = scores_of(q_ref[rows], keys)
        before = top_ref[rows, 0:1]
        top = jnp.maximum(top, before)
        weights = jnp.exp2((scores - top) * SCALE).astype(BF)
        kept = jnp.exp2((before - top) * SCALE)
        both = sum_ref[rows] * kept + jnp.dot(weights, vals, preferred_element_type=F32)
        done = both[:, 0:HD] / both[:, HD : 2 * HD]
        if n >= 8:
            near.append(done)
            continue
        done = done.astype(BF)
        out_ref[n, 32:160] = done
        if n < 7:
            out_ref[n + 1, 0:32] = done[96:128]
        if n > 0:
            out_ref[n - 1, 160:192] = done[0:32]
    none = jnp.zeros((8, HD), F32)
    near = jnp.concatenate([none] + near + [none], axis=0)
    for g in range(8):
        out_ref[g, 192:240] = near[32 * g : 32 * g + 48].astype(BF)


def project_kernel(where_ref, a_ref, w_ref, out_ref):
    seq = where_ref[2]
    rows = jnp.concatenate([a_ref[h] for h in range(H)], axis=1)
    projected = jnp.dot(rows, w_ref[...], preferred_element_type=F32)
    scale = lax.rsqrt(jnp.mean(projected * projected, axis=1, keepdims=True) + 1e-06)
    normed = projected * scale
    half = normed[0:192].reshape(12, 2, 8, 256)
    near = normed[192:240].reshape(6, 8, 256)
    row = lax.broadcasted_iota(jnp.int32, (12, 8, 256), 1)
    for x in range(2):
        middle = pltpu.roll(half[:, x], 2, 1)
        ends = [pltpu.roll(near, (8 - 4 * odd - 2 * x) % 8, 1) if odd + x else near for odd in range(2)]
        ends = jnp.stack(ends, axis=1).reshape(12, 8, 256)
        upper = jnp.where(row < 2, jnp.where(seq == 1, ends, 0.0), middle)
        lower = jnp.where((row < 4) & (seq == 0), pltpu.roll(ends, 2, 1), 0.0)
        lower = jnp.where(row < 2, middle, lower)
        out_ref[x] = jnp.concatenate([upper, lower], axis=1).reshape(192, 256).astype(BF)


def merge_kernel(w_ref, out_ref):
    def both(parts):
        return ((parts[0], parts[1] + parts[2]), (parts[0] + parts[1], parts[2]))

    taps = [[[w_ref[9 * a + 3 * b + c].astype(F32) for c in range(3)] for b in range(3)] for a in range(3)]
    on_z = [[[m for p in both(taps[a][b]) for m in p] for b in range(3)] for a in range(3)]
    for n in range(4):
        on_y = [both([on_z[a][b][n] for b in range(3)]) for a in range(3)]
        for py in range(2):
            for b in range(2):
                on_x = both([on_y[a][py][b] for a in range(3)])
                for px in range(2):
                    for a in range(2):
                        rows = (2 * a + b) * 128
                        out_ref[2 * px + py, rows : rows + 128, n * 128 : (n + 1) * 128] = on_x[px][a].astype(BF)


def shifted(x, by):
    return pltpu.roll(x, by % x.shape[0], 0)


def taps(w1_ref, a, b):
    t = 9 * a + 3 * b
    return jnp.concatenate([w1_ref[t], w1_ref[t + 1], w1_ref[t + 2]], axis=1)


def own_conv_kernel(own_ref, w1_ref, out_ref):
    for x in range(4):
        total = jnp.zeros((160, 384), F32)
        for a in range(3):
            if 2 <= x + a < 4:
                for b in range(3):
                    part = own_ref[x + a - 2, 16 * b : 16 * b + 160]
                    total = total + jnp.dot(part, taps(w1_ref, a, b), preferred_element_type=F32)
        out_ref[x] = total


def conv_kernel(where_ref, own_ref, near_ref, far_ref, w1_ref, w2_ref, out_ref, field):
    gx, gy, seq = where_ref[0], where_ref[1], where_ref[2]
    first_core = gx % 2 == 0
    none = jnp.zeros((192, 256), BF)
    left = [jnp.where(gx == 0, none, jnp.where(first_core, far_ref[x], near_ref[x])) for x in range(2)]
    right = [jnp.where(gx == 15, none, jnp.where(first_core, near_ref[x], far_ref[x])) for x in range(2)]
    slabs = left + [None, None] + right
    row = lax.broadcasted_iota(jnp.int32, (160, 128), 0)
    at_z = seq * 8 - 1 + row % 16
    at_y = gy * 8 - 1 + row // 16
    inside = (at_y >= 0) & (at_y < 64) & (at_z >= 0) & (at_z < 16)
    hidden = []
    for x in range(4):
        total = own_ref[x]
        for a in range(3):
            if slabs[x + a] is not None:
                for b in range(3):
                    part = slabs[x + a][16 * b : 16 * b + 160]
                    total = total + jnp.dot(part, taps(w1_ref, a, b), preferred_element_type=F32)
        first = total[:, 0:128] + shifted(total[:, 128:256], -1) + shifted(total[:, 256:384], -2)
        value = first / (1.0 + jnp.exp(-first))
        at_x = gx * 2 - 1 + x
        hidden.append(jnp.where(inside & (at_x >= 0) & (at_x < 32), value, 0.0).astype(BF))
    for px in range(2):
        for py in range(2):
            rows = jnp.concatenate(
                [
                    jnp.concatenate(
                        [
                            hidden[i + px + a][16 * (py + b) : 16 * (py + b) + 128]
                            for a in range(2)
                            for b in range(2)
                        ],
                        axis=1,
                    )
                    for i in range(2)
                ],
                axis=0,
            )
            parts = jnp.dot(rows, w2_ref[2 * px + py], preferred_element_type=F32)
            even = parts[:, 0:128] + shifted(parts[:, 128:256], -1)
            odd = shifted(parts[:, 256:384], -1) + shifted(parts[:, 384:512], -2)
            for pz, part in ((0, even), (1, odd)):
                part = part.reshape(2, 8, 16, 128)
                for i in range(2):
                    for j in range(8):
                        field[2 * i + px, 2 * j + py, pl.ds(pz, 8, stride=2), :] = part[i, j, 0:8]
    out_ref[...] = field[...].astype(BF)


def body(queries, keys, values, w_out, conv_first, conv_second):
    z, core, gy, seq = (lax.axis_index(name) for name in ("z", "core", "gy", "seq"))
    place = jnp.stack([2 * z + core, gy, seq]).astype(jnp.int32)
    sent = call(
        pack_kernel,
        [(16, 144, HD)],
        [BF],
        [HB] * 3,
        [
            pltpu.VMEM((2, 64, H * HD), BF),
            pltpu.VMEM((8, H * HD), BF),
            pltpu.VMEM((8, H * HD), BF),
            pltpu.SemaphoreType.DMA((3,)),
        ],
        room=62,
    )(queries.reshape(2, 64, H * HD), keys, values)
    got = lax.all_to_all(sent, ("gy", "seq"), 0, 0, tiled=True)
    pair = got[:, 128:144].reshape(16, 2, 8, HD).transpose(1, 0, 2, 3).reshape(1, 256, HD)
    own = lax.all_to_all(jnp.broadcast_to(pair, (8, 256, HD)), "z", 0, 0, tiled=True)
    other = lax.ppermute(own, "core", [(0, 1), (1, 0)])
    half = call(first_half_kernel, [(1280, HD), (1280, 2 * HD), (1280, HD)], [BF, F32, F32], [SM, VM, VM])
    q, summed, top = half(place, got, own)
    attended = call(second_half_kernel, [(8, 240, HD)], [BF], [VM] * 4)(q, other, summed, top)
    back = lax.all_to_all(attended, "gy", 0, 0, tiled=True)
    normed = call(project_kernel, [(2, 192, 256)], [BF], [SM, VM, VM])(place, back, w_out)
    far = lax.ppermute(normed, ("z", "core"), [(i, (i - 1 + 2 * (i % 2)) % 16) for i in range(16)])
    near = lax.ppermute(normed, "core", [(0, 1), (1, 0)])
    w1 = conv_first.reshape(27, 256, 128)
    own_part = call(own_conv_kernel, [(4, 160, 384)], [F32], [VM, VM])(normed, w1)
    merged = call(merge_kernel, [(4, 512, 512)], [BF], [VM])(conv_second.reshape(27, 128, 128))
    final = call(conv_kernel, [(4, 16, 16, 128)], [BF], [SM] + [VM] * 5, [pltpu.VMEM((4, 16, 16, 128), F32)])
    return final(place, own_part, near, far, w1, merged)


def solution(mesh):
    cut = Mesh(mesh.devices.reshape(8, 2, 8, 2), ("z", "core", "gy", "seq"))
    tokens = P(("z", "core", "gy", "seq"), None)
    voxels = P(("z", "core"), "gy", "seq", None)
    return jax.shard_map(
        body, mesh=cut, in_specs=(voxels, tokens, tokens, P(), P(), P()), out_specs=voxels, check_vma=False
    )
```

time: 76.4 us -> 74.6 us (0.976)
  Pallas kernels: 9.8 us -> 11.7 us
  waiting for transfers between devices: 4.57 us -> 2.7 us
  local copies, waits for them, and re-layouts: 2.48 us -> 1.03 us
  blocking collectives: 52.2 us -> 53.2 us
    ppermute x1, starting transfers between devices: 2.23 us -> 0.27 us  [body(): lax.ppermute(normed, ('z', 'core'), [(i, (i - 1 + 2 * (i % 2)) % 16) for...]
    pallas_call x5 -> x7, Pallas kernels: 9.8 us -> 11.7 us  [the longest x1 2.84 us: body(): return final(place, own_part, near, far, w1, merged)]
    ppermute x1, waiting for transfers between devices: 1.46 us -> 0.01 us  [body(): other = lax.ppermute(own, 'core', [(0, 1), (1, 0)])]
    unnamed x12 -> x6, local copies, waits for them, and re-layouts: 2.4 us -> 0.95 us
    ppermute x1, starting transfers between devices: 0.01 us -> 1.21 us  [body(): near = lax.ppermute(normed, 'core', [(0, 1), (1, 0)])]
  transfers between devices with their start and end apart: 3 -> 3, of which waited for: 2 -> 1; matrix products, arithmetic and copies ran while one was open for 0% -> 0% of each run, Pallas kernels for 1% -> 5%
where the time goes in v3:
time: 74.6 us; the launch traced here: 74.3 us
  blocking collectives  53.2 us (71%)
  Pallas kernels  11.7 us (16%)
  starting transfers between devices  5.48 us (7%)
  waiting for transfers between devices  2.7 us (4%)
  local copies, waits for them, and re-layouts  1.03 us (1%)
    all_to_all x1, blocking collectives, body(): lax.all_to_all(jnp.broadcast_to(pair, (8, 256, HD)), 'z', 0, 0, tiled=True)  22.4 us
    all_to_all x1, blocking collectives, body(): got = lax.all_to_all(sent, ('gy', 'seq'), 0, 0, tiled=True)  19.1 us
    all_to_all x1, blocking collectives, body(): back = lax.all_to_all(attended, 'gy', 0, 0, tiled=True)  11.7 us
    ppermute x1, starting transfers between devices, body(): other = lax.ppermute(own, 'core', [(0, 1), (1, 0)])  4 us
    pallas_call x1, Pallas kernels, body(): return final(place, own_part, near, far, w1, merged)  2.84 us
    ppermute x1, waiting for transfers between devices, body(): lax.ppermute(normed, ('z', 'core'), [(i, (i - 1 + 2 * (i % 2)) % 16) for...  2.7 us
    pallas_call x1, Pallas kernels, body(): q, summed, top = half(place, got, own)  2.55 us
    pallas_call x1, Pallas kernels, body(): call(second_half_kernel, [(8, 240, HD)], [BF], [VM] * 4)  2.05 us
  transfers between devices with their start and end apart: 3, of which 1 were waited for; matrix products, arithmetic and copies ran while one was open for 0% of the time, Pallas kernels for 5%

profile of v3, /device:TPU:1, one launch (start us, length us, event | category | flops | bytes accessed | tf_op | source)
XLA Modules:
  0.0 74.3 jit_solution(12139675335780142711)
XLA Ops:
  0.0 1.9 %shard_map.64 = bf16[16,144,128]{2,1,0:T(8,128)(2,1)} custom-call(bf16[2,64,1024]{2,1,0:T(8,128)(2,1)} %bitcast.15, bf16[8,1024]{1,0:T(8,128)(2,1)} %k_hbm.1, bf16[8,1024]{1,0:T(8,128)(2,1)} %v_hbm.1), custom_call_target="tpu_custom_call" | custom-call | flops 1000000000 | bytes 1000000 | tf_op jit(solution)/shard_map/pallas_call | solution.py:217
  1.9 19.1 %all_to_all.15.q_ref = bf16[16,144,128]{2,1,0:T(8,128)(2,1)S(1)} all-to-all(bf16[16,144,128]{2,1,0:T(8,128)(2,1)} %shard_map.64), channel_id=1, replica_groups=mesh['z'=8,'core'=2,'gy'=8,'seq'=2] {'gy','seq'}, dimensions={0} | all-to-all | bytes 1179648 | tf_op jit(solution)/shard_map/all_to_all | solution.py:230
  21.0 0.1 broadcast_in_dim.8
  21.0 22.4 %all_to_all.16.kv_ref = bf16[8,256,128]{2,1,0:T(8,128)(2,1)S(1)} all-to-all(bf16[8,256,128]{2,1,0:T(8,128)(2,1)S(1)} %broadcast_in_dim.8), channel_id=1, replica_groups=mesh['z'=8,'core'=2,'gy'=8,'seq'=2] {'z'}, dimensions={0} | all-to-all | bytes 1048576 | tf_op jit(solution)/shard_map/all_to_all | solution.py:232
  43.5 4.0 %collective-permute-start = (bf16[8,256,128]{2,1,0:T(8,128)(2,1)S(1)}, bf16[8,256,128]{2,1,0:T(8,128)(2,1)S(1)}, u32[]{:S(2)}, u32[]{:S(2)}) collective-permute-start(bf16[8,256,128]{2,1,0:T(8,128)(2,1)S(1)} %all_to_all.16.kv_ref), channel_id=1, source_target_pairs={{0,16},{16,0},{1,17},{17,1},{2,18},{18,2},{3,19},{19,3},{4,20},{20... | collective-permute-start | bytes 1572872 | tf_op jit(solution)/shard_map/ppermute | solution.py:233
  47.5 0.1 pad_add_fusion.where_ref
  47.5 2.5 %shard_map.65 = (bf16[1280,128]{1,0:T(8,128)(2,1)S(1)}, f32[1280,256]{1,0:T(8,128)S(1)}, f32[1280,128]{1,0:T(8,128)S(1)}) custom-call(s32[3]{0:T(128)S(1)} %pad_add_fusion.where_ref, bf16[16,144,128]{2,1,0:T(8,128)(2,1)S(1)} %all_to_all.15.q_ref, bf16[8,256,128]{2,1,0:T(8,128)(2,1)S(1)} %all_to_all.16.kv_ref), custom_call_target="tpu_custom_call" | custom-call | flops 1000000000 | bytes 1000000 | tf_op jit(solution)/shard_map/pallas_call | solution.py:235
  50.1 0.0 collective-permute-done.kv_ref
  50.1 0.0 copy-start.2
  50.1 2.0 %shard_map.66 = bf16[8,240,128]{2,1,0:T(8,128)(2,1)S(1)} custom-call(bf16[1280,128]{1,0:T(8,128)(2,1)S(1)} %get-tuple-element.8.q_ref, bf16[8,256,128]{2,1,0:T(8,128)(2,1)S(1)} %collective-permute-done.kv_ref, f32[1280,256]{1,0:T(8,128)S(1)} %get-tuple-element.9.sum_ref, f32[1280,128]{1,0:T(8,128)S(1)} %get-tuple-element.10.top_ref), custom_call_target="tpu_custom_call" | custom-call | flops 1000000000 | bytes 1000000 | tf_op jit(solution)/shard_map/pallas_call | solution.py:236
  52.2 11.7 %all_to_all.17.a_ref = bf16[8,240,128]{2,1,0:T(8,128)(2,1)S(1)} all-to-all(bf16[8,240,128]{2,1,0:T(8,128)(2,1)S(1)} %shard_map.66), channel_id=1, replica_groups=mesh['z'=8,'core'=2,'gy'=8,'seq'=2] {'gy'}, dimensions={0} | all-to-all | bytes 983040 | tf_op jit(solution)/shard_map/all_to_all | solution.py:237
  63.8 0.0 copy-done.2
  63.8 0.0 copy-start.1
  63.9 1.0 %shard_map.67.own_ref = bf16[2,192,256]{2,1,0:T(8,128)(2,1)S(1)} custom-call(s32[3]{0:T(128)S(1)} %pad_add_fusion.where_ref, bf16[8,240,128]{2,1,0:T(8,128)(2,1)S(1)} %all_to_all.17.a_ref, bf16[1024,256]{1,0:T(8,128)(2,1)S(1)} %copy-done.2), custom_call_target="tpu_custom_call" | custom-call | flops 1000000000 | bytes 1000000 | tf_op jit(solution)/shard_map/pallas_call | solution.py:238
  64.8 1.2 %collective-permute-start.1 = (bf16[2,192,256]{2,1,0:T(8,128)(2,1)S(1)}, bf16[2,192,256]{2,1,0:T(8,128)(2,1)S(1)}, u32[]{:S(2)}, u32[]{:S(2)}) collective-permute-start(bf16[2,192,256]{2,1,0:T(8,128)(2,1)S(1)} %shard_map.67.own_ref), channel_id=1, source_target_pairs={{0,16},{16,0},{1,17},{17,1},{2,18},{18,2},{3,19},{19,3},{4,20},{20... | collective-permute-start | bytes 589832 | tf_op jit(solution)/shard_map/ppermute | solution.py:240
  66.0 0.3 collective-permute-start.2
  66.3 0.0 copy-done.1
  66.3 0.0 copy-start
  66.3 0.5 shard_map.69.w2_ref
  66.8 0.9 %copy-done = bf16[3,3,3,256,128]{4,3,2,1,0:T(8,128)(2,1)S(1)} copy-done((bf16[3,3,3,256,128]{4,3,2,1,0:T(8,128)(2,1)S(1)}, bf16[3,3,3,256,128]{4,3,2,1,0:T(8,128)(2,1)}, u32[]{:S(2)}) %copy-start) | copy-done | bytes 1769496
  67.8 0.9 %shard_map.68.own_ref = f32[4,160,384]{2,1,0:T(8,128)S(1)} custom-call(bf16[2,192,256]{2,1,0:T(8,128)(2,1)S(1)} %shard_map.67.own_ref, bf16[27,256,128]{2,1,0:T(8,128)(2,1)S(1)} %bitcast.11), custom_call_target="tpu_custom_call" | custom-call | flops 1000000000 | bytes 1000000 | tf_op jit(solution)/shard_map/pallas_call | solution.py:242
  68.7 0.0 collective-permute-done.1.near_ref
  68.7 2.7 %collective-permute-done.2.far_ref = bf16[2,192,256]{2,1,0:T(8,128)(2,1)S(1)} collective-permute-done((bf16[2,192,256]{2,1,0:T(8,128)(2,1)S(1)}, bf16[2,192,256]{2,1,0:T(8,128)(2,1)S(1)}, u32[]{:S(2)}, u32[]{:S(2)}) %collective-permute-start.2) | collective-permute-done | bytes 196640 | tf_op jit(solution)/shard_map/ppermute | solution.py:239
  71.4 2.8 %shard_map.70 = bf16[4,16,16,128]{3,2,1,0:T(8,128)(2,1)} custom-call(s32[3]{0:T(128)S(1)} %pad_add_fusion.where_ref, f32[4,160,384]{2,1,0:T(8,128)S(1)} %shard_map.68.own_ref, bf16[2,192,256]{2,1,0:T(8,128)(2,1)S(1)} %collective-permute-done.1.near_ref, bf16[2,192,256]{2,1,0:T(8,128)(2,1)S(1)} %collective-permute-done.2.far_ref, ...), custom_call_target="tpu_custom_call" | custom-call | flops 1000000000 | bytes 1000000 | tf_op jit(solution)/shard_map/pallas_call | solution.py:245
  (2 shorter events, 0.0 us)
Async XLA Ops:
  43.5 6.6 %collective-permute-start = (bf16[8,256,128]{2,1,0:T(8,128)(2,1)S(1)}, bf16[8,256,128]{2,1,0:T(8,128)(2,1)S(1)}, u32[]{:S(2)}, u32[]{:S(2)}) collective-permute-start(bf16[8,256,128]{2,1,0:T(8,128)(2,1)S(1)} %all_to_all.16.kv_ref), channel_id=1, source_target_pairs={{0,16},{16,0},{1,17},{17,1},{2,18},{18,2},{3,19},{19,3},{4,20},{20... | collective-permute-start | bytes 1572872 | tf_op jit(solution)/shard_map/ppermute | solution.py:233
  50.1 13.7 %copy-start.2 = (bf16[1024,256]{1,0:T(8,128)(2,1)S(1)}, bf16[1024,256]{1,0:T(8,128)(2,1)}, u32[]{:S(2)}) copy-start(bf16[1024,256]{1,0:T(8,128)(2,1)} %w_ref.1) | copy-start | bytes 1572868
  63.8 2.5 %copy-start.1 = (bf16[3,3,3,128,128]{4,3,2,1,0:T(8,128)(2,1)S(1)}, bf16[3,3,3,128,128]{4,3,2,1,0:T(8,128)(2,1)}, u32[]{:S(2)}) copy-start(bf16[3,3,3,128,128]{4,3,2,1,0:T(8,128)(2,1)} %param.11) | copy-start | bytes 2654212
  64.8 3.9 %collective-permute-start.1 = (bf16[2,192,256]{2,1,0:T(8,128)(2,1)S(1)}, bf16[2,192,256]{2,1,0:T(8,128)(2,1)S(1)}, u32[]{:S(2)}, u32[]{:S(2)}) collective-permute-start(bf16[2,192,256]{2,1,0:T(8,128)(2,1)S(1)} %shard_map.67.own_ref), channel_id=1, source_target_pairs={{0,16},{16,0},{1,17},{17,1},{2,18},{18,2},{3,19},{19,3},{4,20},{20... | collective-permute-start | bytes 589832 | tf_op jit(solution)/shard_map/ppermute | solution.py:240
  66.0 5.4 %collective-permute-start.2 = (bf16[2,192,256]{2,1,0:T(8,128)(2,1)S(1)}, bf16[2,192,256]{2,1,0:T(8,128)(2,1)S(1)}, u32[]{:S(2)}, u32[]{:S(2)}) collective-permute-start(bf16[2,192,256]{2,1,0:T(8,128)(2,1)S(1)} %shard_map.67.own_ref), channel_id=1, source_target_pairs={{0,240},{16,32},{32,16},{48,64},{64,48},{80,96},{96,80},{112,128},... | collective-permute-start | bytes 589832 | tf_op jit(solution)/shard_map/ppermute | solution.py:239
  66.3 1.5 %copy-start = (bf16[3,3,3,256,128]{4,3,2,1,0:T(8,128)(2,1)S(1)}, bf16[3,3,3,256,128]{4,3,2,1,0:T(8,128)(2,1)}, u32[]{:S(2)}) copy-start(bf16[3,3,3,256,128]{4,3,2,1,0:T(8,128)(2,1)} %param.10) | copy-start | bytes 5308420

commit v4 on v3

--- a/solution.py
+++ b/solution.py
@@ -15,16 +15,16 @@
 SCALE = HD**-0.5 * 1.4426950408889634
 
 
-def call(kernel, shapes, dtypes, in_specs, scratch=(), room=48):
+def call(kernel, shapes, dtypes, in_specs, scratch=(), out_spec=VM):
     outs = [jax.ShapeDtypeStruct(shape, dtype) for shape, dtype in zip(shapes, dtypes)]
     one = len(outs) == 1
     return pl.pallas_call(
         kernel,
         out_shape=outs[0] if one else outs,
         in_specs=in_specs,
-        out_specs=VM if one else [VM] * len(outs),
+        out_specs=out_spec if one else [VM] * len(outs),
         scratch_shapes=list(scratch),
-        compiler_params=pltpu.CompilerParams(vmem_limit_bytes=room * 1024 * 1024),
+        compiler_params=pltpu.CompilerParams(vmem_limit_bytes=24 * 1024 * 1024),
         cost_estimate=pl.CostEstimate(flops=10**9, bytes_accessed=1000000, transcendentals=0),
     )
 
@@ -41,10 +41,9 @@
     for h in range(H):
         cols = slice(h * HD, (h + 1) * HD)
         pair = jnp.concatenate([k_ref[:, cols].astype(F32), v_ref[:, cols].astype(F32)], axis=0).astype(BF)
-        rows = [q_ref[x, :, cols].astype(F32).reshape(8, 8, HD) for x in range(2)]
-        rows = jnp.concatenate(rows, axis=1).reshape(128, HD).astype(BF)
         for s in range(2):
-            out_ref[2 * h + s, 0:128] = rows
+            out_ref[2 * h + s, 0:64] = q_ref[0, :, cols]
+            out_ref[2 * h + s, 64:128] = q_ref[1, :, cols]
             out_ref[2 * h + s, 128:144] = pair
 
 
@@ -63,7 +62,7 @@
     keys, vals = halves(kv_ref)
     row = lax.broadcasted_iota(jnp.int32, (32, 128), 0)
     col = lax.broadcasted_iota(jnp.int32, (32, 128), 1)
-    pick = (col == (row // 2) * 8 + row % 2 + 6 * seq).astype(F32).astype(BF)
+    pick = (col == (row // 2) % 2 * 64 + (row // 4) * 8 + row % 2 + 6 * seq).astype(F32).astype(BF)
     near = [jnp.dot(pick, q_ref[2 * g + 1 - seq, 0:128], preferred_element_type=F32).astype(BF) for g in range(8)]
     for n in range(10):
         rows = slice(128 * n, 128 * n + 128)
@@ -93,7 +92,8 @@
         if n >= 8:
             near.append(done)
             continue
-        done = done.astype(BF)
+        done = done.reshape(2, 8, 8, HD)
+        done = jnp.concatenate([done[0], done[1]], axis=1).reshape(128, HD).astype(BF)
         out_ref[n, 32:160] = done
         if n < 7:
             out_ref[n + 1, 0:32] = done[96:128]
@@ -105,15 +105,18 @@
         out_ref[g, 192:240] = near[32 * g : 32 * g + 48].astype(BF)
 
 
-def project_kernel(where_ref, a_ref, w_ref, out_ref):
-    seq = where_ref[2]
+def project_kernel(a_ref, w_ref, out_ref):
     rows = jnp.concatenate([a_ref[h] for h in range(H)], axis=1)
     projected = jnp.dot(rows, w_ref[...], preferred_element_type=F32)
     scale = lax.rsqrt(jnp.mean(projected * projected, axis=1, keepdims=True) + 1e-06)
-    normed = projected * scale
-    half = normed[0:192].reshape(12, 2, 8, 256)
-    near = normed[192:240].reshape(6, 8, 256)
+    out_ref[...] = (projected * scale).astype(BF)
+
+
+def laid_out(normed, seq):
+    half = normed[0:192].astype(F32).reshape(12, 2, 8, 256)
+    near = normed[192:240].astype(F32).reshape(6, 8, 256)
     row = lax.broadcasted_iota(jnp.int32, (12, 8, 256), 1)
+    slabs = []
     for x in range(2):
         middle = pltpu.roll(half[:, x], 2, 1)
         ends = [pltpu.roll(near, (8 - 4 * odd - 2 * x) % 8, 1) if odd + x else near for odd in range(2)]
@@ -121,7 +124,8 @@
         upper = jnp.where(row < 2, jnp.where(seq == 1, ends, 0.0), middle)
         lower = jnp.where((row < 4) & (seq == 0), pltpu.roll(ends, 2, 1), 0.0)
         lower = jnp.where(row < 2, middle, lower)
-        out_ref[x] = jnp.concatenate([upper, lower], axis=1).reshape(192, 256).astype(BF)
+        slabs.append(jnp.concatenate([upper, lower], axis=1).reshape(192, 256).astype(BF))
+    return slabs
 
 
 def merge_kernel(w_ref, out_ref):
@@ -150,56 +154,64 @@
     return jnp.concatenate([w1_ref[t], w1_ref[t + 1], w1_ref[t + 2]], axis=1)
 
 
-def own_conv_kernel(own_ref, w1_ref, out_ref):
+def own_conv_kernel(where_ref, own_ref, w1_ref, out_ref):
+    slabs = laid_out(own_ref[...], where_ref[2])
     for x in range(4):
         total = jnp.zeros((160, 384), F32)
         for a in range(3):
             if 2 <= x + a < 4:
                 for b in range(3):
-                    part = own_ref[x + a - 2, 16 * b : 16 * b + 160]
+                    part = slabs[x + a - 2][16 * b : 16 * b + 160]
                     total = total + jnp.dot(part, taps(w1_ref, a, b), preferred_element_type=F32)
         out_ref[x] = total
 
 
-def conv_kernel(where_ref, own_ref, near_ref, far_ref, w1_ref, w2_ref, out_ref, field):
+def side(where_ref, at_left, slabs, own_ref, w1_ref):
     gx, gy, seq = where_ref[0], where_ref[1], where_ref[2]
-    first_core = gx % 2 == 0
-    none = jnp.zeros((192, 256), BF)
-    left = [jnp.where(gx == 0, none, jnp.where(first_core, far_ref[x], near_ref[x])) for x in range(2)]
-    right = [jnp.where(gx == 15, none, jnp.where(first_core, near_ref[x], far_ref[x])) for x in range(2)]
-    slabs = left + [None, None] + right
     row = lax.broadcasted_iota(jnp.int32, (160, 128), 0)
     at_z = seq * 8 - 1 + row % 16
     at_y = gy * 8 - 1 + row // 16
     inside = (at_y >= 0) & (at_y < 64) & (at_z >= 0) & (at_z < 16)
-    hidden = []
-    for x in range(4):
+    first_tap = jnp.where(at_left, 0, 1)
+    outer = [(slabs[0], first_tap), (slabs[1], first_tap + 1)]
+    inner = [(jnp.where(at_left, slabs[1], slabs[0]), jnp.where(at_left, 0, 2))]
+    results = []
+    for x, terms in ((jnp.where(at_left, 0, 3), outer), (jnp.where(at_left, 1, 2), inner)):
         total = own_ref[x]
-        for a in range(3):
-            if slabs[x + a] is not None:
-                for b in range(3):
-                    part = slabs[x + a][16 * b : 16 * b + 160]
-                    total = total + jnp.dot(part, taps(w1_ref, a, b), preferred_element_type=F32)
+        for slab, a in terms:
+            for b in range(3):
+                total = total + jnp.dot(slab[16 * b : 16 * b + 160], taps(w1_ref, a, b), preferred_element_type=F32)
         first = total[:, 0:128] + shifted(total[:, 128:256], -1) + shifted(total[:, 256:384], -2)
         value = first / (1.0 + jnp.exp(-first))
         at_x = gx * 2 - 1 + x
-        hidden.append(jnp.where(inside & (at_x >= 0) & (at_x < 32), value, 0.0).astype(BF))
+        results.append((x, jnp.where(inside & (at_x >= 0) & (at_x < 32), value, 0.0).astype(BF)))
+    return results
+
+
+def near_conv_kernel(where_ref, near_ref, own_ref, w1_ref, out_ref):
+    at_left = where_ref[0] % 2 == 1
+    slabs = laid_out(near_ref[...], where_ref[2])
+    for n, (_, rows) in enumerate(side(where_ref, at_left, slabs, own_ref, w1_ref)):
+        out_ref[n] = rows
+
+
+def conv_kernel(where_ref, own_ref, done_ref, far_ref, w1_ref, w2_ref, out_hbm, hidden, field, ready, sems):
+    gx = where_ref[0]
+    at_left = gx % 2 == 0
+    there = jnp.where(at_left, gx > 0, gx < 15)
+    slabs = [jnp.where(there, slab, jnp.zeros_like(slab)) for slab in laid_out(far_ref[...], where_ref[2])]
+    hidden[jnp.where(at_left, 3, 0)] = done_ref[0]
+    hidden[jnp.where(at_left, 2, 1)] = done_ref[1]
+    for x, rows in side(where_ref, at_left, slabs, own_ref, w1_ref):
+        hidden[x] = rows
+    copies = []
     for px in range(2):
         for py in range(2):
-            rows = jnp.concatenate(
-                [
-                    jnp.concatenate(
-                        [
-                            hidden[i + px + a][16 * (py + b) : 16 * (py + b) + 128]
-                            for a in range(2)
-                            for b in range(2)
-                        ],
-                        axis=1,
-                    )
-                    for i in range(2)
-                ],
-                axis=0,
-            )
+            rows = [
+                [hidden[i + px + a, 16 * (py + b) : 16 * (py + b) + 128] for a in range(2) for b in range(2)]
+                for i in range(2)
+            ]
+            rows = jnp.concatenate([jnp.concatenate(parts, axis=1) for parts in rows], axis=0)
             parts = jnp.dot(rows, w2_ref[2 * px + py], preferred_element_type=F32)
             even = parts[:, 0:128] + shifted(parts[:, 128:256], -1)
             odd = shifted(parts[:, 256:384], -1) + shifted(parts[:, 384:512], -2)
@@ -208,7 +220,12 @@
                 for i in range(2):
                     for j in range(8):
                         field[2 * i + px, 2 * j + py, pl.ds(pz, 8, stride=2), :] = part[i, j, 0:8]
-    out_ref[...] = field[...].astype(BF)
+        for x in (px, px + 2):
+            ready[x] = field[x].astype(BF)
+            copies.append(pltpu.make_async_copy(ready.at[x], out_hbm.at[x], sems.at[x]))
+            copies[-1].start()
+    for copy in copies:
+        copy.wait()
 
 
 def body(queries, keys, values, w_out, conv_first, conv_second):
@@ -225,8 +242,7 @@
             pltpu.VMEM((8, H * HD), BF),
             pltpu.SemaphoreType.DMA((3,)),
         ],
-        room=62,
-    )(queries.reshape(2, 64, H * HD), keys, values)
+    )(*(pltpu.with_memory_space_constraint(a, pltpu.HBM) for a in (queries.reshape(2, 64, H * HD), keys, values)))
     got = lax.all_to_all(sent, ("gy", "seq"), 0, 0, tiled=True)
     pair = got[:, 128:144].reshape(16, 2, 8, HD).transpose(1, 0, 2, 3).reshape(1, 256, HD)
     own = lax.all_to_all(jnp.broadcast_to(pair, (8, 256, HD)), "z", 0, 0, tiled=True)
@@ -235,14 +251,21 @@
     q, summed, top = half(place, got, own)
     attended = call(second_half_kernel, [(8, 240, HD)], [BF], [VM] * 4)(q, other, summed, top)
     back = lax.all_to_all(attended, "gy", 0, 0, tiled=True)
-    normed = call(project_kernel, [(2, 192, 256)], [BF], [SM, VM, VM])(place, back, w_out)
+    normed = call(project_kernel, [(240, 256)], [BF], [VM, VM])(back, w_out)
     far = lax.ppermute(normed, ("z", "core"), [(i, (i - 1 + 2 * (i % 2)) % 16) for i in range(16)])
     near = lax.ppermute(normed, "core", [(0, 1), (1, 0)])
     w1 = conv_first.reshape(27, 256, 128)
-    own_part = call(own_conv_kernel, [(4, 160, 384)], [F32], [VM, VM])(normed, w1)
     merged = call(merge_kernel, [(4, 512, 512)], [BF], [VM])(conv_second.reshape(27, 128, 128))
-    final = call(conv_kernel, [(4, 16, 16, 128)], [BF], [SM] + [VM] * 5, [pltpu.VMEM((4, 16, 16, 128), F32)])
-    return final(place, own_part, near, far, w1, merged)
+    own_part = call(own_conv_kernel, [(4, 160, 384)], [F32], [SM, VM, VM])(place, normed, w1)
+    done = call(near_conv_kernel, [(2, 160, 128)], [BF], [SM] + [VM] * 3)(place, near, own_part, w1)
+    scratch = [
+        pltpu.VMEM((4, 160, 128), BF),
+        pltpu.VMEM((4, 16, 16, 128), F32),
+        pltpu.VMEM((4, 16, 16, 128), BF),
+        pltpu.SemaphoreType.DMA((4,)),
+    ]
+    final = call(conv_kernel, [(4, 16, 16, 128)], [BF], [SM] + [VM] * 5, scratch, HB)
+    return final(place, own_part, done, far, w1, merged)
 
 
 def solution(mesh):

time: 74.6 us -> 72.4 us (0.971)
  waiting for transfers between devices: 2.7 us -> 1.13 us
  local copies, waits for them, and re-layouts: 1.03 us -> 0.09 us
    ppermute x1, waiting for transfers between devices: 2.7 us -> 1.13 us  [body(): lax.ppermute(normed, ('z', 'core'), [(i, (i - 1 + 2 * (i % 2)) % 16) for...]
    unnamed x6, local copies, waits for them, and re-layouts: 0.95 us -> 0.01 us
    pallas_call x1, Pallas kernels: 1.87 us -> 1.05 us  [body(): call(pack_kernel, [(16, 144, HD)], [BF], [HB] * 3, [pltpu.VMEM((2, 64, H...]
    pallas_call x3 -> x4, Pallas kernels: 4.73 us -> 5.51 us  [the longest x1 2.54 us: body(): return final(place, own_part, done, far, w1, merged)]
  transfers between devices with their start and end apart: 3 -> 3, of which waited for: 1 -> 1; matrix products, arithmetic and copies ran while one was open for 0% -> 0% of each run, Pallas kernels for 5% -> 8%
where the time goes in v4:
time: 72.4 us; the launch traced here: 72.1 us
  blocking collectives  52.9 us (73%)
  Pallas kernels  11.6 us (16%)
  starting transfers between devices  6.15 us (8%)
  waiting for transfers between devices  1.13 us (2%)
    all_to_all x1, blocking collectives, body(): lax.all_to_all(jnp.broadcast_to(pair, (8, 256, HD)), 'z', 0, 0, tiled=True)  22.4 us
    all_to_all x1, blocking collectives, body(): got = lax.all_to_all(sent, ('gy', 'seq'), 0, 0, tiled=True)  18.8 us
    all_to_all x1, blocking collectives, body(): back = lax.all_to_all(attended, 'gy', 0, 0, tiled=True)  11.7 us
    ppermute x1, starting transfers between devices, body(): other = lax.ppermute(own, 'core', [(0, 1), (1, 0)])  4 us
    pallas_call x1, Pallas kernels, body(): return final(place, own_part, done, far, w1, merged)  2.54 us
    pallas_call x1, Pallas kernels, body(): q, summed, top = half(place, got, own)  2.52 us
    pallas_call x1, Pallas kernels, body(): call(second_half_kernel, [(8, 240, HD)], [BF], [VM] * 4)  2.04 us
    pallas_call x1, Pallas kernels, body(): call(own_conv_kernel, [(4, 160, 384)], [F32], [SM, VM, VM])  1.46 us
  transfers between devices with their start and end apart: 3, of which 1 were waited for; matrix products, arithmetic and copies ran while one was open for 0% of the time, Pallas kernels for 8%

profile of v4, /device:TPU:1, one launch (start us, length us, event | category | flops | bytes accessed | tf_op | source)
XLA Modules:
  0.0 72.1 jit_solution(4581021585615522731)
XLA Ops:
  0.0 1.1 %shard_map.64 = bf16[16,144,128]{2,1,0:T(8,128)(2,1)S(1)} custom-call(bf16[2,64,1024]{2,1,0:T(8,128)(2,1)} %bitcast.16, bf16[8,1024]{1,0:T(8,128)(2,1)} %k_hbm.1, bf16[8,1024]{1,0:T(8,128)(2,1)} %v_hbm.1), custom_call_target="tpu_custom_call" | custom-call | flops 1000000000 | bytes 1000000 | tf_op jit(solution)/shard_map/pallas_call | solution.py:234
  1.1 18.8 %all_to_all.15.q_ref = bf16[16,144,128]{2,1,0:T(8,128)(2,1)S(1)} all-to-all(bf16[16,144,128]{2,1,0:T(8,128)(2,1)S(1)} %shard_map.64), channel_id=1, replica_groups=mesh['z'=8,'core'=2,'gy'=8,'seq'=2] {'gy','seq'}, dimensions={0} | all-to-all | bytes 1179648 | tf_op jit(solution)/shard_map/all_to_all | solution.py:246
  19.9 0.1 broadcast_in_dim.8
  20.0 22.4 %all_to_all.16.kv_ref = bf16[8,256,128]{2,1,0:T(8,128)(2,1)S(1)} all-to-all(bf16[8,256,128]{2,1,0:T(8,128)(2,1)S(1)} %broadcast_in_dim.8), channel_id=1, replica_groups=mesh['z'=8,'core'=2,'gy'=8,'seq'=2] {'z'}, dimensions={0} | all-to-all | bytes 1048576 | tf_op jit(solution)/shard_map/all_to_all | solution.py:248
  42.4 4.0 %collective-permute-start = (bf16[8,256,128]{2,1,0:T(8,128)(2,1)S(1)}, bf16[8,256,128]{2,1,0:T(8,128)(2,1)S(1)}, u32[]{:S(2)}, u32[]{:S(2)}) collective-permute-start(bf16[8,256,128]{2,1,0:T(8,128)(2,1)S(1)} %all_to_all.16.kv_ref), channel_id=1, source_target_pairs={{0,16},{16,0},{1,17},{17,1},{2,18},{18,2},{3,19},{19,3},{4,20},{20... | collective-permute-start | bytes 1572872 | tf_op jit(solution)/shard_map/ppermute | solution.py:249
  46.4 0.1 pad_add_fusion.where_ref
  46.5 2.5 %shard_map.65 = (bf16[1280,128]{1,0:T(8,128)(2,1)S(1)}, f32[1280,256]{1,0:T(8,128)S(1)}, f32[1280,128]{1,0:T(8,128)S(1)}) custom-call(s32[3]{0:T(128)S(1)} %pad_add_fusion.where_ref, bf16[16,144,128]{2,1,0:T(8,128)(2,1)S(1)} %all_to_all.15.q_ref, bf16[8,256,128]{2,1,0:T(8,128)(2,1)S(1)} %all_to_all.16.kv_ref), custom_call_target="tpu_custom_call" | custom-call | flops 1000000000 | bytes 1000000 | tf_op jit(solution)/shard_map/pallas_call | solution.py:251
  49.0 0.0 collective-permute-done.kv_ref
  49.1 0.0 copy-start.2
  49.1 2.0 %shard_map.66 = bf16[8,240,128]{2,1,0:T(8,128)(2,1)S(1)} custom-call(bf16[1280,128]{1,0:T(8,128)(2,1)S(1)} %get-tuple-element.8.q_ref, bf16[8,256,128]{2,1,0:T(8,128)(2,1)S(1)} %collective-permute-done.kv_ref, f32[1280,256]{1,0:T(8,128)S(1)} %get-tuple-element.9.sum_ref, f32[1280,128]{1,0:T(8,128)S(1)} %get-tuple-element.10.top_ref), custom_call_target="tpu_custom_call" | custom-call | flops 1000000000 | bytes 1000000 | tf_op jit(solution)/shard_map/pallas_call | solution.py:252
  51.1 11.7 %all_to_all.17.a_ref = bf16[8,240,128]{2,1,0:T(8,128)(2,1)S(1)} all-to-all(bf16[8,240,128]{2,1,0:T(8,128)(2,1)S(1)} %shard_map.66), channel_id=1, replica_groups=mesh['z'=8,'core'=2,'gy'=8,'seq'=2] {'gy'}, dimensions={0} | all-to-all | bytes 983040 | tf_op jit(solution)/shard_map/all_to_all | solution.py:253
  62.8 0.0 copy-done.2
  62.8 0.0 copy-start.1
  62.8 0.4 shard_map.67.own_ref
  63.2 1.2 %collective-permute-start.1 = (bf16[240,256]{1,0:T(8,128)(2,1)S(1)}, bf16[240,256]{1,0:T(8,128)(2,1)S(1)}, u32[]{:S(2)}, u32[]{:S(2)}) collective-permute-start(bf16[240,256]{1,0:T(8,128)(2,1)S(1)} %shard_map.67.own_ref), channel_id=1, source_target_pairs={{0,16},{16,0},{1,17},{17,1},{2,18},{18,2},{3,19},{19,3},{4,20},{20... | collective-permute-start | bytes 368648 | tf_op jit(solution)/shard_map/ppermute | solution.py:256
  64.4 0.0 copy-done.1
  64.4 0.0 copy-start
  64.4 0.5 shard_map.70.w2_ref
  64.9 0.9 %collective-permute-start.2 = (bf16[240,256]{1,0:T(8,128)(2,1)S(1)}, bf16[240,256]{1,0:T(8,128)(2,1)S(1)}, u32[]{:S(2)}, u32[]{:S(2)}) collective-permute-start(bf16[240,256]{1,0:T(8,128)(2,1)S(1)} %shard_map.67.own_ref), channel_id=1, source_target_pairs={{0,240},{16,32},{32,16},{48,64},{64,48},{80,96},{96,80},{112,128},... | collective-permute-start | bytes 368648 | tf_op jit(solution)/shard_map/ppermute | solution.py:255
  65.9 0.0 copy-done
  65.9 1.5 %shard_map.68.own_ref = f32[4,160,384]{2,1,0:T(8,128)S(1)} custom-call(s32[3]{0:T(128)S(1)} %pad_add_fusion.where_ref, bf16[240,256]{1,0:T(8,128)(2,1)S(1)} %shard_map.67.own_ref, bf16[27,256,128]{2,1,0:T(8,128)(2,1)S(1)} %bitcast.11), custom_call_target="tpu_custom_call" | custom-call | flops 1000000000 | bytes 1000000 | tf_op jit(solution)/shard_map/pallas_call | solution.py:259
  67.3 0.0 collective-permute-done.1.near_ref
  67.3 1.1 %shard_map.69.done_ref = bf16[2,160,128]{2,1,0:T(8,128)(2,1)S(1)} custom-call(s32[3]{0:T(128)S(1)} %pad_add_fusion.where_ref, bf16[240,256]{1,0:T(8,128)(2,1)S(1)} %collective-permute-done.1.near_ref, f32[4,160,384]{2,1,0:T(8,128)S(1)} %shard_map.68.own_ref, bf16[27,256,128]{2,1,0:T(8,128)(2,1)S(1)} %bitcast.12), custom_call_target="tpu_custom_call" | custom-call | flops 1000000000 | bytes 1000000 | tf_op jit(solution)/shard_map/pallas_call | solution.py:260
  68.5 1.1 %collective-permute-done.2.far_ref = bf16[240,256]{1,0:T(8,128)(2,1)S(1)} collective-permute-done((bf16[240,256]{1,0:T(8,128)(2,1)S(1)}, bf16[240,256]{1,0:T(8,128)(2,1)S(1)}, u32[]{:S(2)}, u32[]{:S(2)}) %collective-permute-start.2) | collective-permute-done | bytes 122912 | tf_op jit(solution)/shard_map/ppermute | solution.py:255
  69.6 2.5 %shard_map.71 = bf16[4,16,16,128]{3,2,1,0:T(8,128)(2,1)} custom-call(s32[3]{0:T(128)S(1)} %pad_add_fusion.where_ref, f32[4,160,384]{2,1,0:T(8,128)S(1)} %shard_map.68.own_ref, bf16[2,160,128]{2,1,0:T(8,128)(2,1)S(1)} %shard_map.69.done_ref, bf16[240,256]{1,0:T(8,128)(2,1)S(1)} %collective-permute-done.2.far_ref, bf16[27,256,128]{2,1,0:T(8,128)(2,1)S(1)} %bitcast.13, ...), custom_call_target="tpu_custom_call" | custom-call | flops 1000000000 | bytes 1000000 | tf_op jit(solution)/shard_map/pallas_call | solution.py:268
  (2 shorter events, 0.0 us)
Async XLA Ops:
  42.4 6.6 %collective-permute-start = (bf16[8,256,128]{2,1,0:T(8,128)(2,1)S(1)}, bf16[8,256,128]{2,1,0:T(8,128)(2,1)S(1)}, u32[]{:S(2)}, u32[]{:S(2)}) collective-permute-start(bf16[8,256,128]{2,1,0:T(8,128)(2,1)S(1)} %all_to_all.16.kv_ref), channel_id=1, source_target_pairs={{0,16},{16,0},{1,17},{17,1},{2,18},{18,2},{3,19},{19,3},{4,20},{20... | collective-permute-start | bytes 1572872 | tf_op jit(solution)/shard_map/ppermute | solution.py:249
  49.1 13.7 %copy-start.2 = (bf16[1024,256]{1,0:T(8,128)(2,1)S(1)}, bf16[1024,256]{1,0:T(8,128)(2,1)}, u32[]{:S(2)}) copy-start(bf16[1024,256]{1,0:T(8,128)(2,1)} %w_ref.1) | copy-start | bytes 1572868
  62.8 1.6 %copy-start.1 = (bf16[3,3,3,128,128]{4,3,2,1,0:T(8,128)(2,1)S(1)}, bf16[3,3,3,128,128]{4,3,2,1,0:T(8,128)(2,1)}, u32[]{:S(2)}) copy-start(bf16[3,3,3,128,128]{4,3,2,1,0:T(8,128)(2,1)} %param.11) | copy-start | bytes 2654212
  63.2 4.2 %collective-permute-start.1 = (bf16[240,256]{1,0:T(8,128)(2,1)S(1)}, bf16[240,256]{1,0:T(8,128)(2,1)S(1)}, u32[]{:S(2)}, u32[]{:S(2)}) collective-permute-start(bf16[240,256]{1,0:T(8,128)(2,1)S(1)} %shard_map.67.own_ref), channel_id=1, source_target_pairs={{0,16},{16,0},{1,17},{17,1},{2,18},{18,2},{3,19},{19,3},{4,20},{20... | collective-permute-start | bytes 368648 | tf_op jit(solution)/shard_map/ppermute | solution.py:256
  64.4 1.5 %copy-start = (bf16[3,3,3,256,128]{4,3,2,1,0:T(8,128)(2,1)S(1)}, bf16[3,3,3,256,128]{4,3,2,1,0:T(8,128)(2,1)}, u32[]{:S(2)}) copy-start(bf16[3,3,3,256,128]{4,3,2,1,0:T(8,128)(2,1)} %param.10) | copy-start | bytes 5308420
  64.9 4.7 %collective-permute-start.2 = (bf16[240,256]{1,0:T(8,128)(2,1)S(1)}, bf16[240,256]{1,0:T(8,128)(2,1)S(1)}, u32[]{:S(2)}, u32[]{:S(2)}) collective-permute-start(bf16[240,256]{1,0:T(8,128)(2,1)S(1)} %shard_map.67.own_ref), channel_id=1, source_target_pairs={{0,240},{16,32},{32,16},{48,64},{64,48},{80,96},{96,80},{112,128},... | collective-permute-start | bytes 368648 | tf_op jit(solution)/shard_map/ppermute | solution.py:255

commit v5 on v4

--- a/solution.py
+++ b/solution.py
@@ -10,7 +10,6 @@
 BF = jnp.bfloat16
 F32 = jnp.float32
 VM = pl.BlockSpec(memory_space=pltpu.VMEM)
-SM = pl.BlockSpec(memory_space=pltpu.SMEM)
 HB = pl.BlockSpec(memory_space=pltpu.HBM)
 SCALE = HD**-0.5 * 1.4426950408889634
 
@@ -25,7 +24,7 @@
         out_specs=out_spec if one else [VM] * len(outs),
         scratch_shapes=list(scratch),
         compiler_params=pltpu.CompilerParams(vmem_limit_bytes=24 * 1024 * 1024),
-        cost_estimate=pl.CostEstimate(flops=10**9, bytes_accessed=1000000, transcendentals=0),
+        cost_estimate=pl.CostEstimate(flops=10**6, bytes_accessed=10000, transcendentals=0),
     )
 
 
@@ -57,8 +56,8 @@
     return scores, jnp.max(scores, axis=1, keepdims=True)
 
 
-def first_half_kernel(where_ref, q_ref, kv_ref, q_out, sum_out, top_out):
-    seq = where_ref[2]
+def first_half_kernel(q_ref, kv_ref, q_out, sum_out, top_out):
+    seq = lax.axis_index("seq")
     keys, vals = halves(kv_ref)
     row = lax.broadcasted_iota(jnp.int32, (32, 128), 0)
     col = lax.broadcasted_iota(jnp.int32, (32, 128), 1)
@@ -112,7 +111,8 @@
     out_ref[...] = (projected * scale).astype(BF)
 
 
-def laid_out(normed, seq):
+def laid_out(normed):
+    seq = lax.axis_index("seq")
     half = normed[0:192].astype(F32).reshape(12, 2, 8, 256)
     near = normed[192:240].astype(F32).reshape(6, 8, 256)
     row = lax.broadcasted_iota(jnp.int32, (12, 8, 256), 1)
@@ -149,13 +149,17 @@
     return pltpu.roll(x, by % x.shape[0], 0)
 
 
+def x_tile():
+    return 2 * lax.axis_index("z") + lax.axis_index("core")
+
+
 def taps(w1_ref, a, b):
     t = 9 * a + 3 * b
     return jnp.concatenate([w1_ref[t], w1_ref[t + 1], w1_ref[t + 2]], axis=1)
 
 
-def own_conv_kernel(where_ref, own_ref, w1_ref, out_ref):
-    slabs = laid_out(own_ref[...], where_ref[2])
+def own_conv_kernel(own_ref, w1_ref, out_ref):
+    slabs = laid_out(own_ref[...])
     for x in range(4):
         total = jnp.zeros((160, 384), F32)
         for a in range(3):
@@ -166,8 +170,8 @@
         out_ref[x] = total
 
 
-def side(where_ref, at_left, slabs, own_ref, w1_ref):
-    gx, gy, seq = where_ref[0], where_ref[1], where_ref[2]
+def side(at_left, slabs, own_ref, w1_ref):
+    gx, gy, seq = x_tile(), lax.axis_index("gy"), lax.axis_index("seq")
     row = lax.broadcasted_iota(jnp.int32, (160, 128), 0)
     at_z = seq * 8 - 1 + row % 16
     at_y = gy * 8 - 1 + row // 16
@@ -188,21 +192,21 @@
     return results
 
 
-def near_conv_kernel(where_ref, near_ref, own_ref, w1_ref, out_ref):
-    at_left = where_ref[0] % 2 == 1
-    slabs = laid_out(near_ref[...], where_ref[2])
-    for n, (_, rows) in enumerate(side(where_ref, at_left, slabs, own_ref, w1_ref)):
+def near_conv_kernel(near_ref, own_ref, w1_ref, out_ref):
+    at_left = lax.axis_index("core") == 1
+    slabs = laid_out(near_ref[...])
+    for n, (_, rows) in enumerate(side(at_left, slabs, own_ref, w1_ref)):
         out_ref[n] = rows
 
 
-def conv_kernel(where_ref, own_ref, done_ref, far_ref, w1_ref, w2_ref, out_hbm, hidden, field, ready, sems):
-    gx = where_ref[0]
-    at_left = gx % 2 == 0
+def conv_kernel(own_ref, done_ref, far_ref, w1_ref, w2_ref, out_hbm, hidden, field, ready, sems):
+    gx = x_tile()
+    at_left = lax.axis_index("core") == 0
     there = jnp.where(at_left, gx > 0, gx < 15)
-    slabs = [jnp.where(there, slab, jnp.zeros_like(slab)) for slab in laid_out(far_ref[...], where_ref[2])]
+    slabs = [jnp.where(there, slab, jnp.zeros_like(slab)) for slab in laid_out(far_ref[...])]
     hidden[jnp.where(at_left, 3, 0)] = done_ref[0]
     hidden[jnp.where(at_left, 2, 1)] = done_ref[1]
-    for x, rows in side(where_ref, at_left, slabs, own_ref, w1_ref):
+    for x, rows in side(at_left, slabs, own_ref, w1_ref):
         hidden[x] = rows
     copies = []
     for px in range(2):
@@ -229,8 +233,6 @@
 
 
 def body(queries, keys, values, w_out, conv_first, conv_second):
-    z, core, gy, seq = (lax.axis_index(name) for name in ("z", "core", "gy", "seq"))
-    place = jnp.stack([2 * z + core, gy, seq]).astype(jnp.int32)
     sent = call(
         pack_kernel,
         [(16, 144, HD)],
@@ -247,8 +249,8 @@
     pair = got[:, 128:144].reshape(16, 2, 8, HD).transpose(1, 0, 2, 3).reshape(1, 256, HD)
     own = lax.all_to_all(jnp.broadcast_to(pair, (8, 256, HD)), "z", 0, 0, tiled=True)
     other = lax.ppermute(own, "core", [(0, 1), (1, 0)])
-    half = call(first_half_kernel, [(1280, HD), (1280, 2 * HD), (1280, HD)], [BF, F32, F32], [SM, VM, VM])
-    q, summed, top = half(place, got, own)
+    half = call(first_half_kernel, [(1280, HD), (1280, 2 * HD), (1280, HD)], [BF, F32, F32], [VM, VM])
+    q, summed, top = half(got, own)
     attended = call(second_half_kernel, [(8, 240, HD)], [BF], [VM] * 4)(q, other, summed, top)
     back = lax.all_to_all(attended, "gy", 0, 0, tiled=True)
     normed = call(project_kernel, [(240, 256)], [BF], [VM, VM])(back, w_out)
@@ -256,16 +258,16 @@
     near = lax.ppermute(normed, "core", [(0, 1), (1, 0)])
     w1 = conv_first.reshape(27, 256, 128)
     merged = call(merge_kernel, [(4, 512, 512)], [BF], [VM])(conv_second.reshape(27, 128, 128))
-    own_part = call(own_conv_kernel, [(4, 160, 384)], [F32], [SM, VM, VM])(place, normed, w1)
-    done = call(near_conv_kernel, [(2, 160, 128)], [BF], [SM] + [VM] * 3)(place, near, own_part, w1)
+    own_part = call(own_conv_kernel, [(4, 160, 384)], [F32], [VM, VM])(normed, w1)
+    done = call(near_conv_kernel, [(2, 160, 128)], [BF], [VM] * 3)(near, own_part, w1)
     scratch = [
         pltpu.VMEM((4, 160, 128), BF),
         pltpu.VMEM((4, 16, 16, 128), F32),
         pltpu.VMEM((4, 16, 16, 128), BF),
         pltpu.SemaphoreType.DMA((4,)),
     ]
-    final = call(conv_kernel, [(4, 16, 16, 128)], [BF], [SM] + [VM] * 5, scratch, HB)
-    return final(place, own_part, done, far, w1, merged)
+    final = call(conv_kernel, [(4, 16, 16, 128)], [BF], [VM] * 5, scratch, HB)
+    return final(own_part, done, far, w1, merged)
 
 
 def solution(mesh):

time: 72.4 us -> 70.7 us (0.977)
  Pallas kernels: 11.6 us -> 9.42 us
  waiting for transfers between devices: 1.13 us -> 2.26 us
    pallas_call x4, Pallas kernels: 7.65 us -> 5.48 us  [the longest x1 1.98 us: body(): return final(own_part, done, far, w1, merged)]
    ppermute x1, waiting for transfers between devices: 1.13 us -> 2.25 us  [body(): lax.ppermute(normed, ('z', 'core'), [(i, (i - 1 + 2 * (i % 2)) % 16) for...]
  transfers between devices with their start and end apart: 3 -> 3, of which waited for: 1 -> 1; matrix products, arithmetic and copies ran while one was open for 0% -> 0% of each run, Pallas kernels for 8% -> 6%
where the time goes in v5:
time: 70.7 us; the launch traced here: 70.4 us
  blocking collectives  53.1 us (75%)
  Pallas kernels  9.42 us (13%)
  starting transfers between devices  5.47 us (8%)
  waiting for transfers between devices  2.26 us (3%)
    all_to_all x1, blocking collectives, body(): lax.all_to_all(jnp.broadcast_to(pair, (8, 256, HD)), 'z', 0, 0, tiled=True)  22.4 us
    all_to_all x1, blocking collectives, body(): got = lax.all_to_all(sent, ('gy', 'seq'), 0, 0, tiled=True)  18.8 us
    all_to_all x1, blocking collectives, body(): back = lax.all_to_all(attended, 'gy', 0, 0, tiled=True)  11.8 us
    ppermute x1, starting transfers between devices, body(): other = lax.ppermute(own, 'core', [(0, 1), (1, 0)])  4 us
    ppermute x1, waiting for transfers between devices, body(): lax.ppermute(normed, ('z', 'core'), [(i, (i - 1 + 2 * (i % 2)) % 16) for...  2.25 us
    pallas_call x1, Pallas kernels, body(): return final(own_part, done, far, w1, merged)  1.98 us
    pallas_call x1, Pallas kernels, body(): q, summed, top = half(got, own)  1.98 us
    pallas_call x1, Pallas kernels, body(): call(second_half_kernel, [(8, 240, HD)], [BF], [VM] * 4)  1.98 us
  transfers between devices with their start and end apart: 3, of which 1 were waited for; matrix products, arithmetic and copies ran while one was open for 0% of the time, Pallas kernels for 6%

profile of v5, /device:TPU:1, one launch (start us, length us, event | category | flops | bytes accessed | tf_op | source)
XLA Modules:
  0.0 70.4 jit_solution(10906546622367710932)
XLA Ops:
  0.0 1.1 %shard_map.64 = bf16[16,144,128]{2,1,0:T(8,128)(2,1)S(1)} custom-call(bf16[2,64,1024]{2,1,0:T(8,128)(2,1)} %bitcast.12, bf16[8,1024]{1,0:T(8,128)(2,1)} %k_hbm.1, bf16[8,1024]{1,0:T(8,128)(2,1)} %v_hbm.1), custom_call_target="tpu_custom_call" | custom-call | flops 1000000 | bytes 10000 | tf_op jit(solution)/shard_map/pallas_call | solution.py:236
  1.1 18.8 %all_to_all.15.q_ref = bf16[16,144,128]{2,1,0:T(8,128)(2,1)S(1)} all-to-all(bf16[16,144,128]{2,1,0:T(8,128)(2,1)S(1)} %shard_map.64), channel_id=1, replica_groups=mesh['z'=8,'core'=2,'gy'=8,'seq'=2] {'gy','seq'}, dimensions={0} | all-to-all | bytes 1179648 | tf_op jit(solution)/shard_map/all_to_all | solution.py:248
  19.9 0.1 broadcast_in_dim.8
  20.0 22.4 %all_to_all.16.kv_ref = bf16[8,256,128]{2,1,0:T(8,128)(2,1)S(1)} all-to-all(bf16[8,256,128]{2,1,0:T(8,128)(2,1)S(1)} %broadcast_in_dim.8), channel_id=1, replica_groups=mesh['z'=8,'core'=2,'gy'=8,'seq'=2] {'z'}, dimensions={0} | all-to-all | bytes 1048576 | tf_op jit(solution)/shard_map/all_to_all | solution.py:250
  42.4 4.0 %collective-permute-start = (bf16[8,256,128]{2,1,0:T(8,128)(2,1)S(1)}, bf16[8,256,128]{2,1,0:T(8,128)(2,1)S(1)}, u32[]{:S(2)}, u32[]{:S(2)}) collective-permute-start(bf16[8,256,128]{2,1,0:T(8,128)(2,1)S(1)} %all_to_all.16.kv_ref), channel_id=1, source_target_pairs={{0,16},{16,0},{1,17},{17,1},{2,18},{18,2},{3,19},{19,3},{4,20},{20... | collective-permute-start | bytes 1572872 | tf_op jit(solution)/shard_map/ppermute | solution.py:251
  46.4 2.0 %shard_map.65 = (bf16[1280,128]{1,0:T(8,128)(2,1)S(1)}, f32[1280,256]{1,0:T(8,128)S(1)}, f32[1280,128]{1,0:T(8,128)S(1)}) custom-call(bf16[16,144,128]{2,1,0:T(8,128)(2,1)S(1)} %all_to_all.15.q_ref, bf16[8,256,128]{2,1,0:T(8,128)(2,1)S(1)} %all_to_all.16.kv_ref), custom_call_target="tpu_custom_call" | custom-call | flops 1000000 | bytes 10000 | tf_op jit(solution)/shard_map/pallas_call | solution.py:253
  48.4 0.0 collective-permute-done.kv_ref
  48.4 0.0 copy-start.2
  48.4 2.0 %shard_map.66 = bf16[8,240,128]{2,1,0:T(8,128)(2,1)S(1)} custom-call(bf16[1280,128]{1,0:T(8,128)(2,1)S(1)} %get-tuple-element.8.q_ref, bf16[8,256,128]{2,1,0:T(8,128)(2,1)S(1)} %collective-permute-done.kv_ref, f32[1280,256]{1,0:T(8,128)S(1)} %get-tuple-element.9.sum_ref, f32[1280,128]{1,0:T(8,128)S(1)} %get-tuple-element.10.top_ref), custom_call_target="tpu_custom_call" | custom-call | flops 1000000 | bytes 10000 | tf_op jit(solution)/shard_map/pallas_call | solution.py:254
  50.4 0.0 copy-start.1
  50.4 11.8 %all_to_all.17.a_ref = bf16[8,240,128]{2,1,0:T(8,128)(2,1)S(1)} all-to-all(bf16[8,240,128]{2,1,0:T(8,128)(2,1)S(1)} %shard_map.66), channel_id=1, replica_groups=mesh['z'=8,'core'=2,'gy'=8,'seq'=2] {'gy'}, dimensions={0} | all-to-all | bytes 983040 | tf_op jit(solution)/shard_map/all_to_all | solution.py:255
  62.2 0.0 copy-done.2
  62.3 0.4 shard_map.67.own_ref
  62.6 0.0 copy-start
  62.6 1.2 %collective-permute-start.1 = (bf16[240,256]{1,0:T(8,128)(2,1)S(1)}, bf16[240,256]{1,0:T(8,128)(2,1)S(1)}, u32[]{:S(2)}, u32[]{:S(2)}) collective-permute-start(bf16[240,256]{1,0:T(8,128)(2,1)S(1)} %shard_map.67.own_ref), channel_id=1, source_target_pairs={{0,16},{16,0},{1,17},{17,1},{2,18},{18,2},{3,19},{19,3},{4,20},{20... | collective-permute-start | bytes 368648 | tf_op jit(solution)/shard_map/ppermute | solution.py:258
  63.9 0.3 collective-permute-start.2
  64.1 0.0 copy-done.1
  64.1 0.5 shard_map.70.w2_ref
  64.7 0.0 copy-done
  64.7 0.9 %shard_map.68.own_ref = f32[4,160,384]{2,1,0:T(8,128)S(1)} custom-call(bf16[240,256]{1,0:T(8,128)(2,1)S(1)} %shard_map.67.own_ref, bf16[27,256,128]{2,1,0:T(8,128)(2,1)S(1)} %bitcast.8), custom_call_target="tpu_custom_call" | custom-call | flops 1000000 | bytes 10000 | tf_op jit(solution)/shard_map/pallas_call | solution.py:261
  65.6 0.0 collective-permute-done.1.near_ref
  65.6 0.6 shard_map.69.done_ref
  66.2 2.2 %collective-permute-done.2.far_ref = bf16[240,256]{1,0:T(8,128)(2,1)S(1)} collective-permute-done((bf16[240,256]{1,0:T(8,128)(2,1)S(1)}, bf16[240,256]{1,0:T(8,128)(2,1)S(1)}, u32[]{:S(2)}, u32[]{:S(2)}) %collective-permute-start.2) | collective-permute-done | bytes 122912 | tf_op jit(solution)/shard_map/ppermute | solution.py:257
  68.5 2.0 %shard_map.71 = bf16[4,16,16,128]{3,2,1,0:T(8,128)(2,1)} custom-call(f32[4,160,384]{2,1,0:T(8,128)S(1)} %shard_map.68.own_ref, bf16[2,160,128]{2,1,0:T(8,128)(2,1)S(1)} %shard_map.69.done_ref, bf16[240,256]{1,0:T(8,128)(2,1)S(1)} %collective-permute-done.2.far_ref, bf16[27,256,128]{2,1,0:T(8,128)(2,1)S(1)} %bitcast.10, bf16[4,512,512]{2,1,0:T(8,128)(2,1)S(1)} %shard_map.70.w2_ref), custom_call_target="tpu_custom_call" | custom-call | flops 1000000 | bytes 10000 | tf_op jit(solution)/shard_map/pallas_call | solution.py:270
  (2 shorter events, 0.0 us)
Async XLA Ops:
  42.4 6.0 %collective-permute-start = (bf16[8,256,128]{2,1,0:T(8,128)(2,1)S(1)}, bf16[8,256,128]{2,1,0:T(8,128)(2,1)S(1)}, u32[]{:S(2)}, u32[]{:S(2)}) collective-permute-start(bf16[8,256,128]{2,1,0:T(8,128)(2,1)S(1)} %all_to_all.16.kv_ref), channel_id=1, source_target_pairs={{0,16},{16,0},{1,17},{17,1},{2,18},{18,2},{3,19},{19,3},{4,20},{20... | collective-permute-start | bytes 1572872 | tf_op jit(solution)/shard_map/ppermute | solution.py:251
  48.4 13.8 %copy-start.2 = (bf16[1024,256]{1,0:T(8,128)(2,1)S(1)}, bf16[1024,256]{1,0:T(8,128)(2,1)}, u32[]{:S(2)}) copy-start(bf16[1024,256]{1,0:T(8,128)(2,1)} %w_ref.1) | copy-start | bytes 1572868
  50.4 13.7 %copy-start.1 = (bf16[3,3,3,128,128]{4,3,2,1,0:T(8,128)(2,1)S(1)}, bf16[3,3,3,128,128]{4,3,2,1,0:T(8,128)(2,1)}, u32[]{:S(2)}) copy-start(bf16[3,3,3,128,128]{4,3,2,1,0:T(8,128)(2,1)} %param.11) | copy-start | bytes 2654212
  62.6 2.0 %copy-start = (bf16[3,3,3,256,128]{4,3,2,1,0:T(8,128)(2,1)S(1)}, bf16[3,3,3,256,128]{4,3,2,1,0:T(8,128)(2,1)}, u32[]{:S(2)}) copy-start(bf16[3,3,3,256,128]{4,3,2,1,0:T(8,128)(2,1)} %param.10) | copy-start | bytes 5308420
  62.6 2.9 %collective-permute-start.1 = (bf16[240,256]{1,0:T(8,128)(2,1)S(1)}, bf16[240,256]{1,0:T(8,128)(2,1)S(1)}, u32[]{:S(2)}, u32[]{:S(2)}) collective-permute-start(bf16[240,256]{1,0:T(8,128)(2,1)S(1)} %shard_map.67.own_ref), channel_id=1, source_target_pairs={{0,16},{16,0},{1,17},{17,1},{2,18},{18,2},{3,19},{19,3},{4,20},{20... | collective-permute-start | bytes 368648 | tf_op jit(solution)/shard_map/ppermute | solution.py:258
  63.9 4.6 %collective-permute-start.2 = (bf16[240,256]{1,0:T(8,128)(2,1)S(1)}, bf16[240,256]{1,0:T(8,128)(2,1)S(1)}, u32[]{:S(2)}, u32[]{:S(2)}) collective-permute-start(bf16[240,256]{1,0:T(8,128)(2,1)S(1)} %shard_map.67.own_ref), channel_id=1, source_target_pairs={{0,240},{16,32},{32,16},{48,64},{64,48},{80,96},{96,80},{112,128},... | collective-permute-start | bytes 368648 | tf_op jit(solution)/shard_map/ppermute | solution.py:257

commit v6 on v5

--- a/solution.py
+++ b/solution.py
@@ -26,6 +26,10 @@
         compiler_params=pltpu.CompilerParams(vmem_limit_bytes=24 * 1024 * 1024),
         cost_estimate=pl.CostEstimate(flops=10**6, bytes_accessed=10000, transcendentals=0),
     )
+
+
+def slot(tile, half):
+    return 4 * (tile // 2) + 2 * half + tile % 2
 
 
 def pack_kernel(q_hbm, k_hbm, v_hbm, out_ref, q_ref, k_ref, v_ref, sems):
@@ -41,9 +45,9 @@
         cols = slice(h * HD, (h + 1) * HD)
         pair = jnp.concatenate([k_ref[:, cols].astype(F32), v_ref[:, cols].astype(F32)], axis=0).astype(BF)
         for s in range(2):
-            out_ref[2 * h + s, 0:64] = q_ref[0, :, cols]
-            out_ref[2 * h + s, 64:128] = q_ref[1, :, cols]
-            out_ref[2 * h + s, 128:144] = pair
+            out_ref[slot(h, s), 0:64] = q_ref[0, :, cols]
+            out_ref[slot(h, s), 64:128] = q_ref[1, :, cols]
+            out_ref[slot(h, s), 128:144] = pair
 
 
 def halves(ref):
@@ -62,10 +66,10 @@
     row = lax.broadcasted_iota(jnp.int32, (32, 128), 0)
     col = lax.broadcasted_iota(jnp.int32, (32, 128), 1)
     pick = (col == (row // 2) % 2 * 64 + (row // 4) * 8 + row % 2 + 6 * seq).astype(F32).astype(BF)
-    near = [jnp.dot(pick, q_ref[2 * g + 1 - seq, 0:128], preferred_element_type=F32).astype(BF) for g in range(8)]
+    near = [jnp.dot(pick, q_ref[slot(g, 1 - seq), 0:128], preferred_element_type=F32).astype(BF) for g in range(8)]
     for n in range(10):
         rows = slice(128 * n, 128 * n + 128)
-        q = q_ref[2 * n + seq, 0:128] if n < 8 else jnp.concatenate(near[4 * n - 32 : 4 * n - 28], axis=0)
+        q = q_ref[slot(n, seq), 0:128] if n < 8 else jnp.concatenate(near[4 * n - 32 : 4 * n - 28], axis=0)
         scores, top = scores_of(q, keys)
         weights = jnp.exp2((scores - top) * SCALE).astype(BF)
         q_out[rows] = q
@@ -171,7 +175,7 @@
 
 
 def side(at_left, slabs, own_ref, w1_ref):
-    gx, gy, seq = x_tile(), lax.axis_index("gy"), lax.axis_index("seq")
+    gx, gy, seq = x_tile(), 2 * lax.axis_index("chip_x") + lax.axis_index("low_y"), lax.axis_index("seq")
     row = lax.broadcasted_iota(jnp.int32, (160, 128), 0)
     at_z = seq * 8 - 1 + row % 16
     at_y = gy * 8 - 1 + row // 16
@@ -245,14 +249,14 @@
             pltpu.SemaphoreType.DMA((3,)),
         ],
     )(*(pltpu.with_memory_space_constraint(a, pltpu.HBM) for a in (queries.reshape(2, 64, H * HD), keys, values)))
-    got = lax.all_to_all(sent, ("gy", "seq"), 0, 0, tiled=True)
+    got = lax.all_to_all(sent, ("chip_x", "seq", "low_y"), 0, 0, tiled=True)
     pair = got[:, 128:144].reshape(16, 2, 8, HD).transpose(1, 0, 2, 3).reshape(1, 256, HD)
     own = lax.all_to_all(jnp.broadcast_to(pair, (8, 256, HD)), "z", 0, 0, tiled=True)
     other = lax.ppermute(own, "core", [(0, 1), (1, 0)])
     half = call(first_half_kernel, [(1280, HD), (1280, 2 * HD), (1280, HD)], [BF, F32, F32], [VM, VM])
     q, summed, top = half(got, own)
     attended = call(second_half_kernel, [(8, 240, HD)], [BF], [VM] * 4)(q, other, summed, top)
-    back = lax.all_to_all(attended, "gy", 0, 0, tiled=True)
+    back = lax.all_to_all(attended, ("chip_x", "low_y"), 0, 0, tiled=True)
     normed = call(project_kernel, [(240, 256)], [BF], [VM, VM])(back, w_out)
     far = lax.ppermute(normed, ("z", "core"), [(i, (i - 1 + 2 * (i % 2)) % 16) for i in range(16)])
     near = lax.ppermute(normed, "core", [(0, 1), (1, 0)])
@@ -271,9 +275,9 @@
 
 
 def solution(mesh):
-    cut = Mesh(mesh.devices.reshape(8, 2, 8, 2), ("z", "core", "gy", "seq"))
-    tokens = P(("z", "core", "gy", "seq"), None)
-    voxels = P(("z", "core"), "gy", "seq", None)
+    cut = Mesh(mesh.devices.reshape(8, 2, 4, 2, 2), ("z", "core", "chip_x", "low_y", "seq"))
+    tokens = P(("z", "core", "chip_x", "low_y", "seq"), None)
+    voxels = P(("z", "core"), ("chip_x", "low_y"), "seq", None)
     return jax.shard_map(
         body, mesh=cut, in_specs=(voxels, tokens, tokens, P(), P(), P()), out_specs=voxels, check_vma=False
     )

time: 70.7 us -> 70.1 us (level)
  no operation moved by 1% of the time
where the time goes in v6:
time: 70.1 us; the launch traced here: 69.9 us
  blocking collectives  52.7 us (75%)
  Pallas kernels  9.43 us (13%)
  starting transfers between devices  5.27 us (8%)
  waiting for transfers between devices  2.25 us (3%)
    all_to_all x1, blocking collectives, body(): lax.all_to_all(jnp.broadcast_to(pair, (8, 256, HD)), 'z', 0, 0, tiled=True)  22.4 us
    all_to_all x1, blocking collectives, body(): got = lax.all_to_all(sent, ('chip_x', 'seq', 'low_y'), 0, 0, tiled=True)  18.4 us
    all_to_all x1, blocking collectives, body(): back = lax.all_to_all(attended, ('chip_x', 'low_y'), 0, 0, tiled=True)  11.9 us
    ppermute x1, starting transfers between devices, body(): other = lax.ppermute(own, 'core', [(0, 1), (1, 0)])  4.02 us
    ppermute x1, waiting for transfers between devices, body(): lax.ppermute(normed, ('z', 'core'), [(i, (i - 1 + 2 * (i % 2)) % 16) for...  2.25 us
    pallas_call x1, Pallas kernels, body(): return final(own_part, done, far, w1, merged)  2 us
    pallas_call x1, Pallas kernels, body(): call(second_half_kernel, [(8, 240, HD)], [BF], [VM] * 4)  1.98 us
    pallas_call x1, Pallas kernels, body(): q, summed, top = half(got, own)  1.98 us
  transfers between devices with their start and end apart: 3, of which 1 were waited for; matrix products, arithmetic and copies ran while one was open for 0% of the time, Pallas kernels for 6%

profile of v6, /device:TPU:1, one launch (start us, length us, event | category | flops | bytes accessed | tf_op | source)
XLA Modules:
  0.0 69.9 jit_solution(2295351203944824910)
XLA Ops:
  0.0 1.1 %shard_map.64 = bf16[16,144,128]{2,1,0:T(8,128)(2,1)S(1)} custom-call(bf16[2,64,1024]{2,1,0:T(8,128)(2,1)} %bitcast.12, bf16[8,1024]{1,0:T(8,128)(2,1)} %k_hbm.1, bf16[8,1024]{1,0:T(8,128)(2,1)} %v_hbm.1), custom_call_target="tpu_custom_call" | custom-call | flops 1000000 | bytes 10000 | tf_op jit(solution)/shard_map/pallas_call | solution.py:240
  1.1 18.4 %all_to_all.15.q_ref = bf16[16,144,128]{2,1,0:T(8,128)(2,1)S(1)} all-to-all(bf16[16,144,128]{2,1,0:T(8,128)(2,1)S(1)} %shard_map.64), channel_id=1, replica_groups=mesh['z'=8,'core'=2,'chip_x'=4,'low_y'=2,'seq'=2] {'chip_x','seq','low_y'}, dimensions={0} | all-to-all | bytes 1179648 | tf_op jit(solution)/shard_map/all_to_all | solution.py:252
  19.4 0.1 broadcast_in_dim.8
  19.5 22.4 %all_to_all.16.kv_ref = bf16[8,256,128]{2,1,0:T(8,128)(2,1)S(1)} all-to-all(bf16[8,256,128]{2,1,0:T(8,128)(2,1)S(1)} %broadcast_in_dim.8), channel_id=1, replica_groups=mesh['z'=8,'core'=2,'chip_x'=4,'low_y'=2,'seq'=2] {'z'}, dimensions={0} | all-to-all | bytes 1048576 | tf_op jit(solution)/shard_map/all_to_all | solution.py:254
  41.9 4.0 %collective-permute-start = (bf16[8,256,128]{2,1,0:T(8,128)(2,1)S(1)}, bf16[8,256,128]{2,1,0:T(8,128)(2,1)S(1)}, u32[]{:S(2)}, u32[]{:S(2)}) collective-permute-start(bf16[8,256,128]{2,1,0:T(8,128)(2,1)S(1)} %all_to_all.16.kv_ref), channel_id=1, source_target_pairs={{0,16},{16,0},{1,17},{17,1},{2,18},{18,2},{3,19},{19,3},{4,20},{20... | collective-permute-start | bytes 1572872 | tf_op jit(solution)/shard_map/ppermute | solution.py:255
  45.9 2.0 %shard_map.65 = (bf16[1280,128]{1,0:T(8,128)(2,1)S(1)}, f32[1280,256]{1,0:T(8,128)S(1)}, f32[1280,128]{1,0:T(8,128)S(1)}) custom-call(bf16[16,144,128]{2,1,0:T(8,128)(2,1)S(1)} %all_to_all.15.q_ref, bf16[8,256,128]{2,1,0:T(8,128)(2,1)S(1)} %all_to_all.16.kv_ref), custom_call_target="tpu_custom_call" | custom-call | flops 1000000 | bytes 10000 | tf_op jit(solution)/shard_map/pallas_call | solution.py:257
  47.9 0.0 collective-permute-done.kv_ref
  47.9 0.0 copy-start.2
  47.9 2.0 %shard_map.66 = bf16[8,240,128]{2,1,0:T(8,128)(2,1)S(1)} custom-call(bf16[1280,128]{1,0:T(8,128)(2,1)S(1)} %get-tuple-element.8.q_ref, bf16[8,256,128]{2,1,0:T(8,128)(2,1)S(1)} %collective-permute-done.kv_ref, f32[1280,256]{1,0:T(8,128)S(1)} %get-tuple-element.9.sum_ref, f32[1280,128]{1,0:T(8,128)S(1)} %get-tuple-element.10.top_ref), custom_call_target="tpu_custom_call" | custom-call | flops 1000000 | bytes 10000 | tf_op jit(solution)/shard_map/pallas_call | solution.py:258
  49.9 0.0 copy-start.1
  49.9 11.9 %all_to_all.17.a_ref = bf16[8,240,128]{2,1,0:T(8,128)(2,1)S(1)} all-to-all(bf16[8,240,128]{2,1,0:T(8,128)(2,1)S(1)} %shard_map.66), channel_id=1, replica_groups=mesh['z'=8,'core'=2,'chip_x'=4,'low_y'=2,'seq'=2] {'chip_x','low_y'}, dimensions={0} | all-to-all | bytes 983040 | tf_op jit(solution)/shard_map/all_to_all | solution.py:259
  61.9 0.0 copy-done.2
  61.9 0.4 shard_map.67.own_ref
  62.3 0.0 copy-start
  62.3 1.0 %collective-permute-start.1 = (bf16[240,256]{1,0:T(8,128)(2,1)S(1)}, bf16[240,256]{1,0:T(8,128)(2,1)S(1)}, u32[]{:S(2)}, u32[]{:S(2)}) collective-permute-start(bf16[240,256]{1,0:T(8,128)(2,1)S(1)} %shard_map.67.own_ref), channel_id=1, source_target_pairs={{0,16},{16,0},{1,17},{17,1},{2,18},{18,2},{3,19},{19,3},{4,20},{20... | collective-permute-start | bytes 368648 | tf_op jit(solution)/shard_map/ppermute | solution.py:262
  63.3 0.3 collective-permute-start.2
  63.5 0.0 copy-done.1
  63.5 0.5 shard_map.70.w2_ref
  64.1 0.0 copy-done
  64.1 0.9 %shard_map.68.own_ref = f32[4,160,384]{2,1,0:T(8,128)S(1)} custom-call(bf16[240,256]{1,0:T(8,128)(2,1)S(1)} %shard_map.67.own_ref, bf16[27,256,128]{2,1,0:T(8,128)(2,1)S(1)} %bitcast.8), custom_call_target="tpu_custom_call" | custom-call | flops 1000000 | bytes 10000 | tf_op jit(solution)/shard_map/pallas_call | solution.py:265
  65.0 0.0 collective-permute-done.1.near_ref
  65.0 0.6 shard_map.69.done_ref
  65.6 2.2 %collective-permute-done.2.far_ref = bf16[240,256]{1,0:T(8,128)(2,1)S(1)} collective-permute-done((bf16[240,256]{1,0:T(8,128)(2,1)S(1)}, bf16[240,256]{1,0:T(8,128)(2,1)S(1)}, u32[]{:S(2)}, u32[]{:S(2)}) %collective-permute-start.2) | collective-permute-done | bytes 122912 | tf_op jit(solution)/shard_map/ppermute | solution.py:261
  67.9 2.0 %shard_map.71 = bf16[4,16,16,128]{3,2,1,0:T(8,128)(2,1)} custom-call(f32[4,160,384]{2,1,0:T(8,128)S(1)} %shard_map.68.own_ref, bf16[2,160,128]{2,1,0:T(8,128)(2,1)S(1)} %shard_map.69.done_ref, bf16[240,256]{1,0:T(8,128)(2,1)S(1)} %collective-permute-done.2.far_ref, bf16[27,256,128]{2,1,0:T(8,128)(2,1)S(1)} %bitcast.10, bf16[4,512,512]{2,1,0:T(8,128)(2,1)S(1)} %shard_map.70.w2_ref), custom_call_target="tpu_custom_call" | custom-call | flops 1000000 | bytes 10000 | tf_op jit(solution)/shard_map/pallas_call | solution.py:274
  (2 shorter events, 0.0 us)
Async XLA Ops:
  41.9 6.0 %collective-permute-start = (bf16[8,256,128]{2,1,0:T(8,128)(2,1)S(1)}, bf16[8,256,128]{2,1,0:T(8,128)(2,1)S(1)}, u32[]{:S(2)}, u32[]{:S(2)}) collective-permute-start(bf16[8,256,128]{2,1,0:T(8,128)(2,1)S(1)} %all_to_all.16.kv_ref), channel_id=1, source_target_pairs={{0,16},{16,0},{1,17},{17,1},{2,18},{18,2},{3,19},{19,3},{4,20},{20... | collective-permute-start | bytes 1572872 | tf_op jit(solution)/shard_map/ppermute | solution.py:255
  47.9 13.9 %copy-start.2 = (bf16[1024,256]{1,0:T(8,128)(2,1)S(1)}, bf16[1024,256]{1,0:T(8,128)(2,1)}, u32[]{:S(2)}) copy-start(bf16[1024,256]{1,0:T(8,128)(2,1)} %w_ref.1) | copy-start | bytes 1572868
  49.9 13.6 %copy-start.1 = (bf16[3,3,3,128,128]{4,3,2,1,0:T(8,128)(2,1)S(1)}, bf16[3,3,3,128,128]{4,3,2,1,0:T(8,128)(2,1)}, u32[]{:S(2)}) copy-start(bf16[3,3,3,128,128]{4,3,2,1,0:T(8,128)(2,1)} %param.11) | copy-start | bytes 2654212
  62.3 1.8 %copy-start = (bf16[3,3,3,256,128]{4,3,2,1,0:T(8,128)(2,1)S(1)}, bf16[3,3,3,256,128]{4,3,2,1,0:T(8,128)(2,1)}, u32[]{:S(2)}) copy-start(bf16[3,3,3,256,128]{4,3,2,1,0:T(8,128)(2,1)} %param.10) | copy-start | bytes 5308420
  62.3 2.7 %collective-permute-start.1 = (bf16[240,256]{1,0:T(8,128)(2,1)S(1)}, bf16[240,256]{1,0:T(8,128)(2,1)S(1)}, u32[]{:S(2)}, u32[]{:S(2)}) collective-permute-start(bf16[240,256]{1,0:T(8,128)(2,1)S(1)} %shard_map.67.own_ref), channel_id=1, source_target_pairs={{0,16},{16,0},{1,17},{17,1},{2,18},{18,2},{3,19},{19,3},{4,20},{20... | collective-permute-start | bytes 368648 | tf_op jit(solution)/shard_map/ppermute | solution.py:262
  63.3 4.6 %collective-permute-start.2 = (bf16[240,256]{1,0:T(8,128)(2,1)S(1)}, bf16[240,256]{1,0:T(8,128)(2,1)S(1)}, u32[]{:S(2)}, u32[]{:S(2)}) collective-permute-start(bf16[240,256]{1,0:T(8,128)(2,1)S(1)} %shard_map.67.own_ref), channel_id=1, source_target_pairs={{0,240},{16,32},{32,16},{48,64},{64,48},{80,96},{96,80},{112,128},... | collective-permute-start | bytes 368648 | tf_op jit(solution)/shard_map/ppermute | solution.py:261

commit v7 on v6

--- a/solution.py
+++ b/solution.py
@@ -45,9 +45,8 @@
         cols = slice(h * HD, (h + 1) * HD)
         pair = jnp.concatenate([k_ref[:, cols].astype(F32), v_ref[:, cols].astype(F32)], axis=0).astype(BF)
         for s in range(2):
-            out_ref[slot(h, s), 0:64] = q_ref[0, :, cols]
-            out_ref[slot(h, s), 64:128] = q_ref[1, :, cols]
-            out_ref[slot(h, s), 128:144] = pair
+            out_ref[slot(h, s), 0:64] = q_ref[s, :, cols]
+            out_ref[slot(h, s), 64:80] = pair
 
 
 def halves(ref):
@@ -60,70 +59,66 @@
     return scores, jnp.max(scores, axis=1, keepdims=True)
 
 
-def first_half_kernel(q_ref, kv_ref, q_out, sum_out, top_out):
-    seq = lax.axis_index("seq")
+def queries_of(q_ref, n):
+    return jnp.concatenate([q_ref[slot(n, 0), 0:64], q_ref[slot(n, 1), 0:64]], axis=0)
+
+
+def first_half_kernel(q_ref, kv_ref, sum_out, top_out):
     keys, vals = halves(kv_ref)
-    row = lax.broadcasted_iota(jnp.int32, (32, 128), 0)
-    col = lax.broadcasted_iota(jnp.int32, (32, 128), 1)
-    pick = (col == (row // 2) % 2 * 64 + (row // 4) * 8 + row % 2 + 6 * seq).astype(F32).astype(BF)
-    near = [jnp.dot(pick, q_ref[slot(g, 1 - seq), 0:128], preferred_element_type=F32).astype(BF) for g in range(8)]
-    for n in range(10):
+    for n in range(8):
         rows = slice(128 * n, 128 * n + 128)
-        q = q_ref[slot(n, seq), 0:128] if n < 8 else jnp.concatenate(near[4 * n - 32 : 4 * n - 28], axis=0)
-        scores, top = scores_of(q, keys)
+        scores, top = scores_of(queries_of(q_ref, n), keys)
         weights = jnp.exp2((scores - top) * SCALE).astype(BF)
-        q_out[rows] = q
         sum_out[rows] = jnp.dot(weights, vals, preferred_element_type=F32)
         top_out[rows] = jnp.broadcast_to(top, (128, HD))
 
 
 def second_half_kernel(q_ref, kv_ref, sum_ref, top_ref, out_ref):
     keys, vals = halves(kv_ref)
-    edge = jnp.zeros((32, HD), BF)
-    out_ref[0, 0:32] = edge
-    out_ref[7, 160:192] = edge
-    near = []
-    for n in range(10):
+    edge = jnp.zeros((16, HD), BF)
+    for s in range(2):
+        out_ref[slot(0, s), 0:16] = edge
+        out_ref[slot(7, s), 80:96] = edge
+    for n in range(8):
         rows = slice(128 * n, 128 * n + 128)
-        scores, top = scores_of(q_ref[rows], keys)
+        scores, top = scores_of(queries_of(q_ref, n), keys)
         before = top_ref[rows, 0:1]
         top = jnp.maximum(top, before)
         weights = jnp.exp2((scores - top) * SCALE).astype(BF)
         kept = jnp.exp2((before - top) * SCALE)
         both = sum_ref[rows] * kept + jnp.dot(weights, vals, preferred_element_type=F32)
-        done = both[:, 0:HD] / both[:, HD : 2 * HD]
-        if n >= 8:
-            near.append(done)
-            continue
-        done = done.reshape(2, 8, 8, HD)
-        done = jnp.concatenate([done[0], done[1]], axis=1).reshape(128, HD).astype(BF)
-        out_ref[n, 32:160] = done
-        if n < 7:
-            out_ref[n + 1, 0:32] = done[96:128]
-        if n > 0:
-            out_ref[n - 1, 160:192] = done[0:32]
-    none = jnp.zeros((8, HD), F32)
-    near = jnp.concatenate([none] + near + [none], axis=0)
-    for g in range(8):
-        out_ref[g, 192:240] = near[32 * g : 32 * g + 48].astype(BF)
+        done = (both[:, 0:HD] / both[:, HD : 2 * HD]).astype(BF)
+        for s in range(2):
+            half = done[64 * s : 64 * s + 64]
+            out_ref[slot(n, s), 16:80] = half
+            if n < 7:
+                out_ref[slot(n + 1, s), 0:16] = half[48:64]
+            if n > 0:
+                out_ref[slot(n - 1, s), 80:96] = half[0:16]
+    row = lax.broadcasted_iota(jnp.int32, (32, 96), 0)
+    col = lax.broadcasted_iota(jnp.int32, (32, 96), 1)
+    for s in range(2):
+        pick = ((col == (row // 2) * 8 + row % 2 + 6 * s) & (row < 24)).astype(F32).astype(BF)
+        for n in range(8):
+            other = out_ref[slot(n, 1 - s), 0:96]
+            out_ref[slot(n, s), 96:128] = jnp.dot(pick, other, preferred_element_type=F32).astype(BF)
 
 
 def project_kernel(a_ref, w_ref, out_ref):
-    rows = jnp.concatenate([a_ref[h] for h in range(H)], axis=1)
-    projected = jnp.dot(rows, w_ref[...], preferred_element_type=F32)
+    rows = [jnp.concatenate([a_ref[slot(h, x)] for h in range(H)], axis=1) for x in range(2)]
+    projected = jnp.dot(jnp.concatenate(rows, axis=0), w_ref[...], preferred_element_type=F32)
     scale = lax.rsqrt(jnp.mean(projected * projected, axis=1, keepdims=True) + 1e-06)
     out_ref[...] = (projected * scale).astype(BF)
 
 
 def laid_out(normed):
     seq = lax.axis_index("seq")
-    half = normed[0:192].astype(F32).reshape(12, 2, 8, 256)
-    near = normed[192:240].astype(F32).reshape(6, 8, 256)
     row = lax.broadcasted_iota(jnp.int32, (12, 8, 256), 1)
     slabs = []
     for x in range(2):
-        middle = pltpu.roll(half[:, x], 2, 1)
-        ends = [pltpu.roll(near, (8 - 4 * odd - 2 * x) % 8, 1) if odd + x else near for odd in range(2)]
+        middle = pltpu.roll(normed[128 * x : 128 * x + 96].astype(F32).reshape(12, 8, 256), 2, 1)
+        near = normed[128 * x + 96 : 128 * x + 128].astype(F32).reshape(4, 8, 256)[0:3]
+        ends = [pltpu.roll(near, 8 - 2 * k, 1) if k else near for k in range(4)]
         ends = jnp.stack(ends, axis=1).reshape(12, 8, 256)
         upper = jnp.where(row < 2, jnp.where(seq == 1, ends, 0.0), middle)
         lower = jnp.where((row < 4) & (seq == 0), pltpu.roll(ends, 2, 1), 0.0)
@@ -239,7 +234,7 @@
 def body(queries, keys, values, w_out, conv_first, conv_second):
     sent = call(
         pack_kernel,
-        [(16, 144, HD)],
+        [(16, 80, HD)],
         [BF],
         [HB] * 3,
         [
@@ -250,14 +245,13 @@
         ],
     )(*(pltpu.with_memory_space_constraint(a, pltpu.HBM) for a in (queries.reshape(2, 64, H * HD), keys, values)))
     got = lax.all_to_all(sent, ("chip_x", "seq", "low_y"), 0, 0, tiled=True)
-    pair = got[:, 128:144].reshape(16, 2, 8, HD).transpose(1, 0, 2, 3).reshape(1, 256, HD)
+    pair = got[:, 64:80].reshape(16, 2, 8, HD).transpose(1, 0, 2, 3).reshape(1, 256, HD)
     own = lax.all_to_all(jnp.broadcast_to(pair, (8, 256, HD)), "z", 0, 0, tiled=True)
     other = lax.ppermute(own, "core", [(0, 1), (1, 0)])
-    half = call(first_half_kernel, [(1280, HD), (1280, 2 * HD), (1280, HD)], [BF, F32, F32], [VM, VM])
-    q, summed, top = half(got, own)
-    attended = call(second_half_kernel, [(8, 240, HD)], [BF], [VM] * 4)(q, other, summed, top)
-    back = lax.all_to_all(attended, ("chip_x", "low_y"), 0, 0, tiled=True)
-    normed = call(project_kernel, [(240, 256)], [BF], [VM, VM])(back, w_out)
+    summed, top = call(first_half_kernel, [(1024, 2 * HD), (1024, HD)], [F32, F32], [VM, VM])(got, own)
+    attended = call(second_half_kernel, [(16, 128, HD)], [BF], [VM] * 4)(got, other, summed, top)
+    back = lax.all_to_all(attended, ("chip_x", "seq", "low_y"), 0, 0, tiled=True)
+    normed = call(project_kernel, [(256, 256)], [BF], [VM, VM])(back, w_out)
     far = lax.ppermute(normed, ("z", "core"), [(i, (i - 1 + 2 * (i % 2)) % 16) for i in range(16)])
     near = lax.ppermute(normed, "core", [(0, 1), (1, 0)])
     w1 = conv_first.reshape(27, 256, 128)

time: 70.1 us -> 69.7 us (level)
  starting transfers between devices: 5.27 us -> 6.45 us
  blocking collectives: 52.7 us -> 51.6 us
    all_to_all x1, blocking collectives: 18.4 us -> 15.2 us  [body(): got = lax.all_to_all(sent, ('chip_x', 'seq', 'low_y'), 0, 0, tiled=True)]
    all_to_all x1, blocking collectives: 11.9 us -> 14 us  [body(): lax.all_to_all(attended, ('chip_x', 'seq', 'low_y'), 0, 0, tiled=True)]
    ppermute x1, starting transfers between devices: 0.99 us -> 2.16 us  [body(): near = lax.ppermute(normed, 'core', [(0, 1), (1, 0)])]
  transfers between devices with their start and end apart: 3 -> 3, of which waited for: 1 -> 1; matrix products, arithmetic and copies ran while one was open for 0% -> 0% of each run, Pallas kernels for 6% -> 5%
where the time goes in v7:
time: 69.7 us; the launch traced here: 69.5 us
  blocking collectives  51.6 us (74%)
  Pallas kernels  8.86 us (13%)
  starting transfers between devices  6.45 us (9%)
  waiting for transfers between devices  2.34 us (3%)
    all_to_all x1, blocking collectives, body(): lax.all_to_all(jnp.broadcast_to(pair, (8, 256, HD)), 'z', 0, 0, tiled=True)  22.4 us
    all_to_all x1, blocking collectives, body(): got = lax.all_to_all(sent, ('chip_x', 'seq', 'low_y'), 0, 0, tiled=True)  15.2 us
    all_to_all x1, blocking collectives, body(): lax.all_to_all(attended, ('chip_x', 'seq', 'low_y'), 0, 0, tiled=True)  14 us
    ppermute x1, starting transfers between devices, body(): other = lax.ppermute(own, 'core', [(0, 1), (1, 0)])  4.02 us
    ppermute x1, waiting for transfers between devices, body(): lax.ppermute(normed, ('z', 'core'), [(i, (i - 1 + 2 * (i % 2)) % 16) for...  2.34 us
    ppermute x1, starting transfers between devices, body(): near = lax.ppermute(normed, 'core', [(0, 1), (1, 0)])  2.16 us
    pallas_call x1, Pallas kernels, body(): return final(own_part, done, far, w1, merged)  1.98 us
    pallas_call x1, Pallas kernels, body(): call(second_half_kernel, [(16, 128, HD)], [BF], [VM] * 4)  1.85 us
  transfers between devices with their start and end apart: 3, of which 1 were waited for; matrix products, arithmetic and copies ran while one was open for 0% of the time, Pallas kernels for 5%

profile of v7, /device:TPU:1, one launch (start us, length us, event | category | flops | bytes accessed | tf_op | source)
XLA Modules:
  0.0 69.5 jit_solution(13145324201411575426)
XLA Ops:
  0.0 1.0 %shard_map.64 = bf16[16,80,128]{2,1,0:T(8,128)(2,1)S(1)} custom-call(bf16[2,64,1024]{2,1,0:T(8,128)(2,1)} %bitcast.13, bf16[8,1024]{1,0:T(8,128)(2,1)} %k_hbm.1, bf16[8,1024]{1,0:T(8,128)(2,1)} %v_hbm.1), custom_call_target="tpu_custom_call" | custom-call | flops 1000000 | bytes 10000 | tf_op jit(solution)/shard_map/pallas_call | solution.py:235
  1.0 15.2 %all_to_all.15.q_ref = bf16[16,80,128]{2,1,0:T(8,128)(2,1)S(1)} all-to-all(bf16[16,80,128]{2,1,0:T(8,128)(2,1)S(1)} %shard_map.64), channel_id=1, replica_groups=mesh['z'=8,'core'=2,'chip_x'=4,'low_y'=2,'seq'=2] {'chip_x','seq','low_y'}, dimensions={0} | all-to-all | bytes 655360 | tf_op jit(solution)/shard_map/all_to_all | solution.py:247
  16.3 0.1 broadcast_in_dim.8
  16.3 22.4 %all_to_all.16.kv_ref = bf16[8,256,128]{2,1,0:T(8,128)(2,1)S(1)} all-to-all(bf16[8,256,128]{2,1,0:T(8,128)(2,1)S(1)} %broadcast_in_dim.8), channel_id=1, replica_groups=mesh['z'=8,'core'=2,'chip_x'=4,'low_y'=2,'seq'=2] {'z'}, dimensions={0} | all-to-all | bytes 1048576 | tf_op jit(solution)/shard_map/all_to_all | solution.py:249
  38.8 4.0 %collective-permute-start = (bf16[8,256,128]{2,1,0:T(8,128)(2,1)S(1)}, bf16[8,256,128]{2,1,0:T(8,128)(2,1)S(1)}, u32[]{:S(2)}, u32[]{:S(2)}) collective-permute-start(bf16[8,256,128]{2,1,0:T(8,128)(2,1)S(1)} %all_to_all.16.kv_ref), channel_id=1, source_target_pairs={{0,16},{16,0},{1,17},{17,1},{2,18},{18,2},{3,19},{19,3},{4,20},{20... | collective-permute-start | bytes 1572872 | tf_op jit(solution)/shard_map/ppermute | solution.py:250
  42.8 1.6 %shard_map.65 = (f32[1024,256]{1,0:T(8,128)S(1)}, f32[1024,128]{1,0:T(8,128)S(1)}) custom-call(bf16[16,80,128]{2,1,0:T(8,128)(2,1)S(1)} %all_to_all.15.q_ref, bf16[8,256,128]{2,1,0:T(8,128)(2,1)S(1)} %all_to_all.16.kv_ref), custom_call_target="tpu_custom_call" | custom-call | flops 1000000 | bytes 10000 | tf_op jit(solution)/shard_map/pallas_call | solution.py:251
  44.4 0.0 copy-start.2
  44.4 0.0 collective-permute-done.kv_ref
  44.4 0.0 copy-start.1
  44.4 1.8 %shard_map.66 = bf16[16,128,128]{2,1,0:T(8,128)(2,1)S(1)} custom-call(bf16[16,80,128]{2,1,0:T(8,128)(2,1)S(1)} %all_to_all.15.q_ref, bf16[8,256,128]{2,1,0:T(8,128)(2,1)S(1)} %collective-permute-done.kv_ref, f32[1024,256]{1,0:T(8,128)S(1)} %get-tuple-element.7.sum_ref, f32[1024,128]{1,0:T(8,128)S(1)} %get-tuple-element.8.top_ref), custom_call_target="tpu_custom_call" | custom-call | flops 1000000 | bytes 10000 | tf_op jit(solution)/shard_map/pallas_call | solution.py:252
  46.3 14.0 %all_to_all.17.a_ref = bf16[16,128,128]{2,1,0:T(8,128)(2,1)S(1)} all-to-all(bf16[16,128,128]{2,1,0:T(8,128)(2,1)S(1)} %shard_map.66), channel_id=1, replica_groups=mesh['z'=8,'core'=2,'chip_x'=4,'low_y'=2,'seq'=2] {'chip_x','seq','low_y'}, dimensions={0} | all-to-all | bytes 1048576 | tf_op jit(solution)/shard_map/all_to_all | solution.py:253
  60.2 0.0 copy-done.2
  60.2 0.0 copy-start
  60.3 0.4 shard_map.67.own_ref
  60.6 2.2 %collective-permute-start.1 = (bf16[256,256]{1,0:T(8,128)(2,1)S(1)}, bf16[256,256]{1,0:T(8,128)(2,1)S(1)}, u32[]{:S(2)}, u32[]{:S(2)}) collective-permute-start(bf16[256,256]{1,0:T(8,128)(2,1)S(1)} %shard_map.67.own_ref), channel_id=1, source_target_pairs={{0,16},{16,0},{1,17},{17,1},{2,18},{18,2},{3,19},{19,3},{4,20},{20... | collective-permute-start | bytes 393224 | tf_op jit(solution)/shard_map/ppermute | solution.py:256
  62.8 0.3 collective-permute-start.2
  63.1 0.0 copy-done.1
  63.1 0.5 shard_map.70.w2_ref
  63.6 0.0 copy-done
  63.6 0.9 %shard_map.68.own_ref = f32[4,160,384]{2,1,0:T(8,128)S(1)} custom-call(bf16[256,256]{1,0:T(8,128)(2,1)S(1)} %shard_map.67.own_ref, bf16[27,256,128]{2,1,0:T(8,128)(2,1)S(1)} %bitcast.8), custom_call_target="tpu_custom_call" | custom-call | flops 1000000 | bytes 10000 | tf_op jit(solution)/shard_map/pallas_call | solution.py:259
  64.5 0.0 collective-permute-done.1.near_ref
  64.6 0.6 shard_map.69.done_ref
  65.2 2.3 %collective-permute-done.2.far_ref = bf16[256,256]{1,0:T(8,128)(2,1)S(1)} collective-permute-done((bf16[256,256]{1,0:T(8,128)(2,1)S(1)}, bf16[256,256]{1,0:T(8,128)(2,1)S(1)}, u32[]{:S(2)}, u32[]{:S(2)}) %collective-permute-start.2) | collective-permute-done | bytes 131104 | tf_op jit(solution)/shard_map/ppermute | solution.py:255
  67.5 2.0 %shard_map.71 = bf16[4,16,16,128]{3,2,1,0:T(8,128)(2,1)} custom-call(f32[4,160,384]{2,1,0:T(8,128)S(1)} %shard_map.68.own_ref, bf16[2,160,128]{2,1,0:T(8,128)(2,1)S(1)} %shard_map.69.done_ref, bf16[256,256]{1,0:T(8,128)(2,1)S(1)} %collective-permute-done.2.far_ref, bf16[27,256,128]{2,1,0:T(8,128)(2,1)S(1)} %bitcast.10, bf16[4,512,512]{2,1,0:T(8,128)(2,1)S(1)} %shard_map.70.w2_ref), custom_call_target="tpu_custom_call" | custom-call | flops 1000000 | bytes 10000 | tf_op jit(solution)/shard_map/pallas_call | solution.py:268
  (2 shorter events, 0.0 us)
Async XLA Ops:
  38.8 5.6 %collective-permute-start = (bf16[8,256,128]{2,1,0:T(8,128)(2,1)S(1)}, bf16[8,256,128]{2,1,0:T(8,128)(2,1)S(1)}, u32[]{:S(2)}, u32[]{:S(2)}) collective-permute-start(bf16[8,256,128]{2,1,0:T(8,128)(2,1)S(1)} %all_to_all.16.kv_ref), channel_id=1, source_target_pairs={{0,16},{16,0},{1,17},{17,1},{2,18},{18,2},{3,19},{19,3},{4,20},{20... | collective-permute-start | bytes 1572872 | tf_op jit(solution)/shard_map/ppermute | solution.py:250
  44.4 15.9 %copy-start.2 = (bf16[1024,256]{1,0:T(8,128)(2,1)S(1)}, bf16[1024,256]{1,0:T(8,128)(2,1)}, u32[]{:S(2)}) copy-start(bf16[1024,256]{1,0:T(8,128)(2,1)} %w_ref.1) | copy-start | bytes 1572868
  44.4 18.7 %copy-start.1 = (bf16[3,3,3,128,128]{4,3,2,1,0:T(8,128)(2,1)S(1)}, bf16[3,3,3,128,128]{4,3,2,1,0:T(8,128)(2,1)}, u32[]{:S(2)}) copy-start(bf16[3,3,3,128,128]{4,3,2,1,0:T(8,128)(2,1)} %param.11) | copy-start | bytes 2654212
  60.2 3.4 %copy-start = (bf16[3,3,3,256,128]{4,3,2,1,0:T(8,128)(2,1)S(1)}, bf16[3,3,3,256,128]{4,3,2,1,0:T(8,128)(2,1)}, u32[]{:S(2)}) copy-start(bf16[3,3,3,256,128]{4,3,2,1,0:T(8,128)(2,1)} %param.10) | copy-start | bytes 5308420
  60.6 3.9 %collective-permute-start.1 = (bf16[256,256]{1,0:T(8,128)(2,1)S(1)}, bf16[256,256]{1,0:T(8,128)(2,1)S(1)}, u32[]{:S(2)}, u32[]{:S(2)}) collective-permute-start(bf16[256,256]{1,0:T(8,128)(2,1)S(1)} %shard_map.67.own_ref), channel_id=1, source_target_pairs={{0,16},{16,0},{1,17},{17,1},{2,18},{18,2},{3,19},{19,3},{4,20},{20... | collective-permute-start | bytes 393224 | tf_op jit(solution)/shard_map/ppermute | solution.py:256
  62.8 4.7 %collective-permute-start.2 = (bf16[256,256]{1,0:T(8,128)(2,1)S(1)}, bf16[256,256]{1,0:T(8,128)(2,1)S(1)}, u32[]{:S(2)}, u32[]{:S(2)}) collective-permute-start(bf16[256,256]{1,0:T(8,128)(2,1)S(1)} %shard_map.67.own_ref), channel_id=1, source_target_pairs={{0,240},{16,32},{32,16},{48,64},{64,48},{80,96},{96,80},{112,128},... | collective-permute-start | bytes 393224 | tf_op jit(solution)/shard_map/ppermute | solution.py:255

commit v8 on v7

--- a/solution.py
+++ b/solution.py
@@ -75,10 +75,23 @@
 
 def second_half_kernel(q_ref, kv_ref, sum_ref, top_ref, out_ref):
     keys, vals = halves(kv_ref)
-    edge = jnp.zeros((16, HD), BF)
-    for s in range(2):
-        out_ref[slot(0, s), 0:16] = edge
-        out_ref[slot(7, s), 80:96] = edge
+    row = lax.broadcasted_iota(jnp.int32, (32, 96), 0)
+    col = lax.broadcasted_iota(jnp.int32, (32, 96), 1)
+    picks = [(col == (row // 2) * 8 + row % 2 + 6 * s).astype(F32).astype(BF) for s in range(2)]
+    edge = jnp.zeros((16, HD), F32)
+    done = []
+
+    def finish(n):
+        windows = []
+        for s in range(2):
+            half = slice(64 * s, 64 * s + 64)
+            before = done[n - 1][half][48:64] if n > 0 else edge
+            after = done[n + 1][half][0:16] if n < 7 else edge
+            windows.append(jnp.concatenate([before, done[n][half], after], axis=0))
+        for s in range(2):
+            near = jnp.dot(picks[s], windows[1 - s].astype(BF), preferred_element_type=F32)
+            out_ref[slot(n, s)] = jnp.concatenate([windows[s], near[0:24]], axis=0).astype(BF)
+
     for n in range(8):
         rows = slice(128 * n, 128 * n + 128)
         scores, top = scores_of(queries_of(q_ref, n), keys)
@@ -87,28 +100,18 @@
         weights = jnp.exp2((scores - top) * SCALE).astype(BF)
         kept = jnp.exp2((before - top) * SCALE)
         both = sum_ref[rows] * kept + jnp.dot(weights, vals, preferred_element_type=F32)
-        done = (both[:, 0:HD] / both[:, HD : 2 * HD]).astype(BF)
-        for s in range(2):
-            half = done[64 * s : 64 * s + 64]
-            out_ref[slot(n, s), 16:80] = half
-            if n < 7:
-                out_ref[slot(n + 1, s), 0:16] = half[48:64]
-            if n > 0:
-                out_ref[slot(n - 1, s), 80:96] = half[0:16]
-    row = lax.broadcasted_iota(jnp.int32, (32, 96), 0)
-    col = lax.broadcasted_iota(jnp.int32, (32, 96), 1)
-    for s in range(2):
-        pick = ((col == (row // 2) * 8 + row % 2 + 6 * s) & (row < 24)).astype(F32).astype(BF)
-        for n in range(8):
-            other = out_ref[slot(n, 1 - s), 0:96]
-            out_ref[slot(n, s), 96:128] = jnp.dot(pick, other, preferred_element_type=F32).astype(BF)
+        done.append(both[:, 0:HD] / both[:, HD : 2 * HD])
+        if n > 0:
+            finish(n - 1)
+    finish(7)
 
 
 def project_kernel(a_ref, w_ref, out_ref):
-    rows = [jnp.concatenate([a_ref[slot(h, x)] for h in range(H)], axis=1) for x in range(2)]
-    projected = jnp.dot(jnp.concatenate(rows, axis=0), w_ref[...], preferred_element_type=F32)
-    scale = lax.rsqrt(jnp.mean(projected * projected, axis=1, keepdims=True) + 1e-06)
-    out_ref[...] = (projected * scale).astype(BF)
+    for x in range(2):
+        rows = jnp.concatenate([a_ref[slot(h, x)] for h in range(H)], axis=1)
+        projected = jnp.dot(rows, w_ref[...], preferred_element_type=F32)
+        scale = lax.rsqrt(jnp.mean(projected * projected, axis=1, keepdims=True) + 1e-06)
+        out_ref[x] = (projected * scale).astype(BF)
 
 
 def laid_out(normed):
@@ -116,8 +119,9 @@
     row = lax.broadcasted_iota(jnp.int32, (12, 8, 256), 1)
     slabs = []
     for x in range(2):
-        middle = pltpu.roll(normed[128 * x : 128 * x + 96].astype(F32).reshape(12, 8, 256), 2, 1)
-        near = normed[128 * x + 96 : 128 * x + 128].astype(F32).reshape(4, 8, 256)[0:3]
+        rows = normed[x].astype(F32)
+        middle = pltpu.roll(rows[0:96].reshape(12, 8, 256), 2, 1)
+        near = rows[96:120].reshape(3, 8, 256)
         ends = [pltpu.roll(near, 8 - 2 * k, 1) if k else near for k in range(4)]
         ends = jnp.stack(ends, axis=1).reshape(12, 8, 256)
         upper = jnp.where(row < 2, jnp.where(seq == 1, ends, 0.0), middle)
@@ -249,9 +253,9 @@
     own = lax.all_to_all(jnp.broadcast_to(pair, (8, 256, HD)), "z", 0, 0, tiled=True)
     other = lax.ppermute(own, "core", [(0, 1), (1, 0)])
     summed, top = call(first_half_kernel, [(1024, 2 * HD), (1024, HD)], [F32, F32], [VM, VM])(got, own)
-    attended = call(second_half_kernel, [(16, 128, HD)], [BF], [VM] * 4)(got, other, summed, top)
+    attended = call(second_half_kernel, [(16, 120, HD)], [BF], [VM] * 4)(got, other, summed, top)
     back = lax.all_to_all(attended, ("chip_x", "seq", "low_y"), 0, 0, tiled=True)
-    normed = call(project_kernel, [(256, 256)], [BF], [VM, VM])(back, w_out)
+    normed = call(project_kernel, [(2, 120, 256)], [BF], [VM, VM])(back, w_out)
     far = lax.ppermute(normed, ("z", "core"), [(i, (i - 1 + 2 * (i % 2)) % 16) for i in range(16)])
     near = lax.ppermute(normed, "core", [(0, 1), (1, 0)])
     w1 = conv_first.reshape(27, 256, 128)

time: 69.7 us -> 72.3 us (1.037)
  Pallas kernels: 8.86 us -> 11.9 us
    pallas_call x2, Pallas kernels: 2.24 us -> 5.25 us  [the longest x1 4.86 us: body(): call(second_half_kernel, [(16, 120, HD)], [BF], [VM] * 4)]
where the time goes in v8:
time: 72.3 us; the launch traced here: 72.1 us
  blocking collectives  51.4 us (71%)
  Pallas kernels  11.9 us (16%)
  starting transfers between devices  6.34 us (9%)
  waiting for transfers between devices  2.25 us (3%)
    all_to_all x1, blocking collectives, body(): lax.all_to_all(jnp.broadcast_to(pair, (8, 256, HD)), 'z', 0, 0, tiled=True)  22.4 us
    all_to_all x1, blocking collectives, body(): got = lax.all_to_all(sent, ('chip_x', 'seq', 'low_y'), 0, 0, tiled=True)  15.2 us
    all_to_all x1, blocking collectives, body(): lax.all_to_all(attended, ('chip_x', 'seq', 'low_y'), 0, 0, tiled=True)  13.8 us
    pallas_call x1, Pallas kernels, body(): call(second_half_kernel, [(16, 120, HD)], [BF], [VM] * 4)  4.86 us
    ppermute x1, starting transfers between devices, body(): other = lax.ppermute(own, 'core', [(0, 1), (1, 0)])  4.02 us
    ppermute x1, waiting for transfers between devices, body(): lax.ppermute(normed, ('z', 'core'), [(i, (i - 1 + 2 * (i % 2)) % 16) for...  2.24 us
    ppermute x1, starting transfers between devices, body(): near = lax.ppermute(normed, 'core', [(0, 1), (1, 0)])  2.05 us
    pallas_call x1, Pallas kernels, body(): return final(own_part, done, far, w1, merged)  1.99 us
  transfers between devices with their start and end apart: 3, of which 1 were waited for; matrix products, arithmetic and copies ran while one was open for 0% of the time, Pallas kernels for 5%

profile of v8, /device:TPU:1, one launch (start us, length us, event | category | flops | bytes accessed | tf_op | source)
XLA Modules:
  0.0 72.1 jit_solution(18115027650998989194)
XLA Ops:
  0.0 1.0 %shard_map.64 = bf16[16,80,128]{2,1,0:T(8,128)(2,1)S(1)} custom-call(bf16[2,64,1024]{2,1,0:T(8,128)(2,1)} %bitcast.13, bf16[8,1024]{1,0:T(8,128)(2,1)} %k_hbm.1, bf16[8,1024]{1,0:T(8,128)(2,1)} %v_hbm.1), custom_call_target="tpu_custom_call" | custom-call | flops 1000000 | bytes 10000 | tf_op jit(solution)/shard_map/pallas_call | solution.py:239
  1.0 15.2 %all_to_all.15.q_ref = bf16[16,80,128]{2,1,0:T(8,128)(2,1)S(1)} all-to-all(bf16[16,80,128]{2,1,0:T(8,128)(2,1)S(1)} %shard_map.64), channel_id=1, replica_groups=mesh['z'=8,'core'=2,'chip_x'=4,'low_y'=2,'seq'=2] {'chip_x','seq','low_y'}, dimensions={0} | all-to-all | bytes 655360 | tf_op jit(solution)/shard_map/all_to_all | solution.py:251
  16.3 0.1 broadcast_in_dim.8
  16.3 22.4 %all_to_all.16.kv_ref = bf16[8,256,128]{2,1,0:T(8,128)(2,1)S(1)} all-to-all(bf16[8,256,128]{2,1,0:T(8,128)(2,1)S(1)} %broadcast_in_dim.8), channel_id=1, replica_groups=mesh['z'=8,'core'=2,'chip_x'=4,'low_y'=2,'seq'=2] {'z'}, dimensions={0} | all-to-all | bytes 1048576 | tf_op jit(solution)/shard_map/all_to_all | solution.py:253
  38.8 4.0 %collective-permute-start = (bf16[8,256,128]{2,1,0:T(8,128)(2,1)S(1)}, bf16[8,256,128]{2,1,0:T(8,128)(2,1)S(1)}, u32[]{:S(2)}, u32[]{:S(2)}) collective-permute-start(bf16[8,256,128]{2,1,0:T(8,128)(2,1)S(1)} %all_to_all.16.kv_ref), channel_id=1, source_target_pairs={{0,16},{16,0},{1,17},{17,1},{2,18},{18,2},{3,19},{19,3},{4,20},{20... | collective-permute-start | bytes 1572872 | tf_op jit(solution)/shard_map/ppermute | solution.py:254
  42.8 1.6 %shard_map.65 = (f32[1024,256]{1,0:T(8,128)S(1)}, f32[1024,128]{1,0:T(8,128)S(1)}) custom-call(bf16[16,80,128]{2,1,0:T(8,128)(2,1)S(1)} %all_to_all.15.q_ref, bf16[8,256,128]{2,1,0:T(8,128)(2,1)S(1)} %all_to_all.16.kv_ref), custom_call_target="tpu_custom_call" | custom-call | flops 1000000 | bytes 10000 | tf_op jit(solution)/shard_map/pallas_call | solution.py:255
  44.4 0.0 copy-start.2
  44.4 0.0 collective-permute-done.kv_ref
  44.4 0.0 copy-start.1
  44.4 4.9 %shard_map.66 = bf16[16,120,128]{2,1,0:T(8,128)(2,1)S(1)} custom-call(bf16[16,80,128]{2,1,0:T(8,128)(2,1)S(1)} %all_to_all.15.q_ref, bf16[8,256,128]{2,1,0:T(8,128)(2,1)S(1)} %collective-permute-done.kv_ref, f32[1024,256]{1,0:T(8,128)S(1)} %get-tuple-element.7.sum_ref, f32[1024,128]{1,0:T(8,128)S(1)} %get-tuple-element.8.top_ref), custom_call_target="tpu_custom_call" | custom-call | flops 1000000 | bytes 10000 | tf_op jit(solution)/shard_map/pallas_call | solution.py:256
  49.3 13.8 %all_to_all.17.a_ref = bf16[16,120,128]{2,1,0:T(8,128)(2,1)S(1)} all-to-all(bf16[16,120,128]{2,1,0:T(8,128)(2,1)S(1)} %shard_map.66), channel_id=1, replica_groups=mesh['z'=8,'core'=2,'chip_x'=4,'low_y'=2,'seq'=2] {'chip_x','seq','low_y'}, dimensions={0} | all-to-all | bytes 983040 | tf_op jit(solution)/shard_map/all_to_all | solution.py:257
  63.0 0.0 copy-done.2
  63.0 0.0 copy-start
  63.0 0.4 shard_map.67.own_ref
  63.4 2.0 %collective-permute-start.1 = (bf16[2,120,256]{2,1,0:T(8,128)(2,1)S(1)}, bf16[2,120,256]{2,1,0:T(8,128)(2,1)S(1)}, u32[]{:S(2)}, u32[]{:S(2)}) collective-permute-start(bf16[2,120,256]{2,1,0:T(8,128)(2,1)S(1)} %shard_map.67.own_ref), channel_id=1, source_target_pairs={{0,16},{16,0},{1,17},{17,1},{2,18},{18,2},{3,19},{19,3},{4,20},{20... | collective-permute-start | bytes 368648 | tf_op jit(solution)/shard_map/ppermute | solution.py:260
  65.5 0.3 collective-permute-start.2
  65.7 0.0 copy-done.1
  65.7 0.5 shard_map.70.w2_ref
  66.3 0.0 copy-done
  66.3 0.9 %shard_map.68.own_ref = f32[4,160,384]{2,1,0:T(8,128)S(1)} custom-call(bf16[2,120,256]{2,1,0:T(8,128)(2,1)S(1)} %shard_map.67.own_ref, bf16[27,256,128]{2,1,0:T(8,128)(2,1)S(1)} %bitcast.8), custom_call_target="tpu_custom_call" | custom-call | flops 1000000 | bytes 10000 | tf_op jit(solution)/shard_map/pallas_call | solution.py:263
  67.2 0.0 collective-permute-done.1.near_ref
  67.2 0.6 shard_map.69.done_ref
  67.8 2.2 %collective-permute-done.2.far_ref = bf16[2,120,256]{2,1,0:T(8,128)(2,1)S(1)} collective-permute-done((bf16[2,120,256]{2,1,0:T(8,128)(2,1)S(1)}, bf16[2,120,256]{2,1,0:T(8,128)(2,1)S(1)}, u32[]{:S(2)}, u32[]{:S(2)}) %collective-permute-start.2) | collective-permute-done | bytes 122912 | tf_op jit(solution)/shard_map/ppermute | solution.py:259
  70.1 2.0 %shard_map.71 = bf16[4,16,16,128]{3,2,1,0:T(8,128)(2,1)} custom-call(f32[4,160,384]{2,1,0:T(8,128)S(1)} %shard_map.68.own_ref, bf16[2,160,128]{2,1,0:T(8,128)(2,1)S(1)} %shard_map.69.done_ref, bf16[2,120,256]{2,1,0:T(8,128)(2,1)S(1)} %collective-permute-done.2.far_ref, bf16[27,256,128]{2,1,0:T(8,128)(2,1)S(1)} %bitcast.10, ...), custom_call_target="tpu_custom_call" | custom-call | flops 1000000 | bytes 10000 | tf_op jit(solution)/shard_map/pallas_call | solution.py:272
  (2 shorter events, 0.0 us)
Async XLA Ops:
  38.8 5.6 %collective-permute-start = (bf16[8,256,128]{2,1,0:T(8,128)(2,1)S(1)}, bf16[8,256,128]{2,1,0:T(8,128)(2,1)S(1)}, u32[]{:S(2)}, u32[]{:S(2)}) collective-permute-start(bf16[8,256,128]{2,1,0:T(8,128)(2,1)S(1)} %all_to_all.16.kv_ref), channel_id=1, source_target_pairs={{0,16},{16,0},{1,17},{17,1},{2,18},{18,2},{3,19},{19,3},{4,20},{20... | collective-permute-start | bytes 1572872 | tf_op jit(solution)/shard_map/ppermute | solution.py:254
  44.4 18.6 %copy-start.2 = (bf16[1024,256]{1,0:T(8,128)(2,1)S(1)}, bf16[1024,256]{1,0:T(8,128)(2,1)}, u32[]{:S(2)}) copy-start(bf16[1024,256]{1,0:T(8,128)(2,1)} %w_ref.1) | copy-start | bytes 1572868
  44.4 21.4 %copy-start.1 = (bf16[3,3,3,128,128]{4,3,2,1,0:T(8,128)(2,1)S(1)}, bf16[3,3,3,128,128]{4,3,2,1,0:T(8,128)(2,1)}, u32[]{:S(2)}) copy-start(bf16[3,3,3,128,128]{4,3,2,1,0:T(8,128)(2,1)} %param.11) | copy-start | bytes 2654212
  63.0 3.3 %copy-start = (bf16[3,3,3,256,128]{4,3,2,1,0:T(8,128)(2,1)S(1)}, bf16[3,3,3,256,128]{4,3,2,1,0:T(8,128)(2,1)}, u32[]{:S(2)}) copy-start(bf16[3,3,3,256,128]{4,3,2,1,0:T(8,128)(2,1)} %param.10) | copy-start | bytes 5308420
  63.4 3.8 %collective-permute-start.1 = (bf16[2,120,256]{2,1,0:T(8,128)(2,1)S(1)}, bf16[2,120,256]{2,1,0:T(8,128)(2,1)S(1)}, u32[]{:S(2)}, u32[]{:S(2)}) collective-permute-start(bf16[2,120,256]{2,1,0:T(8,128)(2,1)S(1)} %shard_map.67.own_ref), channel_id=1, source_target_pairs={{0,16},{16,0},{1,17},{17,1},{2,18},{18,2},{3,19},{19,3},{4,20},{20... | collective-permute-start | bytes 368648 | tf_op jit(solution)/shard_map/ppermute | solution.py:260
  65.5 4.6 %collective-permute-start.2 = (bf16[2,120,256]{2,1,0:T(8,128)(2,1)S(1)}, bf16[2,120,256]{2,1,0:T(8,128)(2,1)S(1)}, u32[]{:S(2)}, u32[]{:S(2)}) collective-permute-start(bf16[2,120,256]{2,1,0:T(8,128)(2,1)S(1)} %shard_map.67.own_ref), channel_id=1, source_target_pairs={{0,240},{16,32},{32,16},{48,64},{64,48},{80,96},{96,80},{112,128},... | collective-permute-start | bytes 368648 | tf_op jit(solution)/shard_map/ppermute | solution.py:259

commit v9 on v8

--- a/solution.py
+++ b/solution.py
@@ -73,25 +73,12 @@
         top_out[rows] = jnp.broadcast_to(top, (128, HD))
 
 
-def second_half_kernel(q_ref, kv_ref, sum_ref, top_ref, out_ref):
+def second_half_kernel(q_ref, kv_ref, sum_ref, top_ref, out_ref, windows):
     keys, vals = halves(kv_ref)
-    row = lax.broadcasted_iota(jnp.int32, (32, 96), 0)
-    col = lax.broadcasted_iota(jnp.int32, (32, 96), 1)
-    picks = [(col == (row // 2) * 8 + row % 2 + 6 * s).astype(F32).astype(BF) for s in range(2)]
     edge = jnp.zeros((16, HD), F32)
-    done = []
-
-    def finish(n):
-        windows = []
-        for s in range(2):
-            half = slice(64 * s, 64 * s + 64)
-            before = done[n - 1][half][48:64] if n > 0 else edge
-            after = done[n + 1][half][0:16] if n < 7 else edge
-            windows.append(jnp.concatenate([before, done[n][half], after], axis=0))
-        for s in range(2):
-            near = jnp.dot(picks[s], windows[1 - s].astype(BF), preferred_element_type=F32)
-            out_ref[slot(n, s)] = jnp.concatenate([windows[s], near[0:24]], axis=0).astype(BF)
-
+    for s in range(2):
+        windows[slot(0, s), 0:16] = edge
+        windows[slot(7, s), 80:96] = edge
     for n in range(8):
         rows = slice(128 * n, 128 * n + 128)
         scores, top = scores_of(queries_of(q_ref, n), keys)
@@ -100,10 +87,21 @@
         weights = jnp.exp2((scores - top) * SCALE).astype(BF)
         kept = jnp.exp2((before - top) * SCALE)
         both = sum_ref[rows] * kept + jnp.dot(weights, vals, preferred_element_type=F32)
-        done.append(both[:, 0:HD] / both[:, HD : 2 * HD])
-        if n > 0:
-            finish(n - 1)
-    finish(7)
+        done = both[:, 0:HD] / both[:, HD : 2 * HD]
+        for s in range(2):
+            half = done[64 * s : 64 * s + 64]
+            windows[slot(n, s), 16:80] = half
+            if n < 7:
+                windows[slot(n + 1, s), 0:16] = half[48:64]
+            if n > 0:
+                windows[slot(n - 1, s), 80:96] = half[0:16]
+    row = lax.broadcasted_iota(jnp.int32, (32, 96), 0)
+    col = lax.broadcasted_iota(jnp.int32, (32, 96), 1)
+    for s in range(2):
+        pick = (col == (row // 2) * 8 + row % 2 + 6 * s).astype(F32).astype(BF)
+        for n in range(8):
+            near = jnp.dot(pick, windows[slot(n, 1 - s)].astype(BF), preferred_element_type=F32)
+            out_ref[slot(n, s)] = jnp.concatenate([windows[slot(n, s)], near[0:24]], axis=0).astype(BF)
 
 
 def project_kernel(a_ref, w_ref, out_ref):
@@ -253,7 +251,7 @@
     own = lax.all_to_all(jnp.broadcast_to(pair, (8, 256, HD)), "z", 0, 0, tiled=True)
     other = lax.ppermute(own, "core", [(0, 1), (1, 0)])
     summed, top = call(first_half_kernel, [(1024, 2 * HD), (1024, HD)], [F32, F32], [VM, VM])(got, own)
-    attended = call(second_half_kernel, [(16, 120, HD)], [BF], [VM] * 4)(got, other, summed, top)
+    attended = call(second_half_kernel, [(16, 120, HD)], [BF], [VM] * 4, [pltpu.VMEM((16, 96, HD), F32)])(got, other, summed, top)
     back = lax.all_to_all(attended, ("chip_x", "seq", "low_y"), 0, 0, tiled=True)
     normed = call(project_kernel, [(2, 120, 256)], [BF], [VM, VM])(back, w_out)
     far = lax.ppermute(normed, ("z", "core"), [(i, (i - 1 + 2 * (i % 2)) % 16) for i in range(16)])

time: 72.3 us -> 69.2 us (0.957)
  Pallas kernels: 11.9 us -> 8.85 us
    pallas_call x1, Pallas kernels: 4.86 us -> 1.82 us  [body(): call(second_half_kernel, [(16, 120, HD)], [BF], [VM] * 4, [pltpu.VMEM((16...]
where the time goes in v9:
time: 69.2 us; the launch traced here: 69 us
  blocking collectives  51.4 us (74%)
  Pallas kernels  8.85 us (13%)
  starting transfers between devices  6.34 us (9%)
  waiting for transfers between devices  2.25 us (3%)
    all_to_all x1, blocking collectives, body(): lax.all_to_all(jnp.broadcast_to(pair, (8, 256, HD)), 'z', 0, 0, tiled=True)  22.4 us
    all_to_all x1, blocking collectives, body(): got = lax.all_to_all(sent, ('chip_x', 'seq', 'low_y'), 0, 0, tiled=True)  15.2 us
    all_to_all x1, blocking collectives, body(): lax.all_to_all(attended, ('chip_x', 'seq', 'low_y'), 0, 0, tiled=True)  13.8 us
    ppermute x1, starting transfers between devices, body(): other = lax.ppermute(own, 'core', [(0, 1), (1, 0)])  4.02 us
    ppermute x1, waiting for transfers between devices, body(): lax.ppermute(normed, ('z', 'core'), [(i, (i - 1 + 2 * (i % 2)) % 16) for...  2.24 us
    ppermute x1, starting transfers between devices, body(): near = lax.ppermute(normed, 'core', [(0, 1), (1, 0)])  2.04 us
    pallas_call x1, Pallas kernels, body(): return final(own_part, done, far, w1, merged)  1.98 us
    pallas_call x1, Pallas kernels, body(): call(second_half_kernel, [(16, 120, HD)], [BF], [VM] * 4, [pltpu.VMEM((16...  1.82 us
  transfers between devices with their start and end apart: 3, of which 1 were waited for; matrix products, arithmetic and copies ran while one was open for 0% of the time, Pallas kernels for 5%

profile of v9, /device:TPU:1, one launch (start us, length us, event | category | flops | bytes accessed | tf_op | source)
XLA Modules:
  0.0 69.0 jit_solution(7675939993460060273)
XLA Ops:
  0.0 1.0 %shard_map.64 = bf16[16,80,128]{2,1,0:T(8,128)(2,1)S(1)} custom-call(bf16[2,64,1024]{2,1,0:T(8,128)(2,1)} %bitcast.13, bf16[8,1024]{1,0:T(8,128)(2,1)} %k_hbm.1, bf16[8,1024]{1,0:T(8,128)(2,1)} %v_hbm.1), custom_call_target="tpu_custom_call" | custom-call | flops 1000000 | bytes 10000 | tf_op jit(solution)/shard_map/pallas_call | solution.py:237
  1.0 15.2 %all_to_all.15.q_ref = bf16[16,80,128]{2,1,0:T(8,128)(2,1)S(1)} all-to-all(bf16[16,80,128]{2,1,0:T(8,128)(2,1)S(1)} %shard_map.64), channel_id=1, replica_groups=mesh['z'=8,'core'=2,'chip_x'=4,'low_y'=2,'seq'=2] {'chip_x','seq','low_y'}, dimensions={0} | all-to-all | bytes 655360 | tf_op jit(solution)/shard_map/all_to_all | solution.py:249
  16.3 0.1 broadcast_in_dim.8
  16.3 22.4 %all_to_all.16.kv_ref = bf16[8,256,128]{2,1,0:T(8,128)(2,1)S(1)} all-to-all(bf16[8,256,128]{2,1,0:T(8,128)(2,1)S(1)} %broadcast_in_dim.8), channel_id=1, replica_groups=mesh['z'=8,'core'=2,'chip_x'=4,'low_y'=2,'seq'=2] {'z'}, dimensions={0} | all-to-all | bytes 1048576 | tf_op jit(solution)/shard_map/all_to_all | solution.py:251
  38.8 4.0 %collective-permute-start = (bf16[8,256,128]{2,1,0:T(8,128)(2,1)S(1)}, bf16[8,256,128]{2,1,0:T(8,128)(2,1)S(1)}, u32[]{:S(2)}, u32[]{:S(2)}) collective-permute-start(bf16[8,256,128]{2,1,0:T(8,128)(2,1)S(1)} %all_to_all.16.kv_ref), channel_id=1, source_target_pairs={{0,16},{16,0},{1,17},{17,1},{2,18},{18,2},{3,19},{19,3},{4,20},{20... | collective-permute-start | bytes 1572872 | tf_op jit(solution)/shard_map/ppermute | solution.py:252
  42.8 1.6 %shard_map.65 = (f32[1024,256]{1,0:T(8,128)S(1)}, f32[1024,128]{1,0:T(8,128)S(1)}) custom-call(bf16[16,80,128]{2,1,0:T(8,128)(2,1)S(1)} %all_to_all.15.q_ref, bf16[8,256,128]{2,1,0:T(8,128)(2,1)S(1)} %all_to_all.16.kv_ref), custom_call_target="tpu_custom_call" | custom-call | flops 1000000 | bytes 10000 | tf_op jit(solution)/shard_map/pallas_call | solution.py:253
  44.4 0.0 copy-start.2
  44.4 0.0 collective-permute-done.kv_ref
  44.4 0.0 copy-start.1
  44.4 1.8 %shard_map.66 = bf16[16,120,128]{2,1,0:T(8,128)(2,1)S(1)} custom-call(bf16[16,80,128]{2,1,0:T(8,128)(2,1)S(1)} %all_to_all.15.q_ref, bf16[8,256,128]{2,1,0:T(8,128)(2,1)S(1)} %collective-permute-done.kv_ref, f32[1024,256]{1,0:T(8,128)S(1)} %get-tuple-element.7.sum_ref, f32[1024,128]{1,0:T(8,128)S(1)} %get-tuple-element.8.top_ref), custom_call_target="tpu_custom_call" | custom-call | flops 1000000 | bytes 10000 | tf_op jit(solution)/shard_map/pallas_call | solution.py:254
  46.2 13.8 %all_to_all.17.a_ref = bf16[16,120,128]{2,1,0:T(8,128)(2,1)S(1)} all-to-all(bf16[16,120,128]{2,1,0:T(8,128)(2,1)S(1)} %shard_map.66), channel_id=1, replica_groups=mesh['z'=8,'core'=2,'chip_x'=4,'low_y'=2,'seq'=2] {'chip_x','seq','low_y'}, dimensions={0} | all-to-all | bytes 983040 | tf_op jit(solution)/shard_map/all_to_all | solution.py:255
  60.0 0.0 copy-done.2
  60.0 0.0 copy-start
  60.0 0.4 shard_map.67.own_ref
  60.4 2.0 %collective-permute-start.1 = (bf16[2,120,256]{2,1,0:T(8,128)(2,1)S(1)}, bf16[2,120,256]{2,1,0:T(8,128)(2,1)S(1)}, u32[]{:S(2)}, u32[]{:S(2)}) collective-permute-start(bf16[2,120,256]{2,1,0:T(8,128)(2,1)S(1)} %shard_map.67.own_ref), channel_id=1, source_target_pairs={{0,16},{16,0},{1,17},{17,1},{2,18},{18,2},{3,19},{19,3},{4,20},{20... | collective-permute-start | bytes 368648 | tf_op jit(solution)/shard_map/ppermute | solution.py:258
  62.4 0.3 collective-permute-start.2
  62.7 0.0 copy-done.1
  62.7 0.5 shard_map.70.w2_ref
  63.2 0.0 copy-done
  63.2 0.9 %shard_map.68.own_ref = f32[4,160,384]{2,1,0:T(8,128)S(1)} custom-call(bf16[2,120,256]{2,1,0:T(8,128)(2,1)S(1)} %shard_map.67.own_ref, bf16[27,256,128]{2,1,0:T(8,128)(2,1)S(1)} %bitcast.8), custom_call_target="tpu_custom_call" | custom-call | flops 1000000 | bytes 10000 | tf_op jit(solution)/shard_map/pallas_call | solution.py:261
  64.2 0.0 collective-permute-done.1.near_ref
  64.2 0.6 shard_map.69.done_ref
  64.8 2.2 %collective-permute-done.2.far_ref = bf16[2,120,256]{2,1,0:T(8,128)(2,1)S(1)} collective-permute-done((bf16[2,120,256]{2,1,0:T(8,128)(2,1)S(1)}, bf16[2,120,256]{2,1,0:T(8,128)(2,1)S(1)}, u32[]{:S(2)}, u32[]{:S(2)}) %collective-permute-start.2) | collective-permute-done | bytes 122912 | tf_op jit(solution)/shard_map/ppermute | solution.py:257
  67.0 2.0 %shard_map.71 = bf16[4,16,16,128]{3,2,1,0:T(8,128)(2,1)} custom-call(f32[4,160,384]{2,1,0:T(8,128)S(1)} %shard_map.68.own_ref, bf16[2,160,128]{2,1,0:T(8,128)(2,1)S(1)} %shard_map.69.done_ref, bf16[2,120,256]{2,1,0:T(8,128)(2,1)S(1)} %collective-permute-done.2.far_ref, bf16[27,256,128]{2,1,0:T(8,128)(2,1)S(1)} %bitcast.10, ...), custom_call_target="tpu_custom_call" | custom-call | flops 1000000 | bytes 10000 | tf_op jit(solution)/shard_map/pallas_call | solution.py:270
  (2 shorter events, 0.0 us)
Async XLA Ops:
  38.8 5.6 %collective-permute-start = (bf16[8,256,128]{2,1,0:T(8,128)(2,1)S(1)}, bf16[8,256,128]{2,1,0:T(8,128)(2,1)S(1)}, u32[]{:S(2)}, u32[]{:S(2)}) collective-permute-start(bf16[8,256,128]{2,1,0:T(8,128)(2,1)S(1)} %all_to_all.16.kv_ref), channel_id=1, source_target_pairs={{0,16},{16,0},{1,17},{17,1},{2,18},{18,2},{3,19},{19,3},{4,20},{20... | collective-permute-start | bytes 1572872 | tf_op jit(solution)/shard_map/ppermute | solution.py:252
  44.4 15.6 %copy-start.2 = (bf16[1024,256]{1,0:T(8,128)(2,1)S(1)}, bf16[1024,256]{1,0:T(8,128)(2,1)}, u32[]{:S(2)}) copy-start(bf16[1024,256]{1,0:T(8,128)(2,1)} %w_ref.1) | copy-start | bytes 1572868
  44.4 18.3 %copy-start.1 = (bf16[3,3,3,128,128]{4,3,2,1,0:T(8,128)(2,1)S(1)}, bf16[3,3,3,128,128]{4,3,2,1,0:T(8,128)(2,1)}, u32[]{:S(2)}) copy-start(bf16[3,3,3,128,128]{4,3,2,1,0:T(8,128)(2,1)} %param.11) | copy-start | bytes 2654212
  60.0 3.3 %copy-start = (bf16[3,3,3,256,128]{4,3,2,1,0:T(8,128)(2,1)S(1)}, bf16[3,3,3,256,128]{4,3,2,1,0:T(8,128)(2,1)}, u32[]{:S(2)}) copy-start(bf16[3,3,3,256,128]{4,3,2,1,0:T(8,128)(2,1)} %param.10) | copy-start | bytes 5308420
  60.4 3.8 %collective-permute-start.1 = (bf16[2,120,256]{2,1,0:T(8,128)(2,1)S(1)}, bf16[2,120,256]{2,1,0:T(8,128)(2,1)S(1)}, u32[]{:S(2)}, u32[]{:S(2)}) collective-permute-start(bf16[2,120,256]{2,1,0:T(8,128)(2,1)S(1)} %shard_map.67.own_ref), channel_id=1, source_target_pairs={{0,16},{16,0},{1,17},{17,1},{2,18},{18,2},{3,19},{19,3},{4,20},{20... | collective-permute-start | bytes 368648 | tf_op jit(solution)/shard_map/ppermute | solution.py:258
  62.4 4.6 %collective-permute-start.2 = (bf16[2,120,256]{2,1,0:T(8,128)(2,1)S(1)}, bf16[2,120,256]{2,1,0:T(8,128)(2,1)S(1)}, u32[]{:S(2)}, u32[]{:S(2)}) collective-permute-start(bf16[2,120,256]{2,1,0:T(8,128)(2,1)S(1)} %shard_map.67.own_ref), channel_id=1, source_target_pairs={{0,240},{16,32},{32,16},{48,64},{64,48},{80,96},{96,80},{112,128},... | collective-permute-start | bytes 368648 | tf_op jit(solution)/shard_map/ppermute | solution.py:257

commit v10 on v9

--- a/solution.py
+++ b/solution.py
@@ -32,26 +32,36 @@
     return 4 * (tile // 2) + 2 * half + tile % 2
 
 
-def pack_kernel(q_hbm, k_hbm, v_hbm, out_ref, q_ref, k_ref, v_ref, sems):
+def spread_kernel(q_hbm, k_hbm, v_hbm, out_ref, q_ref, k_ref, v_ref, sems):
     copies = [
         pltpu.make_async_copy(src, dst, sems.at[i])
-        for i, (src, dst) in enumerate(((q_hbm, q_ref), (k_hbm, k_ref), (v_hbm, v_ref)))
+        for i, (src, dst) in enumerate(((k_hbm, k_ref), (v_hbm, v_ref), (q_hbm, q_ref)))
     ]
     for copy in copies:
         copy.start()
-    for copy in copies:
+    for copy in copies[0:2]:
         copy.wait()
+    pair = jnp.concatenate([k_ref[...].astype(F32), v_ref[...].astype(F32)], axis=0).astype(BF)
+    for z in range(8):
+        out_ref[z] = pair
+    copies[2].wait()
+
+
+def pack_kernel(q_ref, kv_ref, out_ref):
     for h in range(H):
         cols = slice(h * HD, (h + 1) * HD)
-        pair = jnp.concatenate([k_ref[:, cols].astype(F32), v_ref[:, cols].astype(F32)], axis=0).astype(BF)
+        pairs = [kv_ref[z, :, cols].astype(F32) for z in range(8)]
+        keys = jnp.concatenate([pair[0:8] for pair in pairs], axis=0).astype(BF)
+        vals = jnp.concatenate([pair[8:16] for pair in pairs], axis=0).astype(BF)
         for s in range(2):
             out_ref[slot(h, s), 0:64] = q_ref[s, :, cols]
-            out_ref[slot(h, s), 64:80] = pair
+            out_ref[slot(h, s), 64:128] = keys
+            out_ref[slot(h, s), 128:192] = vals
 
 
 def halves(ref):
-    keys = ref[:, 0:128].reshape(1024, HD)
-    return keys, jnp.concatenate([ref[:, 128:256].reshape(1024, HD), jnp.ones((1024, HD), BF)], axis=1)
+    keys = ref[:, 64:128].reshape(1024, HD)
+    return keys, jnp.concatenate([ref[:, 128:192].reshape(1024, HD), jnp.ones((1024, HD), BF)], axis=1)
 
 
 def scores_of(q, keys):
@@ -63,8 +73,8 @@
     return jnp.concatenate([q_ref[slot(n, 0), 0:64], q_ref[slot(n, 1), 0:64]], axis=0)
 
 
-def first_half_kernel(q_ref, kv_ref, sum_out, top_out):
-    keys, vals = halves(kv_ref)
+def first_half_kernel(q_ref, sum_out, top_out):
+    keys, vals = halves(q_ref)
     for n in range(8):
         rows = slice(128 * n, 128 * n + 128)
         scores, top = scores_of(queries_of(q_ref, n), keys)
@@ -234,23 +244,15 @@
 
 
 def body(queries, keys, values, w_out, conv_first, conv_second):
-    sent = call(
-        pack_kernel,
-        [(16, 80, HD)],
-        [BF],
-        [HB] * 3,
-        [
-            pltpu.VMEM((2, 64, H * HD), BF),
-            pltpu.VMEM((8, H * HD), BF),
-            pltpu.VMEM((8, H * HD), BF),
-            pltpu.SemaphoreType.DMA((3,)),
-        ],
-    )(*(pltpu.with_memory_space_constraint(a, pltpu.HBM) for a in (queries.reshape(2, 64, H * HD), keys, values)))
+    rows = queries.reshape(2, 64, H * HD)
+    in_hbm = [pltpu.with_memory_space_constraint(array, pltpu.HBM) for array in (rows, keys, values)]
+    scratch = [pltpu.VMEM((8, H * HD), BF), pltpu.VMEM((8, H * HD), BF), pltpu.SemaphoreType.DMA((3,))]
+    spread, rows = call(spread_kernel, [(8, 16, H * HD), rows.shape], [BF, BF], [HB] * 3, scratch)(*in_hbm)
+    tokens = lax.all_to_all(spread, "z", 0, 0, tiled=True)
+    sent = call(pack_kernel, [(16, 192, HD)], [BF], [VM] * 2)(rows, tokens)
     got = lax.all_to_all(sent, ("chip_x", "seq", "low_y"), 0, 0, tiled=True)
-    pair = got[:, 64:80].reshape(16, 2, 8, HD).transpose(1, 0, 2, 3).reshape(1, 256, HD)
-    own = lax.all_to_all(jnp.broadcast_to(pair, (8, 256, HD)), "z", 0, 0, tiled=True)
-    other = lax.ppermute(own, "core", [(0, 1), (1, 0)])
-    summed, top = call(first_half_kernel, [(1024, 2 * HD), (1024, HD)], [F32, F32], [VM, VM])(got, own)
+    other = lax.ppermute(got, "core", [(0, 1), (1, 0)])
+    summed, top = call(first_half_kernel, [(1024, 2 * HD), (1024, HD)], [F32, F32], [VM])(got)
     attended = call(second_half_kernel, [(16, 120, HD)], [BF], [VM] * 4, [pltpu.VMEM((16, 96, HD), F32)])(got, other, summed, top)
     back = lax.all_to_all(attended, ("chip_x", "seq", "low_y"), 0, 0, tiled=True)
     normed = call(project_kernel, [(2, 120, 256)], [BF], [VM, VM])(back, w_out)

time: 69.2 us -> 68.3 us (0.987)
  blocking collectives: 51.4 us -> 49.9 us
    all_to_all x1, blocking collectives: 22.4 us -> 19.2 us  [body(): tokens = lax.all_to_all(spread, 'z', 0, 0, tiled=True)]
    all_to_all x1, blocking collectives: 15.2 us -> 17.4 us  [body(): got = lax.all_to_all(sent, ('chip_x', 'seq', 'low_y'), 0, 0, tiled=True)]
    pallas_call x2 -> x3, Pallas kernels: 2.61 us -> 2.7 us  [the longest x1 1.58 us: body(): call(first_half_kernel, [(1024, 2 * HD), (1024, HD)], [F32, F32], [VM])(got)]
  transfers between devices with their start and end apart: 3 -> 3, of which waited for: 1 -> 2; matrix products, arithmetic and copies ran while one was open for 0% -> 0% of each run, Pallas kernels for 5% -> 5%
where the time goes in v10:
time: 68.3 us; the launch traced here: 68 us
  blocking collectives  49.9 us (73%)
  Pallas kernels  8.95 us (13%)
  starting transfers between devices  6.29 us (9%)
  waiting for transfers between devices  2.84 us (4%)
    all_to_all x1, blocking collectives, body(): tokens = lax.all_to_all(spread, 'z', 0, 0, tiled=True)  19.2 us
    all_to_all x1, blocking collectives, body(): got = lax.all_to_all(sent, ('chip_x', 'seq', 'low_y'), 0, 0, tiled=True)  17.4 us
    all_to_all x1, blocking collectives, body(): lax.all_to_all(attended, ('chip_x', 'seq', 'low_y'), 0, 0, tiled=True)  13.2 us
    ppermute x1, starting transfers between devices, body(): other = lax.ppermute(got, 'core', [(0, 1), (1, 0)])  4.19 us
    ppermute x1, waiting for transfers between devices, body(): lax.ppermute(normed, ('z', 'core'), [(i, (i - 1 + 2 * (i % 2)) % 16) for...  2.51 us
    ppermute x1, starting transfers between devices, body(): near = lax.ppermute(normed, 'core', [(0, 1), (1, 0)])  2.09 us
    pallas_call x1, Pallas kernels, body(): return final(own_part, done, far, w1, merged)  1.99 us
    pallas_call x1, Pallas kernels, body(): call(second_half_kernel, [(16, 120, HD)], [BF], [VM] * 4, [pltpu.VMEM((16...  1.82 us
  transfers between devices with their start and end apart: 3, of which 2 were waited for; matrix products, arithmetic and copies ran while one was open for 0% of the time, Pallas kernels for 5%

profile of v10, /device:TPU:1, one launch (start us, length us, event | category | flops | bytes accessed | tf_op | source)
XLA Modules:
  0.0 68.0 jit_solution(5209876394423296604)
XLA Ops:
  0.0 1.0 %shard_map.64 = (bf16[8,16,1024]{2,1,0:T(8,128)(2,1)S(1)}, bf16[2,64,1024]{2,1,0:T(8,128)(2,1)S(1)}) custom-call(bf16[2,64,1024]{2,1,0:T(8,128)(2,1)} %bitcast.7, bf16[8,1024]{1,0:T(8,128)(2,1)} %k_hbm.1, bf16[8,1024]{1,0:T(8,128)(2,1)} %v_hbm.1), custom_call_target="tpu_custom_call" | custom-call | flops 1000000 | bytes 10000 | tf_op jit(solution)/shard_map/pallas_call | solution.py:250
  1.0 19.2 %all_to_all.15.kv_ref = bf16[8,16,1024]{2,1,0:T(8,128)(2,1)S(1)} all-to-all(bf16[8,16,1024]{2,1,0:T(8,128)(2,1)S(1)} %get-tuple-element.10), channel_id=1, replica_groups=mesh['z'=8,'core'=2,'chip_x'=4,'low_y'=2,'seq'=2] {'z'}, dimensions={0} | all-to-all | bytes 524288 | tf_op jit(solution)/shard_map/all_to_all | solution.py:251
  20.2 0.1 shard_map.65
  20.3 17.4 %all_to_all.16.q_ref = bf16[16,192,128]{2,1,0:T(8,128)(2,1)S(1)} all-to-all(bf16[16,192,128]{2,1,0:T(8,128)(2,1)S(1)} %shard_map.65), channel_id=1, replica_groups=mesh['z'=8,'core'=2,'chip_x'=4,'low_y'=2,'seq'=2] {'chip_x','seq','low_y'}, dimensions={0} | all-to-all | bytes 1572864 | tf_op jit(solution)/shard_map/all_to_all | solution.py:253
  37.8 4.2 %collective-permute-start = (bf16[16,192,128]{2,1,0:T(8,128)(2,1)S(1)}, bf16[16,192,128]{2,1,0:T(8,128)(2,1)S(1)}, u32[]{:S(2)}, u32[]{:S(2)}) collective-permute-start(bf16[16,192,128]{2,1,0:T(8,128)(2,1)S(1)} %all_to_all.16.q_ref), channel_id=1, source_target_pairs={{0,16},{16,0},{1,17},{17,1},{2,18},{18,2},{3,19},{19,3},{4,20},{20... | collective-permute-start | bytes 2359304 | tf_op jit(solution)/shard_map/ppermute | solution.py:254
  42.0 1.6 %shard_map.66 = (f32[1024,256]{1,0:T(8,128)S(1)}, f32[1024,128]{1,0:T(8,128)S(1)}) custom-call(bf16[16,192,128]{2,1,0:T(8,128)(2,1)S(1)} %all_to_all.16.q_ref), custom_call_target="tpu_custom_call" | custom-call | flops 1000000 | bytes 10000 | tf_op jit(solution)/shard_map/pallas_call | solution.py:255
  43.5 0.3 collective-permute-done.kv_ref
  43.9 0.0 copy-start.2
  43.9 0.0 copy-start.1
  43.9 1.8 %shard_map.67 = bf16[16,120,128]{2,1,0:T(8,128)(2,1)S(1)} custom-call(bf16[16,192,128]{2,1,0:T(8,128)(2,1)S(1)} %all_to_all.16.q_ref, bf16[16,192,128]{2,1,0:T(8,128)(2,1)S(1)} %collective-permute-done.kv_ref, f32[1024,256]{1,0:T(8,128)S(1)} %get-tuple-element.11.sum_ref, f32[1024,128]{1,0:T(8,128)S(1)} %get-tuple-element.12.top_ref), custom_call_target="tpu_custom_call" | custom-call | flops 1000000 | bytes 10000 | tf_op jit(solution)/shard_map/pallas_call | solution.py:256
  45.7 13.2 %all_to_all.17.a_ref = bf16[16,120,128]{2,1,0:T(8,128)(2,1)S(1)} all-to-all(bf16[16,120,128]{2,1,0:T(8,128)(2,1)S(1)} %shard_map.67), channel_id=1, replica_groups=mesh['z'=8,'core'=2,'chip_x'=4,'low_y'=2,'seq'=2] {'chip_x','seq','low_y'}, dimensions={0} | all-to-all | bytes 983040 | tf_op jit(solution)/shard_map/all_to_all | solution.py:257
  58.9 0.0 copy-done.2
  58.9 0.0 copy-start
  58.9 0.4 shard_map.68.own_ref
  59.3 2.1 %collective-permute-start.1 = (bf16[2,120,256]{2,1,0:T(8,128)(2,1)S(1)}, bf16[2,120,256]{2,1,0:T(8,128)(2,1)S(1)}, u32[]{:S(2)}, u32[]{:S(2)}) collective-permute-start(bf16[2,120,256]{2,1,0:T(8,128)(2,1)S(1)} %shard_map.68.own_ref), channel_id=1, source_target_pairs={{0,16},{16,0},{1,17},{17,1},{2,18},{18,2},{3,19},{19,3},{4,20},{20... | collective-permute-start | bytes 368648 | tf_op jit(solution)/shard_map/ppermute | solution.py:260
  61.4 0.0 collective-permute-start.2
  61.4 0.0 copy-done.1
  61.4 0.5 shard_map.71.w2_ref
  62.0 0.0 copy-done
  62.0 0.9 %shard_map.69.own_ref = f32[4,160,384]{2,1,0:T(8,128)S(1)} custom-call(bf16[2,120,256]{2,1,0:T(8,128)(2,1)S(1)} %shard_map.68.own_ref, bf16[27,256,128]{2,1,0:T(8,128)(2,1)S(1)} %bitcast.3), custom_call_target="tpu_custom_call" | custom-call | flops 1000000 | bytes 10000 | tf_op jit(solution)/shard_map/pallas_call | solution.py:263
  62.9 0.0 collective-permute-done.1.near_ref
  62.9 0.6 shard_map.70.done_ref
  63.5 2.5 %collective-permute-done.2.far_ref = bf16[2,120,256]{2,1,0:T(8,128)(2,1)S(1)} collective-permute-done((bf16[2,120,256]{2,1,0:T(8,128)(2,1)S(1)}, bf16[2,120,256]{2,1,0:T(8,128)(2,1)S(1)}, u32[]{:S(2)}, u32[]{:S(2)}) %collective-permute-start.2) | collective-permute-done | bytes 122912 | tf_op jit(solution)/shard_map/ppermute | solution.py:259
  66.0 2.0 %shard_map.72 = bf16[4,16,16,128]{3,2,1,0:T(8,128)(2,1)} custom-call(f32[4,160,384]{2,1,0:T(8,128)S(1)} %shard_map.69.own_ref, bf16[2,160,128]{2,1,0:T(8,128)(2,1)S(1)} %shard_map.70.done_ref, bf16[2,120,256]{2,1,0:T(8,128)(2,1)S(1)} %collective-permute-done.2.far_ref, bf16[27,256,128]{2,1,0:T(8,128)(2,1)S(1)} %bitcast.5, ...), custom_call_target="tpu_custom_call" | custom-call | flops 1000000 | bytes 10000 | tf_op jit(solution)/shard_map/pallas_call | solution.py:272
Async XLA Ops:
  37.8 6.1 %collective-permute-start = (bf16[16,192,128]{2,1,0:T(8,128)(2,1)S(1)}, bf16[16,192,128]{2,1,0:T(8,128)(2,1)S(1)}, u32[]{:S(2)}, u32[]{:S(2)}) collective-permute-start(bf16[16,192,128]{2,1,0:T(8,128)(2,1)S(1)} %all_to_all.16.q_ref), channel_id=1, source_target_pairs={{0,16},{16,0},{1,17},{17,1},{2,18},{18,2},{3,19},{19,3},{4,20},{20... | collective-permute-start | bytes 2359304 | tf_op jit(solution)/shard_map/ppermute | solution.py:254
  43.9 15.1 %copy-start.2 = (bf16[1024,256]{1,0:T(8,128)(2,1)S(1)}, bf16[1024,256]{1,0:T(8,128)(2,1)}, u32[]{:S(2)}) copy-start(bf16[1024,256]{1,0:T(8,128)(2,1)} %w_ref.1) | copy-start | bytes 1572868
  43.9 17.6 %copy-start.1 = (bf16[3,3,3,128,128]{4,3,2,1,0:T(8,128)(2,1)S(1)}, bf16[3,3,3,128,128]{4,3,2,1,0:T(8,128)(2,1)}, u32[]{:S(2)}) copy-start(bf16[3,3,3,128,128]{4,3,2,1,0:T(8,128)(2,1)} %param.11) | copy-start | bytes 2654212
  58.9 3.0 %copy-start = (bf16[3,3,3,256,128]{4,3,2,1,0:T(8,128)(2,1)S(1)}, bf16[3,3,3,256,128]{4,3,2,1,0:T(8,128)(2,1)}, u32[]{:S(2)}) copy-start(bf16[3,3,3,256,128]{4,3,2,1,0:T(8,128)(2,1)} %param.10) | copy-start | bytes 5308420
  59.3 3.6 %collective-permute-start.1 = (bf16[2,120,256]{2,1,0:T(8,128)(2,1)S(1)}, bf16[2,120,256]{2,1,0:T(8,128)(2,1)S(1)}, u32[]{:S(2)}, u32[]{:S(2)}) collective-permute-start(bf16[2,120,256]{2,1,0:T(8,128)(2,1)S(1)} %shard_map.68.own_ref), channel_id=1, source_target_pairs={{0,16},{16,0},{1,17},{17,1},{2,18},{18,2},{3,19},{19,3},{4,20},{20... | collective-permute-start | bytes 368648 | tf_op jit(solution)/shard_map/ppermute | solution.py:260
  61.4 4.6 %collective-permute-start.2 = (bf16[2,120,256]{2,1,0:T(8,128)(2,1)S(1)}, bf16[2,120,256]{2,1,0:T(8,128)(2,1)S(1)}, u32[]{:S(2)}, u32[]{:S(2)}) collective-permute-start(bf16[2,120,256]{2,1,0:T(8,128)(2,1)S(1)} %shard_map.68.own_ref), channel_id=1, source_target_pairs={{0,240},{16,32},{32,16},{48,64},{64,48},{80,96},{96,80},{112,128},... | collective-permute-start | bytes 368648 | tf_op jit(solution)/shard_map/ppermute | solution.py:259

commit v11 on v10

--- a/solution.py
+++ b/solution.py
@@ -29,7 +29,7 @@
 
 
 def slot(tile, half):
-    return 4 * (tile // 2) + 2 * half + tile % 2
+    return 8 * half + 4 * (tile % 2) + tile // 2
 
 
 def spread_kernel(q_hbm, k_hbm, v_hbm, out_ref, q_ref, k_ref, v_ref, sems):
@@ -59,9 +59,9 @@
             out_ref[slot(h, s), 128:192] = vals
 
 
-def halves(ref):
-    keys = ref[:, 64:128].reshape(1024, HD)
-    return keys, jnp.concatenate([ref[:, 128:192].reshape(1024, HD), jnp.ones((1024, HD), BF)], axis=1)
+def halves(ref, at):
+    keys = ref[:, at : at + 64].reshape(1024, HD)
+    return keys, jnp.concatenate([ref[:, at + 64 : at + 128].reshape(1024, HD), jnp.ones((1024, HD), BF)], axis=1)
 
 
 def scores_of(q, keys):
@@ -74,7 +74,7 @@
 
 
 def first_half_kernel(q_ref, sum_out, top_out):
-    keys, vals = halves(q_ref)
+    keys, vals = halves(q_ref, 64)
     for n in range(8):
         rows = slice(128 * n, 128 * n + 128)
         scores, top = scores_of(queries_of(q_ref, n), keys)
@@ -84,7 +84,7 @@
 
 
 def second_half_kernel(q_ref, kv_ref, sum_ref, top_ref, out_ref, windows):
-    keys, vals = halves(kv_ref)
+    keys, vals = halves(kv_ref, 0)
     edge = jnp.zeros((16, HD), F32)
     for s in range(2):
         windows[slot(0, s), 0:16] = edge
@@ -250,11 +250,11 @@
     spread, rows = call(spread_kernel, [(8, 16, H * HD), rows.shape], [BF, BF], [HB] * 3, scratch)(*in_hbm)
     tokens = lax.all_to_all(spread, "z", 0, 0, tiled=True)
     sent = call(pack_kernel, [(16, 192, HD)], [BF], [VM] * 2)(rows, tokens)
-    got = lax.all_to_all(sent, ("chip_x", "seq", "low_y"), 0, 0, tiled=True)
-    other = lax.ppermute(got, "core", [(0, 1), (1, 0)])
+    got = lax.all_to_all(sent, ("seq", "low_y", "chip_x"), 0, 0, tiled=True)
+    other = lax.ppermute(got[:, 64:192], "core", [(0, 1), (1, 0)])
     summed, top = call(first_half_kernel, [(1024, 2 * HD), (1024, HD)], [F32, F32], [VM])(got)
     attended = call(second_half_kernel, [(16, 120, HD)], [BF], [VM] * 4, [pltpu.VMEM((16, 96, HD), F32)])(got, other, summed, top)
-    back = lax.all_to_all(attended, ("chip_x", "seq", "low_y"), 0, 0, tiled=True)
+    back = lax.all_to_all(attended, ("seq", "low_y", "chip_x"), 0, 0, tiled=True)
     normed = call(project_kernel, [(2, 120, 256)], [BF], [VM, VM])(back, w_out)
     far = lax.ppermute(normed, ("z", "core"), [(i, (i - 1 + 2 * (i % 2)) % 16) for i in range(16)])
     near = lax.ppermute(normed, "core", [(0, 1), (1, 0)])

time: 68.3 us -> 67.9 us (level)
  starting transfers between devices: 6.29 us -> 5.45 us
  blocking collectives: 49.9 us -> 50.6 us
    all_to_all x2, blocking collectives: 30.7 us -> 31.4 us  [the longest x1 18.3 us: body(): got = lax.all_to_all(sent, ('seq', 'low_y', 'chip_x'), 0, 0, tiled=True)]
  transfers between devices with their start and end apart: 3 -> 3, of which waited for: 2 -> 1; matrix products, arithmetic and copies ran while one was open for 0% -> 0% of each run, Pallas kernels for 5% -> 5%
where the time goes in v11:
time: 67.9 us; the launch traced here: 67.6 us
  blocking collectives  50.6 us (75%)
  Pallas kernels  8.94 us (13%)
  starting transfers between devices  5.45 us (8%)
  waiting for transfers between devices  2.52 us (4%)
    all_to_all x1, blocking collectives, body(): tokens = lax.all_to_all(spread, 'z', 0, 0, tiled=True)  19.2 us
    all_to_all x1, blocking collectives, body(): got = lax.all_to_all(sent, ('seq', 'low_y', 'chip_x'), 0, 0, tiled=True)  18.3 us
    all_to_all x1, blocking collectives, body(): lax.all_to_all(attended, ('seq', 'low_y', 'chip_x'), 0, 0, tiled=True)  13.1 us
    ppermute x1, starting transfers between devices, body(): other = lax.ppermute(got[:, 64:192], 'core', [(0, 1), (1, 0)])  3.71 us
    ppermute x1, waiting for transfers between devices, body(): lax.ppermute(normed, ('z', 'core'), [(i, (i - 1 + 2 * (i % 2)) % 16) for...  2.51 us
    pallas_call x1, Pallas kernels, body(): return final(own_part, done, far, w1, merged)  1.99 us
    pallas_call x1, Pallas kernels, body(): call(second_half_kernel, [(16, 120, HD)], [BF], [VM] * 4, [pltpu.VMEM((16...  1.81 us
    ppermute x1, starting transfers between devices, body(): near = lax.ppermute(normed, 'core', [(0, 1), (1, 0)])  1.74 us
  transfers between devices with their start and end apart: 3, of which 1 were waited for; matrix products, arithmetic and copies ran while one was open for 0% of the time, Pallas kernels for 5%

profile of v11, /device:TPU:1, one launch (start us, length us, event | category | flops | bytes accessed | tf_op | source)
XLA Modules:
  0.0 67.6 jit_solution(6235724990583329077)
XLA Ops:
  0.0 1.0 %shard_map.64 = (bf16[8,16,1024]{2,1,0:T(8,128)(2,1)S(1)}, bf16[2,64,1024]{2,1,0:T(8,128)(2,1)S(1)}) custom-call(bf16[2,64,1024]{2,1,0:T(8,128)(2,1)} %bitcast.7, bf16[8,1024]{1,0:T(8,128)(2,1)} %k_hbm.1, bf16[8,1024]{1,0:T(8,128)(2,1)} %v_hbm.1), custom_call_target="tpu_custom_call" | custom-call | flops 1000000 | bytes 10000 | tf_op jit(solution)/shard_map/pallas_call | solution.py:250
  1.0 19.2 %all_to_all.15.kv_ref = bf16[8,16,1024]{2,1,0:T(8,128)(2,1)S(1)} all-to-all(bf16[8,16,1024]{2,1,0:T(8,128)(2,1)S(1)} %get-tuple-element.10), channel_id=1, replica_groups=mesh['z'=8,'core'=2,'chip_x'=4,'low_y'=2,'seq'=2] {'z'}, dimensions={0} | all-to-all | bytes 524288 | tf_op jit(solution)/shard_map/all_to_all | solution.py:251
  20.2 0.1 shard_map.65
  20.3 18.3 %all_to_all.16.q_ref = bf16[16,192,128]{2,1,0:T(8,128)(2,1)S(1)} all-to-all(bf16[16,192,128]{2,1,0:T(8,128)(2,1)S(1)} %shard_map.65), channel_id=1, replica_groups=mesh['z'=8,'core'=2,'chip_x'=4,'low_y'=2,'seq'=2] {'seq','low_y','chip_x'}, dimensions={0} | all-to-all | bytes 1572864 | tf_op jit(solution)/shard_map/all_to_all | solution.py:253
  38.6 3.7 %collective-permute-start = (bf16[16,128,128]{2,1,0:T(8,128)(2,1)S(1)}, bf16[16,128,128]{2,1,0:T(8,128)(2,1)S(1)}, u32[]{:S(2)}, u32[]{:S(2)}) collective-permute-start(bf16[16,128,128]{2,1,0:T(8,128)(2,1)S(1)} %slice.4), channel_id=1, source_target_pairs={{0,16},{16,0},{1,17},{17,1},{2,18},{18,2},{3,19},{19,3},{4,20},{20... | collective-permute-start | bytes 1572872 | tf_op jit(solution)/shard_map/ppermute | solution.py:254
  42.3 1.6 %shard_map.66 = (f32[1024,256]{1,0:T(8,128)S(1)}, f32[1024,128]{1,0:T(8,128)S(1)}) custom-call(bf16[16,192,128]{2,1,0:T(8,128)(2,1)S(1)} %all_to_all.16.q_ref), custom_call_target="tpu_custom_call" | custom-call | flops 1000000 | bytes 10000 | tf_op jit(solution)/shard_map/pallas_call | solution.py:255
  43.9 0.0 collective-permute-done.kv_ref
  43.9 0.0 copy-start.2
  44.0 0.0 copy-start.1
  44.0 1.8 %shard_map.67 = bf16[16,120,128]{2,1,0:T(8,128)(2,1)S(1)} custom-call(bf16[16,192,128]{2,1,0:T(8,128)(2,1)S(1)} %all_to_all.16.q_ref, bf16[16,128,128]{2,1,0:T(8,128)(2,1)S(1)} %collective-permute-done.kv_ref, f32[1024,256]{1,0:T(8,128)S(1)} %get-tuple-element.11.sum_ref, f32[1024,128]{1,0:T(8,128)S(1)} %get-tuple-element.12.top_ref), custom_call_target="tpu_custom_call" | custom-call | flops 1000000 | bytes 10000 | tf_op jit(solution)/shard_map/pallas_call | solution.py:256
  45.8 13.1 %all_to_all.17.a_ref = bf16[16,120,128]{2,1,0:T(8,128)(2,1)S(1)} all-to-all(bf16[16,120,128]{2,1,0:T(8,128)(2,1)S(1)} %shard_map.67), channel_id=1, replica_groups=mesh['z'=8,'core'=2,'chip_x'=4,'low_y'=2,'seq'=2] {'seq','low_y','chip_x'}, dimensions={0} | all-to-all | bytes 983040 | tf_op jit(solution)/shard_map/all_to_all | solution.py:257
  58.9 0.0 copy-done.2
  58.9 0.0 copy-start
  58.9 0.4 shard_map.68.own_ref
  59.3 1.7 %collective-permute-start.1 = (bf16[2,120,256]{2,1,0:T(8,128)(2,1)S(1)}, bf16[2,120,256]{2,1,0:T(8,128)(2,1)S(1)}, u32[]{:S(2)}, u32[]{:S(2)}) collective-permute-start(bf16[2,120,256]{2,1,0:T(8,128)(2,1)S(1)} %shard_map.68.own_ref), channel_id=1, source_target_pairs={{0,16},{16,0},{1,17},{17,1},{2,18},{18,2},{3,19},{19,3},{4,20},{20... | collective-permute-start | bytes 368648 | tf_op jit(solution)/shard_map/ppermute | solution.py:260
  61.0 0.0 collective-permute-start.2
  61.0 0.0 copy-done.1
  61.0 0.5 shard_map.71.w2_ref
  61.6 0.0 copy-done
  61.6 0.9 %shard_map.69.own_ref = f32[4,160,384]{2,1,0:T(8,128)S(1)} custom-call(bf16[2,120,256]{2,1,0:T(8,128)(2,1)S(1)} %shard_map.68.own_ref, bf16[27,256,128]{2,1,0:T(8,128)(2,1)S(1)} %bitcast.3), custom_call_target="tpu_custom_call" | custom-call | flops 1000000 | bytes 10000 | tf_op jit(solution)/shard_map/pallas_call | solution.py:263
  62.5 0.0 collective-permute-done.1.near_ref
  62.5 0.6 shard_map.70.done_ref
  63.1 2.5 %collective-permute-done.2.far_ref = bf16[2,120,256]{2,1,0:T(8,128)(2,1)S(1)} collective-permute-done((bf16[2,120,256]{2,1,0:T(8,128)(2,1)S(1)}, bf16[2,120,256]{2,1,0:T(8,128)(2,1)S(1)}, u32[]{:S(2)}, u32[]{:S(2)}) %collective-permute-start.2) | collective-permute-done | bytes 122912 | tf_op jit(solution)/shard_map/ppermute | solution.py:259
  65.6 2.0 %shard_map.72 = bf16[4,16,16,128]{3,2,1,0:T(8,128)(2,1)} custom-call(f32[4,160,384]{2,1,0:T(8,128)S(1)} %shard_map.69.own_ref, bf16[2,160,128]{2,1,0:T(8,128)(2,1)S(1)} %shard_map.70.done_ref, bf16[2,120,256]{2,1,0:T(8,128)(2,1)S(1)} %collective-permute-done.2.far_ref, bf16[27,256,128]{2,1,0:T(8,128)(2,1)S(1)} %bitcast.5, ...), custom_call_target="tpu_custom_call" | custom-call | flops 1000000 | bytes 10000 | tf_op jit(solution)/shard_map/pallas_call | solution.py:272
  (1 shorter events, 0.0 us)
Async XLA Ops:
  38.6 5.3 %collective-permute-start = (bf16[16,128,128]{2,1,0:T(8,128)(2,1)S(1)}, bf16[16,128,128]{2,1,0:T(8,128)(2,1)S(1)}, u32[]{:S(2)}, u32[]{:S(2)}) collective-permute-start(bf16[16,128,128]{2,1,0:T(8,128)(2,1)S(1)} %slice.4), channel_id=1, source_target_pairs={{0,16},{16,0},{1,17},{17,1},{2,18},{18,2},{3,19},{19,3},{4,20},{20... | collective-permute-start | bytes 1572872 | tf_op jit(solution)/shard_map/ppermute | solution.py:254
  43.9 15.0 %copy-start.2 = (bf16[1024,256]{1,0:T(8,128)(2,1)S(1)}, bf16[1024,256]{1,0:T(8,128)(2,1)}, u32[]{:S(2)}) copy-start(bf16[1024,256]{1,0:T(8,128)(2,1)} %w_ref.1) | copy-start | bytes 1572868
  44.0 17.1 %copy-start.1 = (bf16[3,3,3,128,128]{4,3,2,1,0:T(8,128)(2,1)S(1)}, bf16[3,3,3,128,128]{4,3,2,1,0:T(8,128)(2,1)}, u32[]{:S(2)}) copy-start(bf16[3,3,3,128,128]{4,3,2,1,0:T(8,128)(2,1)} %param.11) | copy-start | bytes 2654212
  58.9 2.7 %copy-start = (bf16[3,3,3,256,128]{4,3,2,1,0:T(8,128)(2,1)S(1)}, bf16[3,3,3,256,128]{4,3,2,1,0:T(8,128)(2,1)}, u32[]{:S(2)}) copy-start(bf16[3,3,3,256,128]{4,3,2,1,0:T(8,128)(2,1)} %param.10) | copy-start | bytes 5308420
  59.3 3.2 %collective-permute-start.1 = (bf16[2,120,256]{2,1,0:T(8,128)(2,1)S(1)}, bf16[2,120,256]{2,1,0:T(8,128)(2,1)S(1)}, u32[]{:S(2)}, u32[]{:S(2)}) collective-permute-start(bf16[2,120,256]{2,1,0:T(8,128)(2,1)S(1)} %shard_map.68.own_ref), channel_id=1, source_target_pairs={{0,16},{16,0},{1,17},{17,1},{2,18},{18,2},{3,19},{19,3},{4,20},{20... | collective-permute-start | bytes 368648 | tf_op jit(solution)/shard_map/ppermute | solution.py:260
  61.0 4.6 %collective-permute-start.2 = (bf16[2,120,256]{2,1,0:T(8,128)(2,1)S(1)}, bf16[2,120,256]{2,1,0:T(8,128)(2,1)S(1)}, u32[]{:S(2)}, u32[]{:S(2)}) collective-permute-start(bf16[2,120,256]{2,1,0:T(8,128)(2,1)S(1)} %shard_map.68.own_ref), channel_id=1, source_target_pairs={{0,240},{16,32},{32,16},{48,64},{64,48},{80,96},{96,80},{112,128},... | collective-permute-start | bytes 368648 | tf_op jit(solution)/shard_map/ppermute | solution.py:259

commit v12 on v11

--- a/solution.py
+++ b/solution.py
@@ -205,7 +205,7 @@
 
 def near_conv_kernel(near_ref, own_ref, w1_ref, out_ref):
     at_left = lax.axis_index("core") == 1
-    slabs = laid_out(near_ref[...])
+    slabs = laid_out(near_ref[1 - lax.axis_index("core")])
     for n, (_, rows) in enumerate(side(at_left, slabs, own_ref, w1_ref)):
         out_ref[n] = rows
 
@@ -257,7 +257,7 @@
     back = lax.all_to_all(attended, ("seq", "low_y", "chip_x"), 0, 0, tiled=True)
     normed = call(project_kernel, [(2, 120, 256)], [BF], [VM, VM])(back, w_out)
     far = lax.ppermute(normed, ("z", "core"), [(i, (i - 1 + 2 * (i % 2)) % 16) for i in range(16)])
-    near = lax.ppermute(normed, "core", [(0, 1), (1, 0)])
+    near = lax.all_gather(normed, "core")
     w1 = conv_first.reshape(27, 256, 128)
     merged = call(merge_kernel, [(4, 512, 512)], [BF], [VM])(conv_second.reshape(27, 128, 128))
     own_part = call(own_conv_kernel, [(4, 160, 384)], [F32], [VM, VM])(normed, w1)

time: 67.9 us -> 67.4 us (level)
  blocking collectives: 50.6 us -> 53.2 us
  waiting for transfers between devices: 2.52 us -> 0.01 us
    all_gather x0 -> x1, blocking collectives: none -> 2.67 us  [body(): near = lax.all_gather(normed, 'core')]
    ppermute x1, waiting for transfers between devices: 2.51 us -> 0.01 us  [body(): lax.ppermute(normed, ('z', 'core'), [(i, (i - 1 + 2 * (i % 2)) % 16) for...]
    ppermute x1 -> x0, starting transfers between devices: 1.74 us -> none  [body(): near = lax.ppermute(normed, 'core', [(0, 1), (1, 0)])]
    ppermute x1, starting transfers between devices: 0.01 us -> 1.13 us  [body(): lax.ppermute(normed, ('z', 'core'), [(i, (i - 1 + 2 * (i % 2)) % 16) for...]
  transfers between devices with their start and end apart: 3 -> 2, of which waited for: 1 -> 0; matrix products, arithmetic and copies ran while one was open for 0% -> 0% of each run, Pallas kernels for 5% -> 5%
where the time goes in v12:
time: 67.4 us; the launch traced here: 67.2 us
  blocking collectives  53.2 us (79%)
  Pallas kernels  8.92 us (13%)
  starting transfers between devices  4.83 us (7%)
    all_to_all x1, blocking collectives, body(): tokens = lax.all_to_all(spread, 'z', 0, 0, tiled=True)  19.2 us
    all_to_all x1, blocking collectives, body(): got = lax.all_to_all(sent, ('seq', 'low_y', 'chip_x'), 0, 0, tiled=True)  18.3 us
    all_to_all x1, blocking collectives, body(): lax.all_to_all(attended, ('seq', 'low_y', 'chip_x'), 0, 0, tiled=True)  13.1 us
    ppermute x1, starting transfers between devices, body(): other = lax.ppermute(got[:, 64:192], 'core', [(0, 1), (1, 0)])  3.71 us
    all_gather x1, blocking collectives, body(): near = lax.all_gather(normed, 'core')  2.67 us
    pallas_call x1, Pallas kernels, body(): return final(own_part, done, far, w1, merged)  1.99 us
    pallas_call x1, Pallas kernels, body(): call(second_half_kernel, [(16, 120, HD)], [BF], [VM] * 4, [pltpu.VMEM((16...  1.81 us
    pallas_call x1, Pallas kernels, body(): call(first_half_kernel, [(1024, 2 * HD), (1024, HD)], [F32, F32], [VM])(got)  1.58 us
  transfers between devices with their start and end apart: 2, of which 0 were waited for; matrix products, arithmetic and copies ran while one was open for 0% of the time, Pallas kernels for 5%

profile of v12, /device:TPU:1, one launch (start us, length us, event | category | flops | bytes accessed | tf_op | source)
XLA Modules:
  0.0 67.2 jit_solution(7204063315353492752)
XLA Ops:
  0.0 1.0 %shard_map.64 = (bf16[8,16,1024]{2,1,0:T(8,128)(2,1)S(1)}, bf16[2,64,1024]{2,1,0:T(8,128)(2,1)S(1)}) custom-call(bf16[2,64,1024]{2,1,0:T(8,128)(2,1)} %bitcast.9, bf16[8,1024]{1,0:T(8,128)(2,1)} %k_hbm.1, bf16[8,1024]{1,0:T(8,128)(2,1)} %v_hbm.1), custom_call_target="tpu_custom_call" | custom-call | flops 1000000 | bytes 10000 | tf_op jit(solution)/shard_map/pallas_call | solution.py:250
  1.0 19.2 %all_to_all.15.kv_ref = bf16[8,16,1024]{2,1,0:T(8,128)(2,1)S(1)} all-to-all(bf16[8,16,1024]{2,1,0:T(8,128)(2,1)S(1)} %get-tuple-element.10), channel_id=1, replica_groups=mesh['z'=8,'core'=2,'chip_x'=4,'low_y'=2,'seq'=2] {'z'}, dimensions={0} | all-to-all | bytes 524288 | tf_op jit(solution)/shard_map/all_to_all | solution.py:251
  20.2 0.1 shard_map.65
  20.3 18.3 %all_to_all.16.q_ref = bf16[16,192,128]{2,1,0:T(8,128)(2,1)S(1)} all-to-all(bf16[16,192,128]{2,1,0:T(8,128)(2,1)S(1)} %shard_map.65), channel_id=1, replica_groups=mesh['z'=8,'core'=2,'chip_x'=4,'low_y'=2,'seq'=2] {'seq','low_y','chip_x'}, dimensions={0} | all-to-all | bytes 1572864 | tf_op jit(solution)/shard_map/all_to_all | solution.py:253
  38.6 3.7 %collective-permute-start = (bf16[16,128,128]{2,1,0:T(8,128)(2,1)S(1)}, bf16[16,128,128]{2,1,0:T(8,128)(2,1)S(1)}, u32[]{:S(2)}, u32[]{:S(2)}) collective-permute-start(bf16[16,128,128]{2,1,0:T(8,128)(2,1)S(1)} %slice.4), channel_id=1, source_target_pairs={{0,16},{16,0},{1,17},{17,1},{2,18},{18,2},{3,19},{19,3},{4,20},{20... | collective-permute-start | bytes 1572872 | tf_op jit(solution)/shard_map/ppermute | solution.py:254
  42.3 1.6 %shard_map.66 = (f32[1024,256]{1,0:T(8,128)S(1)}, f32[1024,128]{1,0:T(8,128)S(1)}) custom-call(bf16[16,192,128]{2,1,0:T(8,128)(2,1)S(1)} %all_to_all.16.q_ref), custom_call_target="tpu_custom_call" | custom-call | flops 1000000 | bytes 10000 | tf_op jit(solution)/shard_map/pallas_call | solution.py:255
  43.9 0.0 collective-permute-done.kv_ref
  43.9 0.0 copy-start.2
  44.0 0.0 copy-start.1
  44.0 1.8 %shard_map.67 = bf16[16,120,128]{2,1,0:T(8,128)(2,1)S(1)} custom-call(bf16[16,192,128]{2,1,0:T(8,128)(2,1)S(1)} %all_to_all.16.q_ref, bf16[16,128,128]{2,1,0:T(8,128)(2,1)S(1)} %collective-permute-done.kv_ref, f32[1024,256]{1,0:T(8,128)S(1)} %get-tuple-element.11.sum_ref, f32[1024,128]{1,0:T(8,128)S(1)} %get-tuple-element.12.top_ref), custom_call_target="tpu_custom_call" | custom-call | flops 1000000 | bytes 10000 | tf_op jit(solution)/shard_map/pallas_call | solution.py:256
  45.8 13.1 %all_to_all.17.a_ref = bf16[16,120,128]{2,1,0:T(8,128)(2,1)S(1)} all-to-all(bf16[16,120,128]{2,1,0:T(8,128)(2,1)S(1)} %shard_map.67), channel_id=1, replica_groups=mesh['z'=8,'core'=2,'chip_x'=4,'low_y'=2,'seq'=2] {'seq','low_y','chip_x'}, dimensions={0} | all-to-all | bytes 983040 | tf_op jit(solution)/shard_map/all_to_all | solution.py:257
  58.9 0.0 copy-done.2
  58.9 0.0 copy-start
  58.9 0.4 shard_map.68.own_ref
  59.3 1.1 %collective-permute-start.1 = (bf16[2,120,256]{2,1,0:T(8,128)(2,1)S(1)}, bf16[2,120,256]{2,1,0:T(8,128)(2,1)S(1)}, u32[]{:S(2)}, u32[]{:S(2)}) collective-permute-start(bf16[2,120,256]{2,1,0:T(8,128)(2,1)S(1)} %shard_map.68.own_ref), channel_id=1, source_target_pairs={{0,240},{16,32},{32,16},{48,64},{64,48},{80,96},{96,80},{112,128},... | collective-permute-start | bytes 368648 | tf_op jit(solution)/shard_map/ppermute | solution.py:259
  60.4 0.0 copy-done.1
  60.4 0.5 shard_map.71.w2_ref
  61.0 0.0 copy-done
  61.0 0.9 %shard_map.69.own_ref = f32[4,160,384]{2,1,0:T(8,128)S(1)} custom-call(bf16[2,120,256]{2,1,0:T(8,128)(2,1)S(1)} %shard_map.68.own_ref, bf16[27,256,128]{2,1,0:T(8,128)(2,1)S(1)} %bitcast.4), custom_call_target="tpu_custom_call" | custom-call | flops 1000000 | bytes 10000 | tf_op jit(solution)/shard_map/pallas_call | solution.py:263
  61.9 2.7 %all-gather = bf16[4,120,256]{2,1,0:T(8,128)(2,1)S(1)} all-gather(bf16[2,120,256]{2,1,0:T(8,128)(2,1)S(1)} %shard_map.68.own_ref), channel_id=2, replica_groups=mesh['z'=8,'core'=2,'chip_x'=4,'low_y'=2,'seq'=2] {'core'}, dimensions={0}, use_global_device_ids=true | all-gather | bytes 368640 | tf_op jit(solution)/shard_map/all_gather | solution.py:260
  64.6 0.6 shard_map.70.done_ref
  65.2 0.0 collective-permute-done.1.far_ref
  65.2 2.0 %shard_map.72 = bf16[4,16,16,128]{3,2,1,0:T(8,128)(2,1)} custom-call(f32[4,160,384]{2,1,0:T(8,128)S(1)} %shard_map.69.own_ref, bf16[2,160,128]{2,1,0:T(8,128)(2,1)S(1)} %shard_map.70.done_ref, bf16[2,120,256]{2,1,0:T(8,128)(2,1)S(1)} %collective-permute-done.1.far_ref, bf16[27,256,128]{2,1,0:T(8,128)(2,1)S(1)} %bitcast.6, ...), custom_call_target="tpu_custom_call" | custom-call | flops 1000000 | bytes 10000 | tf_op jit(solution)/shard_map/pallas_call | solution.py:272
  (1 shorter events, 0.0 us)
Async XLA Ops:
  38.6 5.3 %collective-permute-start = (bf16[16,128,128]{2,1,0:T(8,128)(2,1)S(1)}, bf16[16,128,128]{2,1,0:T(8,128)(2,1)S(1)}, u32[]{:S(2)}, u32[]{:S(2)}) collective-permute-start(bf16[16,128,128]{2,1,0:T(8,128)(2,1)S(1)} %slice.4), channel_id=1, source_target_pairs={{0,16},{16,0},{1,17},{17,1},{2,18},{18,2},{3,19},{19,3},{4,20},{20... | collective-permute-start | bytes 1572872 | tf_op jit(solution)/shard_map/ppermute | solution.py:254
  43.9 15.0 %copy-start.2 = (bf16[1024,256]{1,0:T(8,128)(2,1)S(1)}, bf16[1024,256]{1,0:T(8,128)(2,1)}, u32[]{:S(2)}) copy-start(bf16[1024,256]{1,0:T(8,128)(2,1)} %w_ref.1) | copy-start | bytes 1572868
  44.0 16.5 %copy-start.1 = (bf16[3,3,3,128,128]{4,3,2,1,0:T(8,128)(2,1)S(1)}, bf16[3,3,3,128,128]{4,3,2,1,0:T(8,128)(2,1)}, u32[]{:S(2)}) copy-start(bf16[3,3,3,128,128]{4,3,2,1,0:T(8,128)(2,1)} %param.11) | copy-start | bytes 2654212
  58.9 2.1 %copy-start = (bf16[3,3,3,256,128]{4,3,2,1,0:T(8,128)(2,1)S(1)}, bf16[3,3,3,256,128]{4,3,2,1,0:T(8,128)(2,1)}, u32[]{:S(2)}) copy-start(bf16[3,3,3,256,128]{4,3,2,1,0:T(8,128)(2,1)} %param.10) | copy-start | bytes 5308420
  59.3 5.9 %collective-permute-start.1 = (bf16[2,120,256]{2,1,0:T(8,128)(2,1)S(1)}, bf16[2,120,256]{2,1,0:T(8,128)(2,1)S(1)}, u32[]{:S(2)}, u32[]{:S(2)}) collective-permute-start(bf16[2,120,256]{2,1,0:T(8,128)(2,1)S(1)} %shard_map.68.own_ref), channel_id=1, source_target_pairs={{0,240},{16,32},{32,16},{48,64},{64,48},{80,96},{96,80},{112,128},... | collective-permute-start | bytes 368648 | tf_op jit(solution)/shard_map/ppermute | solution.py:259

commit v13 on v12

--- a/solution.py
+++ b/solution.py
@@ -109,9 +109,11 @@
     col = lax.broadcasted_iota(jnp.int32, (32, 96), 1)
     for s in range(2):
         pick = (col == (row // 2) * 8 + row % 2 + 6 * s).astype(F32).astype(BF)
-        for n in range(8):
-            near = jnp.dot(pick, windows[slot(n, 1 - s)].astype(BF), preferred_element_type=F32)
-            out_ref[slot(n, s)] = jnp.concatenate([windows[slot(n, s)], near[0:24]], axis=0).astype(BF)
+        for n in range(0, 8, 2):
+            two = jnp.concatenate([windows[slot(n, 1 - s)], windows[slot(n + 1, 1 - s)]], axis=1).astype(BF)
+            near = jnp.dot(pick, two, preferred_element_type=F32)
+            for m, part in ((n, near[0:24, 0:HD]), (n + 1, near[0:24, HD : 2 * HD])):
+                out_ref[slot(m, s)] = jnp.concatenate([windows[slot(m, s)], part], axis=0).astype(BF)
 
 
 def project_kernel(a_ref, w_ref, out_ref):

time: 67.4 us -> 67.4 us (level)
  no operation moved by 1% of the time
where the time goes in v13:
time: 67.4 us; the launch traced here: 67.1 us
  blocking collectives  53.2 us (79%)
  Pallas kernels  8.9 us (13%)
  starting transfers between devices  4.84 us (7%)
    all_to_all x1, blocking collectives, body(): tokens = lax.all_to_all(spread, 'z', 0, 0, tiled=True)  19.2 us
    all_to_all x1, blocking collectives, body(): got = lax.all_to_all(sent, ('seq', 'low_y', 'chip_x'), 0, 0, tiled=True)  18.3 us
    all_to_all x1, blocking collectives, body(): lax.all_to_all(attended, ('seq', 'low_y', 'chip_x'), 0, 0, tiled=True)  13.1 us
    ppermute x1, starting transfers between devices, body(): other = lax.ppermute(got[:, 64:192], 'core', [(0, 1), (1, 0)])  3.71 us
    all_gather x1, blocking collectives, body(): near = lax.all_gather(normed, 'core')  2.67 us
    pallas_call x1, Pallas kernels, body(): return final(own_part, done, far, w1, merged)  1.99 us
    pallas_call x1, Pallas kernels, body(): call(second_half_kernel, [(16, 120, HD)], [BF], [VM] * 4, [pltpu.VMEM((16...  1.79 us
    pallas_call x1, Pallas kernels, body(): call(first_half_kernel, [(1024, 2 * HD), (1024, HD)], [F32, F32], [VM])(got)  1.58 us
  transfers between devices with their start and end apart: 2, of which 0 were waited for; matrix products, arithmetic and copies ran while one was open for 0% of the time, Pallas kernels for 5%

profile of v13, /device:TPU:1, one launch (start us, length us, event | category | flops | bytes accessed | tf_op | source)
XLA Modules:
  0.0 67.1 jit_solution(4571207758499348678)
XLA Ops:
  0.0 1.0 %shard_map.64 = (bf16[8,16,1024]{2,1,0:T(8,128)(2,1)S(1)}, bf16[2,64,1024]{2,1,0:T(8,128)(2,1)S(1)}) custom-call(bf16[2,64,1024]{2,1,0:T(8,128)(2,1)} %bitcast.9, bf16[8,1024]{1,0:T(8,128)(2,1)} %k_hbm.1, bf16[8,1024]{1,0:T(8,128)(2,1)} %v_hbm.1), custom_call_target="tpu_custom_call" | custom-call | flops 1000000 | bytes 10000 | tf_op jit(solution)/shard_map/pallas_call | solution.py:252
  1.0 19.2 %all_to_all.15.kv_ref = bf16[8,16,1024]{2,1,0:T(8,128)(2,1)S(1)} all-to-all(bf16[8,16,1024]{2,1,0:T(8,128)(2,1)S(1)} %get-tuple-element.10), channel_id=1, replica_groups=mesh['z'=8,'core'=2,'chip_x'=4,'low_y'=2,'seq'=2] {'z'}, dimensions={0} | all-to-all | bytes 524288 | tf_op jit(solution)/shard_map/all_to_all | solution.py:253
  20.2 0.1 shard_map.65
  20.3 18.3 %all_to_all.16.q_ref = bf16[16,192,128]{2,1,0:T(8,128)(2,1)S(1)} all-to-all(bf16[16,192,128]{2,1,0:T(8,128)(2,1)S(1)} %shard_map.65), channel_id=1, replica_groups=mesh['z'=8,'core'=2,'chip_x'=4,'low_y'=2,'seq'=2] {'seq','low_y','chip_x'}, dimensions={0} | all-to-all | bytes 1572864 | tf_op jit(solution)/shard_map/all_to_all | solution.py:255
  38.6 3.7 %collective-permute-start = (bf16[16,128,128]{2,1,0:T(8,128)(2,1)S(1)}, bf16[16,128,128]{2,1,0:T(8,128)(2,1)S(1)}, u32[]{:S(2)}, u32[]{:S(2)}) collective-permute-start(bf16[16,128,128]{2,1,0:T(8,128)(2,1)S(1)} %slice.4), channel_id=1, source_target_pairs={{0,16},{16,0},{1,17},{17,1},{2,18},{18,2},{3,19},{19,3},{4,20},{20... | collective-permute-start | bytes 1572872 | tf_op jit(solution)/shard_map/ppermute | solution.py:256
  42.3 1.6 %shard_map.66 = (f32[1024,256]{1,0:T(8,128)S(1)}, f32[1024,128]{1,0:T(8,128)S(1)}) custom-call(bf16[16,192,128]{2,1,0:T(8,128)(2,1)S(1)} %all_to_all.16.q_ref), custom_call_target="tpu_custom_call" | custom-call | flops 1000000 | bytes 10000 | tf_op jit(solution)/shard_map/pallas_call | solution.py:257
  43.9 0.0 collective-permute-done.kv_ref
  43.9 0.0 copy-start.2
  44.0 0.0 copy-start.1
  44.0 1.8 %shard_map.67 = bf16[16,120,128]{2,1,0:T(8,128)(2,1)S(1)} custom-call(bf16[16,192,128]{2,1,0:T(8,128)(2,1)S(1)} %all_to_all.16.q_ref, bf16[16,128,128]{2,1,0:T(8,128)(2,1)S(1)} %collective-permute-done.kv_ref, f32[1024,256]{1,0:T(8,128)S(1)} %get-tuple-element.11.sum_ref, f32[1024,128]{1,0:T(8,128)S(1)} %get-tuple-element.12.top_ref), custom_call_target="tpu_custom_call" | custom-call | flops 1000000 | bytes 10000 | tf_op jit(solution)/shard_map/pallas_call | solution.py:258
  45.8 13.1 %all_to_all.17.a_ref = bf16[16,120,128]{2,1,0:T(8,128)(2,1)S(1)} all-to-all(bf16[16,120,128]{2,1,0:T(8,128)(2,1)S(1)} %shard_map.67), channel_id=1, replica_groups=mesh['z'=8,'core'=2,'chip_x'=4,'low_y'=2,'seq'=2] {'seq','low_y','chip_x'}, dimensions={0} | all-to-all | bytes 983040 | tf_op jit(solution)/shard_map/all_to_all | solution.py:259
  58.9 0.0 copy-done.2
  58.9 0.0 copy-start
  58.9 0.4 shard_map.68.own_ref
  59.3 1.1 %collective-permute-start.1 = (bf16[2,120,256]{2,1,0:T(8,128)(2,1)S(1)}, bf16[2,120,256]{2,1,0:T(8,128)(2,1)S(1)}, u32[]{:S(2)}, u32[]{:S(2)}) collective-permute-start(bf16[2,120,256]{2,1,0:T(8,128)(2,1)S(1)} %shard_map.68.own_ref), channel_id=1, source_target_pairs={{0,240},{16,32},{32,16},{48,64},{64,48},{80,96},{96,80},{112,128},... | collective-permute-start | bytes 368648 | tf_op jit(solution)/shard_map/ppermute | solution.py:261
  60.4 0.0 copy-done.1
  60.4 0.5 shard_map.71.w2_ref
  60.9 0.0 copy-done
  60.9 0.9 %shard_map.69.own_ref = f32[4,160,384]{2,1,0:T(8,128)S(1)} custom-call(bf16[2,120,256]{2,1,0:T(8,128)(2,1)S(1)} %shard_map.68.own_ref, bf16[27,256,128]{2,1,0:T(8,128)(2,1)S(1)} %bitcast.4), custom_call_target="tpu_custom_call" | custom-call | flops 1000000 | bytes 10000 | tf_op jit(solution)/shard_map/pallas_call | solution.py:265
  61.9 2.7 %all-gather = bf16[4,120,256]{2,1,0:T(8,128)(2,1)S(1)} all-gather(bf16[2,120,256]{2,1,0:T(8,128)(2,1)S(1)} %shard_map.68.own_ref), channel_id=2, replica_groups=mesh['z'=8,'core'=2,'chip_x'=4,'low_y'=2,'seq'=2] {'core'}, dimensions={0}, use_global_device_ids=true | all-gather | bytes 368640 | tf_op jit(solution)/shard_map/all_gather | solution.py:262
  64.5 0.6 shard_map.70.done_ref
  65.1 0.0 collective-permute-done.1.far_ref
  65.1 2.0 %shard_map.72 = bf16[4,16,16,128]{3,2,1,0:T(8,128)(2,1)} custom-call(f32[4,160,384]{2,1,0:T(8,128)S(1)} %shard_map.69.own_ref, bf16[2,160,128]{2,1,0:T(8,128)(2,1)S(1)} %shard_map.70.done_ref, bf16[2,120,256]{2,1,0:T(8,128)(2,1)S(1)} %collective-permute-done.1.far_ref, bf16[27,256,128]{2,1,0:T(8,128)(2,1)S(1)} %bitcast.6, ...), custom_call_target="tpu_custom_call" | custom-call | flops 1000000 | bytes 10000 | tf_op jit(solution)/shard_map/pallas_call | solution.py:274
  (1 shorter events, 0.0 us)
Async XLA Ops:
  38.6 5.3 %collective-permute-start = (bf16[16,128,128]{2,1,0:T(8,128)(2,1)S(1)}, bf16[16,128,128]{2,1,0:T(8,128)(2,1)S(1)}, u32[]{:S(2)}, u32[]{:S(2)}) collective-permute-start(bf16[16,128,128]{2,1,0:T(8,128)(2,1)S(1)} %slice.4), channel_id=1, source_target_pairs={{0,16},{16,0},{1,17},{17,1},{2,18},{18,2},{3,19},{19,3},{4,20},{20... | collective-permute-start | bytes 1572872 | tf_op jit(solution)/shard_map/ppermute | solution.py:256
  43.9 14.9 %copy-start.2 = (bf16[1024,256]{1,0:T(8,128)(2,1)S(1)}, bf16[1024,256]{1,0:T(8,128)(2,1)}, u32[]{:S(2)}) copy-start(bf16[1024,256]{1,0:T(8,128)(2,1)} %w_ref.1) | copy-start | bytes 1572868
  44.0 16.4 %copy-start.1 = (bf16[3,3,3,128,128]{4,3,2,1,0:T(8,128)(2,1)S(1)}, bf16[3,3,3,128,128]{4,3,2,1,0:T(8,128)(2,1)}, u32[]{:S(2)}) copy-start(bf16[3,3,3,128,128]{4,3,2,1,0:T(8,128)(2,1)} %param.11) | copy-start | bytes 2654212
  58.9 2.1 %copy-start = (bf16[3,3,3,256,128]{4,3,2,1,0:T(8,128)(2,1)S(1)}, bf16[3,3,3,256,128]{4,3,2,1,0:T(8,128)(2,1)}, u32[]{:S(2)}) copy-start(bf16[3,3,3,256,128]{4,3,2,1,0:T(8,128)(2,1)} %param.10) | copy-start | bytes 5308420
  59.3 5.9 %collective-permute-start.1 = (bf16[2,120,256]{2,1,0:T(8,128)(2,1)S(1)}, bf16[2,120,256]{2,1,0:T(8,128)(2,1)S(1)}, u32[]{:S(2)}, u32[]{:S(2)}) collective-permute-start(bf16[2,120,256]{2,1,0:T(8,128)(2,1)S(1)} %shard_map.68.own_ref), channel_id=1, source_target_pairs={{0,240},{16,32},{32,16},{48,64},{64,48},{80,96},{96,80},{112,128},... | collective-permute-start | bytes 368648 | tf_op jit(solution)/shard_map/ppermute | solution.py:261
